TPU v7x, 1024 devices: a whole 4x4x32 slice. The times are simulated.
1024 devices in a mesh: dp: 4 (over x), expert: 32 (over y, z_lo), tensor: 8 (over z_hi, core).
Axes of the slice: x: 4, y: 4, z: 32 (z_hi: 4, z_lo: 8; z = z_hi * 8 + z_lo), core: 2. Of those that a mesh axis runs over, the one named last changes fastest.
Arguments:
- hidden_states: bfloat16 [8192, 2048], P(('dp', 'expert'), 'tensor'), may hold values from -6 to 6
- expert_ids: int32 [8192, 8], P(('dp', 'expert')), may hold values from 0 to 63, all different within a row; in each aligned block of 64 rows (0 to 63, 64 to 127, ...) at most 8 rows name the same one
- gate_weights: bfloat16 [8192, 8], P(('dp', 'expert')), may hold values from 0.029907227 to 0.3984375
- completion_lengths: int32 [4], P('dp'), may hold values from 256 to 2048
- output_grad: bfloat16 [8192, 2048], P(('dp', 'expert'), 'tensor'), may hold values from -3 to 3
- gate_up_proj: bfloat16 [64, 2, 1536, 2048], P('expert', None, 'tensor'), may hold values from -0.125 to 0.125
- down_proj: bfloat16 [64, 1536, 2048], P('expert', 'tensor'), may hold values from -0.15625 to 0.15625
Outputs:
- input_grad: bfloat16 [8192, 2048], P(('dp', 'expert'), 'tensor')
- gate_grad: float32 [8192, 8], P(('dp', 'expert'), 'tensor')
- gate_up_grad: bfloat16 [64, 2, 1536, 2048], P('expert', None, 'tensor', 'dp')
- down_grad: bfloat16 [64, 1536, 2048], P('expert', 'tensor', 'dp')
Inputs may be any that keep to these rules, and one draw needn't show every extreme that they name: `expert_ids`: among the routes of the 64 tokens of one index of dp and expert together, every expert is named exactly 8 times.
All inputs are finite; a program needn't handle non-finite values.
Results may differ from a plain program's by a relative error of at most 0.028.
Values may be sent and summed in bfloat16 or wider, within the bound.
No kernel may reach another device: no remote copies, remote signals or barrier semaphores. Data moves between devices by JAX's collectives and lax.ppermute only.
A program may use at most 64 MiB of HBM per device.

v0:
```python
import jax
import jax.numpy as jnp
from jax import lax
from jax.sharding import PartitionSpec as P


def silu_parts(pre_act):
    sigmoid_value = jax.nn.sigmoid(pre_act)
    return (pre_act * sigmoid_value, sigmoid_value * (1.0 + pre_act * (1.0 - sigmoid_value)))


def expert_work(rows_in, rows_grad, gate_up_proj, down_proj):
    sources, per_dest, feature_width = rows_in.shape
    local_experts = gate_up_proj.shape[0]
    capacity = per_dest // local_experts
    inputs = rows_in.reshape(sources, local_experts, capacity, feature_width)
    grad_rows = rows_grad.reshape(sources, local_experts, capacity, feature_width)
    projected = jnp.einsum(
        "sjcd,jgfd->sjcgf", inputs, gate_up_proj, preferred_element_type=jnp.float32
    )
    pre_gate = projected[:, :, :, 0]
    pre_up = projected[:, :, :, 1]
    activated, slope = silu_parts(pre_gate)
    hidden = (activated * pre_up).astype(jnp.bfloat16)
    hidden_grad = jnp.einsum(
        "sjcd,jfd->sjcf", grad_rows, down_proj, preferred_element_type=jnp.float32
    )
    gate_part = jnp.sum(hidden.astype(jnp.float32) * hidden_grad, axis=-1).astype(jnp.bfloat16)
    act_grad = jnp.stack([hidden_grad * pre_up * slope, hidden_grad * activated], axis=3).astype(
        jnp.bfloat16
    )
    row_part = jnp.einsum(
        "sjcgf,jgfd->sjcd", act_grad, gate_up_proj, preferred_element_type=jnp.float32
    ).astype(jnp.bfloat16)
    down_term = jnp.einsum("sjcf,sjcd->jfd", hidden, grad_rows, preferred_element_type=jnp.float32)
    gate_up_term = jnp.einsum(
        "sjcgf,sjcd->jgfd", act_grad, inputs, preferred_element_type=jnp.float32
    )
    return (
        row_part.reshape(sources, per_dest, feature_width),
        gate_part.reshape(sources, per_dest),
        gate_up_term,
        down_term,
    )


def local(
    hidden_states,
    expert_ids,
    gate_weights,
    completion_lengths,
    output_grad,
    gate_up_proj,
    down_proj,
):
    tokens_here, route_width = expert_ids.shape
    groups = lax.axis_size("expert")
    splits = lax.axis_size("tensor")
    local_experts = gate_up_proj.shape[0]
    block_units = gate_up_proj.shape[2]
    experts_all = local_experts * groups
    capacity = tokens_here * route_width // experts_all
    per_dest = local_experts * capacity
    slot_total = experts_all * capacity
    routes = tokens_here * route_width
    flat_ids = expert_ids.reshape(routes)
    expert_hits = (flat_ids[:, None] == jnp.arange(experts_all, dtype=jnp.int32)[None, :]).astype(
        jnp.int32
    )
    route_rank = jnp.sum(jnp.cumsum(expert_hits, axis=0) * expert_hits, axis=1) - 1
    slot_of_route = flat_ids * capacity + route_rank
    slot_match = jnp.arange(slot_total, dtype=jnp.int32)[:, None] == slot_of_route[None, :]
    placing = jnp.sum(
        slot_match.reshape(slot_total, tokens_here, route_width).astype(jnp.int32), axis=2
    ).astype(jnp.bfloat16)
    sequence_length = tokens_here * groups
    position = lax.axis_index("expert") * tokens_here + jnp.arange(tokens_here, dtype=jnp.int32)
    length_here = completion_lengths[0]
    keep_mask = (position < length_here).astype(jnp.float32)
    loss_scale = sequence_length / length_here.astype(jnp.float32)
    coefficient = gate_weights.astype(jnp.float32) * (keep_mask * loss_scale)[:, None]
    slot_coef = jnp.sum(jnp.where(slot_match, coefficient.reshape(routes)[None, :], 0.0), axis=1)
    send_rows = jnp.dot(placing, hidden_states, preferred_element_type=jnp.float32).astype(
        jnp.bfloat16
    )
    send_grad = (
        slot_coef[:, None] * jnp.dot(placing, output_grad, preferred_element_type=jnp.float32)
    ).astype(jnp.bfloat16)
    part_rows, part_grad = (
        lax.all_to_all(
            send_rows.reshape(groups, per_dest, -1),
            "expert",
            split_axis=0,
            concat_axis=0,
            tiled=True,
        ),
        lax.all_to_all(
            send_grad.reshape(groups, per_dest, -1),
            "expert",
            split_axis=0,
            concat_axis=0,
            tiled=True,
        ),
    )
    recv_rows, recv_grad = (
        lax.all_gather(part_rows, "tensor", axis=2, tiled=True),
        lax.all_gather(part_grad, "tensor", axis=2, tiled=True),
    )
    row_part, gate_part, gate_up_term, down_term = expert_work(
        recv_rows, recv_grad, gate_up_proj, down_proj
    )
    spread_gate = jnp.broadcast_to(
        gate_part.astype(jnp.float32)[:, :, None], gate_part.shape + (splits,)
    )
    row_sum, gate_sum = (
        lax.psum_scatter(
            row_part.astype(jnp.float32).astype(jnp.bfloat16),
            "tensor",
            scatter_dimension=2,
            tiled=True,
        ).astype(jnp.float32),
        lax.psum_scatter(
            spread_gate.astype(jnp.bfloat16), "tensor", scatter_dimension=2, tiled=True
        ).astype(jnp.float32),
    )
    back_rows, back_gate = (
        lax.all_to_all(
            row_sum.astype(jnp.bfloat16), "expert", split_axis=0, concat_axis=0, tiled=True
        ),
        lax.all_to_all(
            gate_sum.astype(jnp.bfloat16), "expert", split_axis=0, concat_axis=0, tiled=True
        ),
    )
    input_cols = jnp.dot(
        placing.T, back_rows.reshape(slot_total, -1), preferred_element_type=jnp.float32
    )
    route_full = jnp.sum(
        jnp.where(slot_match, back_gate.astype(jnp.float32).reshape(slot_total, 1), 0.0), axis=0
    ).reshape(tokens_here, route_width)
    share_width = route_width // splits
    route_start = lax.axis_index("tensor") * share_width
    gate_cols = lax.dynamic_slice_in_dim(route_full, route_start, share_width, 1)
    gate_here = lax.dynamic_slice_in_dim(gate_weights, route_start, share_width, 1).astype(
        jnp.float32
    )
    gate_grad = gate_cols / gate_here
    input_grad = input_cols.astype(jnp.bfloat16)
    feature_width = gate_up_proj.shape[3]
    gate_up_cols, down_cols = (
        lax.psum_scatter(
            gate_up_term.astype(jnp.bfloat16), "dp", scatter_dimension=3, tiled=True
        ).astype(jnp.float32),
        lax.psum_scatter(
            down_term.reshape(local_experts, 1, block_units, feature_width).astype(jnp.bfloat16),
            "dp",
            scatter_dimension=3,
            tiled=True,
        ).astype(jnp.float32),
    )
    gate_up_grad = gate_up_cols.astype(jnp.bfloat16)
    down_grad = down_cols.reshape(local_experts, block_units, -1).astype(jnp.bfloat16)
    return (input_grad, gate_grad, gate_up_grad, down_grad)


def solution(mesh):
    placed = (
        P(("dp", "expert"), "tensor"),
        P(("dp", "expert"), None),
        P(("dp", "expert"), None),
        P("dp"),
        P(("dp", "expert"), "tensor"),
        P("expert", None, "tensor", None),
        P("expert", "tensor", None),
    )
    return jax.shard_map(
        local,
        mesh=mesh,
        in_specs=placed,
        out_specs=(
            P(("dp", "expert"), "tensor"),
            P(("dp", "expert"), "tensor"),
            P("expert", None, "tensor", "dp"),
            P("expert", "tensor", "dp"),
        ),
        check_vma=False,
    )
```

profile of v0, /device:TPU:1, one launch (start us, length us, event | category | flops | bytes accessed | tf_op | source)
XLA Modules:
  0.0 585.6 jit_solution(4785787898685186697)
XLA Ops:
  7.2 0.0 copy-start
  7.2 0.0 copy-start.3
  7.2 0.0 copy-start.1
  7.2 0.0 all-gather.5.cloned.1.call-start
  7.2 0.9 copy.90
  8.2 0.1 eq.46
  8.3 0.1 eq.50
  8.4 1.2 reduce-window.6
  9.6 0.2 slice_reduce_fusion
  9.9 0.1 fusion.30
  10.0 0.0 copy-start.2
  10.0 0.1 sub.10
  10.1 0.1 copy.93
  10.1 0.7 multiply_add_fusion
  10.9 0.1 copy.94
  10.9 0.4 convert_reduce_fusion
  11.3 1.0 convolution_convert_fusion
  12.3 34.7 %all_to_all.20 = bf16[32,16,256]{2,1,0:T(8,128)(2,1)} all-to-all(bf16[32,16,256]{2,1,0:T(8,128)(2,1)S(1)} %bitcast.121), channel_id=1, replica_groups=mesh['dp'=4,'expert'=32,'tensor'=8] {'expert'}, dimensions={0} | all-to-all | bytes 524288 | tf_op jit(solution)/shard_map/all_to_all | solution.py:90
  47.0 0.0 all-gather.5.cloned.1.call-update
  47.0 0.0 all-gather.3.cloned.1.call-start
  47.8 0.0 copy-done.3
  47.8 0.1 copy.95
  47.9 0.1 broadcast_in_dim.40
  48.0 0.2 select_reduce_fusion.1
  48.2 0.0 copy-done.1
  48.2 0.3 fusion.23
  48.4 23.8 %all_to_all.21 = bf16[32,16,256]{2,1,0:T(8,128)(2,1)} all-to-all(bf16[32,16,256]{2,1,0:T(8,128)(2,1)S(1)} %bitcast.119), channel_id=1, replica_groups=mesh['dp'=4,'expert'=32,'tensor'=8] {'expert'}, dimensions={0} | all-to-all | bytes 524288 | tf_op jit(solution)/shard_map/all_to_all | solution.py:97
  72.2 0.0 all-gather.3.cloned.1.call-update
  72.2 0.0 reduce-scatter.7.cloned.1.call-start
  72.3 97.3 %all-gather.5.cloned.1.call-done = bf16[32,16,2048]{2,1,0:T(8,128)(2,1)} async-done(((bf16[32,16,256]{2,1,0:T(8,128)(2,1)}), bf16[32,16,2048]{2,1,0:T(8,128)(2,1)}) %all-gather.5.cloned.1.call-update) | async-done | bytes 2097168 | tf_op jit(solution)/shard_map/all_gather | solution.py:106
  169.5 3.8 fusion.13
  173.4 108.2 %all-gather.3.cloned.1.call-done = bf16[32,16,2048]{2,1,0:T(8,128)(2,1)} async-done(((bf16[32,16,256]{2,1,0:T(8,128)(2,1)}), bf16[32,16,2048]{2,1,0:T(8,128)(2,1)}) %all-gather.3.cloned.1.call-update) | async-done | bytes 2097168 | tf_op jit(solution)/shard_map/all_gather | solution.py:107
  281.6 4.1 multiply_reduce_fusion
  285.7 0.1 copy.101
  285.8 0.6 broadcast_in_dim.43
  286.4 0.0 reduce-scatter.7.cloned.1.call-update
  286.4 0.0 reduce-scatter.5.cloned.1.call-start
  286.5 2.3 fusion
  288.8 1.6 copy_bitcast_fusion
  290.4 0.0 reduce-scatter.5.cloned.1.call-update
  290.5 0.0 reduce-scatter.11.cloned.1.call-start
  290.5 0.0 copy-start.4
  290.5 3.6 fusion.4
  294.1 0.0 reduce-scatter.11.cloned.1.call-update
  294.1 0.0 reduce-scatter.9.cloned.1.call-start
  294.2 4.4 bitcast_convert_fusion
  298.6 0.0 reduce-scatter.9.cloned.1.call-update
  298.6 53.0 %reduce-scatter.7.cloned.1.call-done = bf16[32,16,1]{0,1,2:T(8,128)(2,1)} async-done(((bf16[32,16,8]{0,1,2:T(8,128)(2,1)}), bf16[32,16,1]{0,1,2:T(8,128)(2,1)}) %reduce-scatter.7.cloned.1.call-update) | async-done | bytes 1040 | tf_op jit(solution)/shard_map/reduce_scatter | solution.py:122
  351.6 0.8 copy.102
  352.4 23.8 %all_to_all.22 = bf16[32,16,1]{1,2,0:T(2,128)(2,1)} all-to-all(bf16[32,16,1]{1,2,0:T(2,128)(2,1)S(1)} %copy.102), channel_id=1, replica_groups=mesh['dp'=4,'expert'=32,'tensor'=8] {'expert'}, dimensions={0} | all-to-all | bytes 2048 | tf_op jit(solution)/shard_map/all_to_all | solution.py:130
  376.2 87.0 %reduce-scatter.5.cloned.1.call-done = bf16[32,16,256]{2,1,0:T(8,128)(2,1)} async-done(((bf16[32,16,2048]{2,1,0:T(8,128)(2,1)}), bf16[32,16,256]{2,1,0:T(8,128)(2,1)}) %reduce-scatter.5.cloned.1.call-update) | async-done | bytes 262160 | tf_op jit(solution)/shard_map/reduce_scatter | solution.py:116
  463.2 15.3 %all-to-all-start.2 = ((bf16[32,16,256]{2,1,0:T(8,128)(2,1)}), bf16[32,16,256]{2,1,0:T(8,128)(2,1)S(1)}, u32[]{:S(2)}, u32[]{:S(2)}) async-start(bf16[32,16,256]{2,1,0:T(8,128)(2,1)} %reduce-scatter.5.cloned.1.call-done), calls=%async_computation.3 | async-start | bytes 524288 | tf_op jit(solution)/shard_map/all_to_all | solution.py:127
  478.5 0.5 constant_dynamic-slice_fusion
  479.0 0.8 copy.121
  479.8 1.4 convert_reduce_fusion.1
  481.1 1.4 reshape.99
  482.5 1.4 select_reduce_fusion
  484.0 1.3 reshape.98
  485.3 1.4 convert_divide_fusion
  486.7 1.3 copy.107
  488.1 10.0 %all-to-all-done.2 = bf16[32,16,256]{2,1,0:T(8,128)(2,1)S(1)} async-done(((bf16[32,16,256]{2,1,0:T(8,128)(2,1)}), bf16[32,16,256]{2,1,0:T(8,128)(2,1)S(1)}, u32[]{:S(2)}, u32[]{:S(2)}) %all-to-all-start.2) | async-done | bytes 262176 | tf_op jit(solution)/shard_map/all_to_all | solution.py:127
  498.1 0.8 convolution_convert_fusion.1
  498.9 18.6 %reduce-scatter.11.cloned.1.call-done = bf16[2,1,192,512]{3,2,0,1:T(8,128)(2,1)} async-done(((bf16[2,1,192,2048]{3,2,0,1:T(8,128)(2,1)}), bf16[2,1,192,512]{3,2,0,1:T(8,128)(2,1)}) %reduce-scatter.11.cloned.1.call-update) | async-done | bytes 393232 | tf_op jit(solution)/shard_map/reduce_scatter | solution.py:153
  517.5 61.3 %reduce-scatter.9.cloned.1.call-done = bf16[2,2,192,512]{3,2,1,0:T(8,128)(2,1)} async-done(((bf16[2,2,192,2048]{3,2,1,0:T(8,128)(2,1)}), bf16[2,2,192,512]{3,2,1,0:T(8,128)(2,1)}) %reduce-scatter.9.cloned.1.call-update) | async-done | bytes 786448 | tf_op jit(solution)/shard_map/reduce_scatter | solution.py:150
  (9 shorter events, 0.1 us)
Async XLA Ops:
  7.2 162.4 %copy-start = (bf16[2,2,192,2048]{3,2,1,0:T(8,128)(2,1)S(1)}, bf16[2,2,192,2048]{3,2,1,0:T(8,128)(2,1)}, u32[]{:S(2)}) copy-start(bf16[2,2,192,2048]{3,2,1,0:T(8,128)(2,1)} %param.12) | copy-start | bytes 9437188
  7.2 40.6 %copy-start.3 = (bf16[64,8]{0,1:T(8,128)(2,1)S(1)}, bf16[64,8]{0,1:T(8,128)(2,1)}, u32[]{:S(2)}) copy-start(bf16[64,8]{0,1:T(8,128)(2,1)} %param.9) | copy-start | bytes 3076
  7.2 41.0 %copy-start.1 = (bf16[64,256]{1,0:T(8,128)(2,1)S(1)}, bf16[64,256]{1,0:T(8,128)(2,1)}, u32[]{:S(2)}) copy-start(bf16[64,256]{1,0:T(8,128)(2,1)} %param.11) | copy-start | bytes 98308
  7.2 162.3 %all-gather.5.cloned.1.call-start = ((), (), s32[]{:S(2)}) async-start(), calls=%async_computation.9 | async-start | bytes 2359296 | tf_op jit(solution)/shard_map/all_gather | solution.py:106
  10.0 163.4 %copy-start.2 = (s32[512]{0:T(512)}, s32[512]{0:T(512)S(1)}, u32[]{:S(2)}) copy-start(s32[512]{0:T(512)S(1)} %get-tuple-element.29) | copy-start | bytes 6148
  47.0 234.6 %all-gather.3.cloned.1.call-start = ((), (), s32[]{:S(2)}) async-start(), calls=%async_computation.8 | async-start | bytes 2359296 | tf_op jit(solution)/shard_map/all_gather | solution.py:107
  72.2 279.4 %reduce-scatter.7.cloned.1.call-start = ((), (), s32[]{:S(2)}) async-start(), calls=%async_computation.11 | async-start | bytes 36864 | tf_op jit(solution)/shard_map/reduce_scatter | solution.py:122
  286.4 176.7 %reduce-scatter.5.cloned.1.call-start = ((), (), s32[]{:S(2)}) async-start(), calls=%async_computation.10 | async-start | bytes 2359296 | tf_op jit(solution)/shard_map/reduce_scatter | solution.py:116
  290.5 227.0 %reduce-scatter.11.cloned.1.call-start = ((), (), s32[]{:S(2)}) async-start(), calls=%async_computation.13 | async-start | bytes 1966080 | tf_op jit(solution)/shard_map/reduce_scatter | solution.py:153
  290.5 3.7 copy-start.4
  294.1 284.6 %reduce-scatter.9.cloned.1.call-start = ((), (), s32[]{:S(2)}) async-start(), calls=%async_computation.12 | async-start | bytes 3932160 | tf_op jit(solution)/shard_map/reduce_scatter | solution.py:150
  463.2 34.9 %all-to-all-start.2 = ((bf16[32,16,256]{2,1,0:T(8,128)(2,1)}), bf16[32,16,256]{2,1,0:T(8,128)(2,1)S(1)}, u32[]{:S(2)}, u32[]{:S(2)}) async-start(bf16[32,16,256]{2,1,0:T(8,128)(2,1)} %reduce-scatter.5.cloned.1.call-done), calls=%async_computation.3 | async-start | bytes 524288 | tf_op jit(solution)/shard_map/all_to_all | solution.py:127
Sparse Core Ops, SparseCore 0:
  47.1 122.3 all-gather.4
  172.2 109.3 all-gather.2
  286.6 65.0 reduce-scatter.6
  355.3 107.8 reduce-scatter.4
  467.4 50.0 reduce-scatter.10
  521.7 56.9 reduce-scatter.8
where the time goes:
time: 586 us
  waiting for transfers between devices  435 us (74%)
  blocking collectives  82.2 us (14%)
  matrix products  20.3 us (3%)
  starting transfers between devices  15.6 us (3%)
  between operations  15 us (3%)
  local copies, waits for them, and re-layouts  10.2 us (2%)
  other arithmetic  6.91 us (1%)
    all_gather x1, waiting for transfers between devices, local(): lax.all_gather(part_grad, 'tensor', axis=2, tiled=True)  108 us
    all_gather x1, waiting for transfers between devices, local(): lax.all_gather(part_rows, 'tensor', axis=2, tiled=True)  97.3 us
    reduce_scatter x1, waiting for transfers between devices, local(): lax.psum_scatter(row_part.astype(jnp.float32).astype(jnp.bfloat16), 'tens...  87 us
    reduce_scatter x1, waiting for transfers between devices, local(): lax.psum_scatter(gate_up_term.astype(jnp.bfloat16), 'dp', scatter_dimensi...  61.3 us
    reduce_scatter x1, waiting for transfers between devices, local(): lax.psum_scatter(spread_gate.astype(jnp.bfloat16), 'tensor', scatter_dime...  53 us
    all_to_all x1, blocking collectives, local(): lax.all_to_all(send_rows.reshape(groups, per_dest, -1), 'expert', split_a...  34.7 us
    all_to_all x1, blocking collectives, local(): lax.all_to_all(gate_sum.astype(jnp.bfloat16), 'expert', split_axis=0, con...  23.8 us
    all_to_all x1, blocking collectives, local(): lax.all_to_all(send_grad.reshape(groups, per_dest, -1), 'expert', split_a...  23.8 us
  transfers between devices with their start and end apart: 7, of which 7 were waited for; matrix products, arithmetic and copies ran while one was open for 5% of the time, Pallas kernels for 0%

commit v1 on v0

v1 whole, which is shorter than its diff:
```python
import functools

import jax
import jax.numpy as jnp
from jax import lax
from jax.experimental import pallas as pl
from jax.experimental.pallas import tpu as pltpu
from jax.sharding import PartitionSpec as P

BF = jnp.bfloat16
F32 = jnp.float32
NY, NLO, NHI, NCORE = 4, 8, 4, 2
NZ = NLO * NHI
META = 128
NT_DIMS = (((1,), (1,)), ((), ()))
TN_DIMS = (((0,), (0,)), ((), ()))
PLANE = ("expert", "tensor")
VMEM = pl.BlockSpec(memory_space=pltpu.VMEM)
SMEM = pl.BlockSpec(memory_space=pltpu.SMEM)
LIMIT = 56 * 1024 * 1024


def place(y, z, core):
    return ((y * NLO + z % NLO) * NHI + z // NLO) * NCORE + core


def send(array, to):
    pairs = []
    for y in range(NY):
        for z in range(NZ):
            for core in range(NCORE):
                step = to(core)
                if step is None:
                    continue
                dy, dz, dcore = step
                there = place((y + dy) % NY, (z + dz) % NZ, (core + dcore) % NCORE)
                pairs.append((place(y, z, core), there))
    return lax.ppermute(array, PLANE, pairs)


def along_y(array, step):
    return send(array, lambda core: (step, 0, 0))


def along_z(array, step):
    return send(array, lambda core: (0, step, 0))


def to_other_core(array):
    return send(array, lambda core: (0, 0, 1))


def call(kernel, outs, *args, scalars=0, flops=0):
    moved = sum(a.size * a.dtype.itemsize for a in args)
    moved += sum(o.size * o.dtype.itemsize for o in outs)
    return pl.pallas_call(
        kernel,
        out_shape=outs,
        in_specs=[SMEM] * scalars + [VMEM] * (len(args) - scalars),
        out_specs=[VMEM] * len(outs),
        compiler_params=pltpu.CompilerParams(vmem_limit_bytes=LIMIT),
        cost_estimate=pl.CostEstimate(flops=flops, bytes_accessed=moved, transcendentals=0),
    )(*args)


def struct(shape, dtype=BF):
    return jax.ShapeDtypeStruct(shape, dtype)


def lanes(start, size):
    return pl.ds(pl.multiple_of(start, 128), size)


def gather_hi_kernel(where, own, before, after, across, out):
    hi = where[2]
    width = own.shape[1] // 2
    for block, step in ((own, 0), (before, NHI - 1), (after, 1), (across, 2)):
        at = ((hi + step) % NHI) * width
        out[:, lanes(at, width)] = block[:, :width]
        out[:, lanes(NHI * width + at, width)] = block[:, width:]


def gather_core_kernel(where, own, other, ids, weights, rows, grads):
    core = where[3]
    half = own.shape[1] // 2
    width = half // NHI
    for block, side in ((own, core), (other, 1 - core)):
        for hi in range(NHI):
            at = (hi * NCORE + side) * width
            rows[:, lanes(at, width)] = block[:, hi * width : (hi + 1) * width]
            grads[:, lanes(at, width)] = block[:, half + hi * width : half + (hi + 1) * width]
    top = ids.shape[1]
    lane = lax.broadcasted_iota(jnp.int32, (top, META), 1)
    row = lax.broadcasted_iota(jnp.int32, (top, META), 0)
    spread_ids = (lane == row).astype(F32).astype(BF)
    spread_weights = (lane == row + top).astype(F32).astype(BF)
    meta = jnp.dot(ids[...].astype(F32).astype(BF), spread_ids, preferred_element_type=F32)
    meta += jnp.dot(weights[...], spread_weights, preferred_element_type=F32)
    rows[:, 2 * half :] = meta.astype(BF)


def group_rows(core, received, fourth, own):
    blocks = [r[...] for r in received]
    last = jnp.where(core == 0, fourth[...].astype(F32), own[...].astype(F32)).astype(BF)
    return jnp.concatenate(blocks + [last], axis=0)


def select_rows_kernel(where, scale, first, second, third, fourth, own, *outs):
    sends, (placing, coefs, metas) = outs[:NY], outs[NY:]
    y, lo, core, length = where[0], where[1], where[3], where[4]
    tokens = own.shape[0]
    features = own.shape[1] - META
    total = placing.shape[1]
    slots = total // (NY * 2 * 4)
    blocks = group_rows(core, (first, second, third), fourth, own)
    meta = blocks[:, features:].astype(F32)
    metas[...] = meta
    slot = lax.broadcasted_iota(jnp.int32, (tokens, total), 1)
    expert = ((((y + slot // (8 * slots)) % NY) * NLO + lo) * 2 + (slot // (4 * slots)) % 2).astype(F32)
    rank_of = (slot % slots).astype(F32)
    group_of = (slot // slots) % 4
    token = lax.broadcasted_iota(jnp.int32, (tokens, total), 0)
    lower = (
        lax.broadcasted_iota(jnp.int32, (tokens, tokens), 0)
        >= lax.broadcasted_iota(jnp.int32, (tokens, tokens), 1)
    ).astype(F32).astype(BF)
    parts, weighted = [], []
    for group in range(4):
        named = meta[group * tokens : (group + 1) * tokens]
        hit = jnp.zeros((tokens, total), F32)
        weight = jnp.zeros((tokens, total), F32)
        for k in range(8):
            same = named[:, k : k + 1] == expert
            hit += same.astype(F32)
            weight += jnp.where(same, named[:, 8 + k : 9 + k], 0.0)
        hit = jnp.where(group_of == group, hit, 0.0)
        rank = jnp.dot(lower, hit.astype(BF), preferred_element_type=F32)
        placed = jnp.where(rank == rank_of + 1.0, hit, 0.0)
        step = group + 1
        offset = jnp.where(core == 0, -step, step if group < 3 else 0)
        position = (y * NLO + (lo + offset + NLO) % NLO) * tokens + token
        parts.append(placed)
        weighted.append(jnp.where(position < length, placed * weight, 0.0))
    place_matrix = jnp.concatenate(parts, axis=0).astype(BF)
    weight_matrix = jnp.concatenate(weighted, axis=0).astype(BF)
    placing[...] = place_matrix
    ones = jnp.ones((4 * tokens, META), BF)
    coefs[...] = lax.dot_general(weight_matrix, ones, TN_DIMS, preferred_element_type=F32) * scale[0]
    chosen = lax.dot_general(
        place_matrix, blocks[:, :features], TN_DIMS, preferred_element_type=F32
    ).astype(BF)
    share = total // NY
    for step in range(NY):
        sends[step][...] = chosen[step * share : (step + 1) * share]


def select_grads_kernel(where, placing, coefs, first, second, third, fourth, own, *sends):
    blocks = group_rows(where[3], (first, second, third), fourth, own)
    chosen = lax.dot_general(placing[...], blocks, TN_DIMS, preferred_element_type=F32)
    chosen = (chosen * coefs[:, :1]).astype(BF)
    share = placing.shape[1] // NY
    for step in range(NY):
        sends[step][...] = chosen[step * share : (step + 1) * share]


def of_expert(array, expert, share):
    half = share // 2
    return jnp.concatenate(
        [
            array[step * share + expert * half : step * share + (expert + 1) * half]
            for step in range(NY)
        ],
        axis=0,
    )


def expert_kernel(rows, grads, gate_up, down, gate_up_other, down_other, *outs):
    returns, (acts, acts_other) = outs[:NY], outs[NY:]
    share = rows.shape[0] // NY
    half = share // 2
    features = rows.shape[1]
    lane = lax.broadcasted_iota(jnp.int32, (half, META), 1)
    for expert in range(2):
        inputs = of_expert(rows, expert, share)
        cotangents = of_expert(grads, expert, share)
        back = jnp.zeros((NY * half, features), F32)
        gate = jnp.zeros((NY * half, 1), F32)
        for w_in, w_out, acts_here in ((gate_up, down, acts), (gate_up_other, down_other, acts_other)):
            w_gate, w_up = w_in[expert, 0], w_in[expert, 1]
            pre_gate = lax.dot_general(inputs, w_gate, NT_DIMS, preferred_element_type=F32)
            pre_up = lax.dot_general(inputs, w_up, NT_DIMS, preferred_element_type=F32)
            hidden_grad = lax.dot_general(cotangents, w_out[expert], NT_DIMS, preferred_element_type=F32)
            sigmoid = jax.nn.sigmoid(pre_gate)
            active = pre_gate * sigmoid
            slope = sigmoid * (1.0 + pre_gate * (1.0 - sigmoid))
            hidden = (active * pre_up).astype(BF)
            gate += jnp.sum(hidden.astype(F32) * hidden_grad, axis=1, keepdims=True)
            act_gate = (hidden_grad * pre_up * slope).astype(BF)
            act_up = (hidden_grad * active).astype(BF)
            acts_here[expert, 0] = act_gate
            acts_here[expert, 1] = act_up
            acts_here[expert, 2] = hidden
            back += jnp.dot(act_gate, w_gate, preferred_element_type=F32)
            back += jnp.dot(act_up, w_up, preferred_element_type=F32)
        back = back.astype(BF)
        for step in range(NY):
            here = slice(expert * half, (expert + 1) * half)
            there = slice(step * half, (step + 1) * half)
            returns[step][here, :features] = back[there]
            returns[step][here, features:] = jnp.where(lane == step * 2 + expert, gate[there], 0.0).astype(BF)


def weight_grad_kernel(rows, rows_other, grads, grads_other, acts, acts_other, out):
    share = rows.shape[0] // NY
    units = acts.shape[3]
    for expert in range(2):
        inputs = jnp.concatenate(
            [of_expert(rows, expert, share), of_expert(rows_other, expert, share)], axis=0
        )
        cotangents = jnp.concatenate(
            [of_expert(grads, expert, share), of_expert(grads_other, expert, share)], axis=0
        )
        for which, right, at in (
            (0, inputs, expert * 2 * units),
            (1, inputs, (expert * 2 + 1) * units),
            (2, cotangents, (4 + expert) * units),
        ):
            left = jnp.concatenate([acts[expert, which], acts_other[expert, which]], axis=0)
            out[at : at + units] = lax.dot_general(
                left, right, TN_DIMS, preferred_element_type=F32
            ).astype(BF)


def combine_kernel(where, placing, metas, first, second, third, fourth, *outs):
    y, lo = where[0], where[1]
    features = first.shape[1] - META
    width = features // (NHI * NCORE)
    back = jnp.concatenate([first[...], second[...], third[...], fourth[...]], axis=0)
    summed = jnp.dot(placing[...], back, preferred_element_type=F32)
    meta = metas[...]
    lane = lax.broadcasted_iota(jnp.int32, meta.shape, 1)
    gate = jnp.zeros(meta.shape, F32)
    for step in range(NY):
        for j in range(2):
            expert = (((y + step) % NY) * NLO + lo) * 2 + j
            at = features + step * 2 + j
            same = jnp.logical_and(meta == expert.astype(F32), lane < 8)
            gate += jnp.where(same, summed[:, at : at + 1], 0.0)
    gate = gate.astype(BF)
    tokens = outs[0].shape[0]
    for group in range(4):
        here = slice(group * tokens, (group + 1) * tokens)
        for core in range(NCORE):
            for hi in range(NHI):
                there = (hi * NCORE + core) * width
                at = (core * NHI + hi) * width
                outs[group][:, at : at + width] = summed[here, there : there + width].astype(BF)
        outs[group][:, features:] = gate[here]


def split_core_kernel(where, arrived, own, keep, give):
    core = where[3]
    half = (arrived.shape[1] - META) // 2
    mine = jnp.where(core == 1, 1.0, 0.0)
    for out, side in ((keep, core), (give, 1 - core)):
        at = lanes(side * half, half)
        out[:, :half] = (arrived[:, at].astype(F32) + mine * own[:, at].astype(F32)).astype(BF)
        out[:, half:] = (arrived[:, 2 * half :].astype(F32) + mine * own[:, 2 * half :].astype(F32)).astype(BF)


def split_hi_kernel(where, kept, arrived, *outs):
    hi = where[2]
    half = kept.shape[1] - META
    width = half // NHI
    gate = (kept[:, half:].astype(F32) + arrived[:, half:].astype(F32)).astype(BF)
    for step in range(NHI):
        at = lanes(((hi + step) % NHI) * width, width)
        outs[step][:, :width] = (kept[:, at].astype(F32) + arrived[:, at].astype(F32)).astype(BF)
        outs[step][:, width:] = gate


def finish_kernel(where, weights, own, before, after, across, input_grad, gate_grad):
    column = where[2] * NCORE + where[3]
    width = own.shape[1] - META
    total = own[...].astype(F32) + before[...].astype(F32)
    total += after[...].astype(F32) + across[...].astype(F32)
    input_grad[...] = total[:, :width].astype(BF)
    gate = total[:, width:]
    lane = lax.broadcasted_iota(jnp.int32, gate.shape, 1)
    route = lax.broadcasted_iota(jnp.int32, weights.shape, 1)
    top = jnp.sum(jnp.where(lane == column, gate, 0.0), axis=1, keepdims=True)
    under = jnp.sum(jnp.where(route == column, weights[...].astype(F32), 0.0), axis=1, keepdims=True)
    gate_grad[...] = top / under


def local(
    hidden_states,
    expert_ids,
    gate_weights,
    completion_lengths,
    output_grad,
    gate_up_proj,
    down_proj,
):
    tokens, width = hidden_states.shape
    features = width * NHI * NCORE
    units = gate_up_proj.shape[2]
    slots = tokens * expert_ids.shape[1] // (NY * NLO * 2)
    total = NY * 2 * 4 * slots
    share = total // NY
    expert_at, tensor_at = lax.axis_index("expert"), lax.axis_index("tensor")
    length = completion_lengths[0]
    where = jnp.stack(
        [expert_at // NLO, expert_at % NLO, tensor_at // NCORE, tensor_at % NCORE, length]
    ).astype(jnp.int32)
    scale = ((tokens * NY * NLO) / completion_lengths.astype(F32)).astype(F32)

    own = jnp.concatenate([hidden_states, output_grad], axis=1)
    before, after, across = along_z(own, NLO), along_z(own, -NLO), along_z(own, 2 * NLO)
    gate_up_other, down_other = to_other_core(gate_up_proj), to_other_core(down_proj)
    (half,) = call(
        gather_hi_kernel,
        [struct((tokens, 2 * NHI * width))],
        where, own, before, after, across, scalars=1,
    )
    rows, grads = call(
        gather_core_kernel,
        [struct((tokens, features + META)), struct((tokens, features))],
        where, half, to_other_core(half), expert_ids, gate_weights, scalars=1,
    )

    def onward(block):
        got, passed = [], block
        for _ in range(3):
            passed = send(passed, lambda core: (0, 1 if core == 0 else -1, 0))
            got.append(passed)
        got.append(send(passed, lambda core: (0, 1, 0) if core == 0 else None))
        return got

    row_blocks, grad_blocks = onward(rows), onward(grads)
    *row_sends, placing, coefs, metas = call(
        select_rows_kernel,
        [struct((share, features))] * NY
        + [struct((4 * tokens, total)), struct((total, META), F32), struct((4 * tokens, META), F32)],
        where, scale, *row_blocks, rows, scalars=2, flops=2 * 4 * tokens * total * features,
    )
    grad_sends = call(
        select_grads_kernel,
        [struct((share, features))] * NY,
        where, placing, coefs, *grad_blocks, grads, scalars=1, flops=2 * 4 * tokens * total * features,
    )

    def over_y(blocks, sign):
        return [blocks[0]] + [along_y(blocks[step], sign * step) for step in range(1, NY)]

    expert_rows = jnp.concatenate(over_y(row_sends, 1), axis=0)
    expert_grads = jnp.concatenate(over_y(grad_sends, 1), axis=0)
    rows_other, grads_other = to_other_core(expert_rows), to_other_core(expert_grads)
    acts_shape = struct((2, 3, total // 2, units))
    *returns, acts, acts_theirs = call(
        expert_kernel,
        [struct((share, features + META))] * NY + [acts_shape, acts_shape],
        expert_rows, expert_grads, gate_up_proj, down_proj, gate_up_other, down_other,
        flops=2 * total * 2 * units * features * 5,
    )
    acts_other = to_other_core(acts_theirs)
    returned = over_y(returns, -1)
    (weight_parts,) = call(
        weight_grad_kernel,
        [struct((6 * units, features))],
        expert_rows, rows_other, expert_grads, grads_other, acts, acts_other,
        flops=2 * 2 * total * units * features * 3,
    )
    weight_grads = lax.psum_scatter(weight_parts, "dp", scatter_dimension=1, tiled=True)

    sums = call(
        combine_kernel,
        [struct((tokens, features + META))] * 4,
        where, placing, metas, *returned, scalars=1, flops=2 * 4 * tokens * total * features,
    )
    passed = send(sums[3], lambda core: (0, -1, 0) if core == 0 else None)
    for group in (2, 1, 0):
        passed = (passed.astype(F32) + sums[group].astype(F32)).astype(BF)
        passed = send(passed, lambda core: (0, -1 if core == 0 else 1, 0))
    half_shape = struct((tokens, features // 2 + META))
    keep, give = call(split_core_kernel, [half_shape, half_shape], where, passed, sums[3], scalars=1)
    pieces = call(
        split_hi_kernel,
        [struct((tokens, width + META))] * NHI,
        where, keep, to_other_core(give), scalars=1,
    )
    input_grad, gate_grad = call(
        finish_kernel,
        [struct((tokens, width)), struct((tokens, 1), F32)],
        where,
        gate_weights,
        pieces[0],
        along_z(pieces[1], NLO),
        along_z(pieces[3], -NLO),
        along_z(pieces[2], 2 * NLO),
        scalars=1,
    )
    part = weight_grads.shape[1]
    gate_up_grad = weight_grads[: 4 * units].reshape(2, 2, units, part)
    down_grad = weight_grads[4 * units :].reshape(2, units, part)
    return (input_grad, gate_grad, gate_up_grad, down_grad)


def solution(mesh):
    placed = (
        P(("dp", "expert"), "tensor"),
        P(("dp", "expert"), None),
        P(("dp", "expert"), None),
        P("dp"),
        P(("dp", "expert"), "tensor"),
        P("expert", None, "tensor", None),
        P("expert", "tensor", None),
    )
    return jax.shard_map(
        local,
        mesh=mesh,
        in_specs=placed,
        out_specs=(
            P(("dp", "expert"), "tensor"),
            P(("dp", "expert"), "tensor"),
            P("expert", None, "tensor", "dp"),
            P("expert", "tensor", "dp"),
        ),
        check_vma=False,
    )
```

time: 586 us -> 329 us (0.56)
  the two profiles are of different devices: /device:TPU:1 before, /device:TPU:4 now
where the time goes in v1:
time: 329 us; the launch traced here: 327 us
  starting transfers between devices  170 us (52%)
  waiting for transfers between devices  83.1 us (25%)
  Pallas kernels  34.4 us (10%)
  local copies, waits for them, and re-layouts  21.3 us (6%)
  between operations  15.4 us (5%)
    ppermute x34, starting transfers between devices, send(): return lax.ppermute(array, PLANE, pairs)  170 us
    ppermute x34, waiting for transfers between devices, send(): return lax.ppermute(array, PLANE, pairs)  83 us
    pallas_call x10, Pallas kernels, call(): pl.pallas_call(kernel, out_shape=outs, in_specs=[SMEM] * scalars + [VMEM]...  34.4 us
    unnamed x70, local copies, waits for them, and re-layouts  16.1 us
  transfers between devices with their start and end apart: 35, of which 19 were waited for; matrix products, arithmetic and copies ran while one was open for 3% of the time, Pallas kernels for 8%

profile of v1, /device:TPU:4, one launch (start us, length us, event | category | flops | bytes accessed | tf_op | source)
XLA Modules:
  0.0 327.1 jit_solution(15585819515460922873)
XLA Ops:
  8.7 15.7 %collective-permute-start = (bf16[64,512]{1,0:T(8,128)(2,1)S(1)}, bf16[64,512]{1,0:T(8,128)(2,1)S(1)}, u32[]{:S(2)}, u32[]{:S(2)}) collective-permute-start(bf16[64,512]{1,0:T(8,128)(2,1)S(1)} %constant_dynamic-update-slice_fusion.own), channel_id=1, source_target_pairs={{0,2},{1,3},{8,10},{9,11},{16,18},{17,19},{24,26},{25,27},{32,34},... | collective-permute-start | bytes 196616 | tf_op jit(solution)/shard_map/ppermute | solution.py:38
  24.5 9.2 %collective-permute-start.1 = (bf16[64,512]{1,0:T(8,128)(2,1)S(1)}, bf16[64,512]{1,0:T(8,128)(2,1)S(1)}, u32[]{:S(2)}, u32[]{:S(2)}) collective-permute-start(bf16[64,512]{1,0:T(8,128)(2,1)S(1)} %constant_dynamic-update-slice_fusion.own), channel_id=1, source_target_pairs={{0,6},{1,7},{8,14},{9,15},{16,22},{17,23},{24,30},{25,31},{32,38},... | collective-permute-start | bytes 196616 | tf_op jit(solution)/shard_map/ppermute | solution.py:38
  33.7 18.6 %collective-permute-start.2 = (bf16[64,512]{1,0:T(8,128)(2,1)S(1)}, bf16[64,512]{1,0:T(8,128)(2,1)S(1)}, u32[]{:S(2)}, u32[]{:S(2)}) collective-permute-start(bf16[64,512]{1,0:T(8,128)(2,1)S(1)} %constant_dynamic-update-slice_fusion.own), channel_id=1, source_target_pairs={{0,4},{1,5},{8,12},{9,13},{16,20},{17,21},{24,28},{25,29},{32,36},... | collective-permute-start | bytes 196616 | tf_op jit(solution)/shard_map/ppermute | solution.py:38
  53.6 5.9 %collective-permute-done.2.across = bf16[64,512]{1,0:T(8,128)(2,1)S(1)} collective-permute-done((bf16[64,512]{1,0:T(8,128)(2,1)S(1)}, bf16[64,512]{1,0:T(8,128)(2,1)S(1)}, u32[]{:S(2)}, u32[]{:S(2)}) %collective-permute-start.2) | collective-permute-done | bytes 65568 | tf_op jit(solution)/shard_map/ppermute | solution.py:38
  60.1 1.7 shard_map.102.own
  61.8 1.9 collective-permute-start.3
  65.1 1.4 copy.11.ids
  67.2 1.9 shard_map.103
  69.1 15.5 %collective-permute-start.4 = (bf16[64,2176]{1,0:T(8,128)(2,1)}, bf16[64,2176]{1,0:T(8,128)(2,1)S(1)}, u32[]{:S(2)}, u32[]{:S(2)}) collective-permute-start(bf16[64,2176]{1,0:T(8,128)(2,1)} %get-tuple-element.35.own), channel_id=1, source_target_pairs={{0,8},{1,63},{8,16},{9,1},{16,24},{17,9},{24,32},{25,17},{32,40},{... | collective-permute-start | bytes 835592 | tf_op jit(solution)/shard_map/ppermute | solution.py:38
  84.6 4.5 %collective-permute-done.4.first = bf16[64,2176]{1,0:T(8,128)(2,1)S(1)} collective-permute-done((bf16[64,2176]{1,0:T(8,128)(2,1)}, bf16[64,2176]{1,0:T(8,128)(2,1)S(1)}, u32[]{:S(2)}, u32[]{:S(2)}) %collective-permute-start.4) | collective-permute-done | bytes 278560 | tf_op jit(solution)/shard_map/ppermute | solution.py:38
  89.1 4.2 %collective-permute-start.5 = (bf16[64,2176]{1,0:T(8,128)(2,1)S(1)}, bf16[64,2176]{1,0:T(8,128)(2,1)S(1)}, u32[]{:S(2)}, u32[]{:S(2)}) collective-permute-start(bf16[64,2176]{1,0:T(8,128)(2,1)S(1)} %collective-permute-done.4.first), channel_id=1, source_target_pairs={{0,8},{1,63},{8,16},{9,1},{16,24},{17,9},{24,32},{25,17},{32,40},{... | collective-permute-start | bytes 835592 | tf_op jit(solution)/shard_map/ppermute | solution.py:38
  93.3 1.9 collective-permute-start.11
  95.2 1.9 collective-permute-start.18
  97.2 1.6 collective-permute-done.5.second
  98.8 3.0 collective-permute-start.6
  103.0 1.9 collective-permute-start.12
  104.9 3.5 %collective-permute-done.6.third = bf16[64,2176]{1,0:T(8,128)(2,1)S(1)} collective-permute-done((bf16[64,2176]{1,0:T(8,128)(2,1)S(1)}, bf16[64,2176]{1,0:T(8,128)(2,1)S(1)}, u32[]{:S(2)}, u32[]{:S(2)}) %collective-permute-start.6) | collective-permute-done | bytes 278560 | tf_op jit(solution)/shard_map/ppermute | solution.py:38
  108.4 1.9 collective-permute-start.7
  110.3 2.1 collective-permute-done.12.second
  112.4 1.9 collective-permute-start.13
  114.4 7.5 %collective-permute-done.13.third = bf16[64,2048]{1,0:T(8,128)(2,1)S(1)} collective-permute-done((bf16[64,2048]{1,0:T(8,128)(2,1)S(1)}, bf16[64,2048]{1,0:T(8,128)(2,1)S(1)}, u32[]{:S(2)}, u32[]{:S(2)}) %collective-permute-start.13) | collective-permute-done | bytes 262176 | tf_op jit(solution)/shard_map/ppermute | solution.py:38
  121.9 1.9 collective-permute-start.14
  123.8 1.9 collective-permute-start.19
  126.5 3.5 %shard_map.104 = (bf16[64,2048]{1,0:T(8,128)(2,1)}, bf16[64,2048]{1,0:T(8,128)(2,1)}, bf16[64,2048]{1,0:T(8,128)(2,1)}, bf16[64,2048]{1,0:T(8,128)(2,1)}, bf16[2...) custom-call(s32[5]{0:T(128)} %stack.19.where, f32[1]{0:T(128)S(6)} %div.24.scale, ...), custom_call_target="tpu_custom_call" | custom-call | flops 268435456 | bytes 2834456 | tf_op jit(solution)/shard_map/pallas_call | solution.py:56
  130.1 3.5 %collective-permute-start.8 = (bf16[64,2048]{1,0:T(8,128)(2,1)}, bf16[64,2048]{1,0:T(8,128)(2,1)S(1)}, u32[]{:S(2)}, u32[]{:S(2)}) collective-permute-start(bf16[64,2048]{1,0:T(8,128)(2,1)} %get-tuple-element.39), channel_id=1, source_target_pairs={{0,64},{1,65},{8,72},{9,73},{16,80},{17,81},{24,88},{25,89},{32,96... | collective-permute-start | bytes 786440 | tf_op jit(solution)/shard_map/ppermute | solution.py:38
  134.5 4.8 %collective-permute-start.9 = (bf16[64,2048]{1,0:T(8,128)(2,1)}, bf16[64,2048]{1,0:T(8,128)(2,1)S(1)}, u32[]{:S(2)}, u32[]{:S(2)}) collective-permute-start(bf16[64,2048]{1,0:T(8,128)(2,1)} %get-tuple-element.40), channel_id=1, source_target_pairs={{0,128},{1,129},{8,136},{9,137},{16,144},{17,145},{24,152},{25,153... | collective-permute-start | bytes 786440 | tf_op jit(solution)/shard_map/ppermute | solution.py:38
  139.4 3.3 collective-permute-start.10
  142.7 2.8 shard_map.105
  146.4 2.6 collective-permute-start.15
  149.0 4.5 %collective-permute-start.16 = (bf16[64,2048]{1,0:T(8,128)(2,1)}, bf16[64,2048]{1,0:T(8,128)(2,1)S(1)}, u32[]{:S(2)}, u32[]{:S(2)}) collective-permute-start(bf16[64,2048]{1,0:T(8,128)(2,1)} %get-tuple-element.46), channel_id=1, source_target_pairs={{0,128},{1,129},{8,136},{9,137},{16,144},{17,145},{24,152},{25,153... | collective-permute-start | bytes 786440 | tf_op jit(solution)/shard_map/ppermute | solution.py:38
  153.6 4.5 %collective-permute-start.17 = (bf16[64,2048]{1,0:T(8,128)(2,1)}, bf16[64,2048]{1,0:T(8,128)(2,1)S(1)}, u32[]{:S(2)}, u32[]{:S(2)}) collective-permute-start(bf16[64,2048]{1,0:T(8,128)(2,1)} %get-tuple-element.47), channel_id=1, source_target_pairs={{0,192},{1,193},{8,200},{9,201},{16,208},{17,209},{24,216},{25,217... | collective-permute-start | bytes 786440 | tf_op jit(solution)/shard_map/ppermute | solution.py:38
  158.2 5.0 %collective-permute-done.15 = bf16[64,2048]{1,0:T(8,128)(2,1)S(1)} collective-permute-done((bf16[64,2048]{1,0:T(8,128)(2,1)}, bf16[64,2048]{1,0:T(8,128)(2,1)S(1)}, u32[]{:S(2)}, u32[]{:S(2)}) %collective-permute-start.15) | collective-permute-done | bytes 262176 | tf_op jit(solution)/shard_map/ppermute | solution.py:38
  163.2 1.9 collective-permute-start.31
  165.8 1.9 collective-permute-start.32
  168.9 1.6 copy-done.2
  170.5 10.3 %shard_map.106 = (bf16[64,2176]{1,0:T(8,128)(2,1)}, bf16[64,2176]{1,0:T(8,128)(2,1)}, bf16[64,2176]{1,0:T(8,128)(2,1)}, bf16[64,2176]{1,0:T(8,128)(2,1)}, bf16[2...) custom-call(bf16[256,2048]{1,0:T(8,128)(2,1)} %copy-done.1, bf16[256,2048]{1,0:T(8,128)(2,1)} %copy-done, ...), custom_call_target="tpu_custom_call" | custom-call | flops 2013265920 | bytes 13238272 | tf_op jit(solution)/shard_map/pallas_call | solution.py:56
  180.8 2.4 collective-permute-start.33
  183.3 1.5 collective-permute-done.33.acts_other
  185.5 6.0 %shard_map.111 = bf16[1152,2048]{1,0:T(8,128)(2,1)} custom-call(bf16[256,2048]{1,0:T(8,128)(2,1)} %copy-done.1, bf16[256,2048]{1,0:T(8,128)(2,1)} %copy-done.4, bf16[256,2048]{1,0:T(8,128)(2,1)} %copy-done, bf16[256,2048]{1,0:T(8,128)(2,1)} %collective-permute-done.32.grads_other, bf16[2,3,128,192]{3,2,1,0:T(8,128)(2,1)} %get-tuple-element.64.acts, ...), custom_call_target="tpu_custom_call" | custom-call | flops 1207959552 | bytes 9502720 | tf_op jit(solution)/shard_map/pallas_call | solution.py:56
  192.5 4.6 %collective-permute-start.20 = (bf16[64,2176]{1,0:T(8,128)(2,1)S(1)}, bf16[64,2176]{1,0:T(8,128)(2,1)S(1)}, u32[]{:S(2)}, u32[]{:S(2)}) collective-permute-start(bf16[64,2176]{1,0:T(8,128)(2,1)S(1)} %copy-done.29), channel_id=1, source_target_pairs={{0,192},{1,193},{8,200},{9,201},{16,208},{17,209},{24,216},{25,217... | collective-permute-start | bytes 835592 | tf_op jit(solution)/shard_map/ppermute | solution.py:38
  197.1 2.5 collective-permute-start.21
  199.5 2.2 collective-permute-start.22
  201.8 7.7 %collective-permute-done.20.second = bf16[64,2176]{1,0:T(8,128)(2,1)S(1)} collective-permute-done((bf16[64,2176]{1,0:T(8,128)(2,1)S(1)}, bf16[64,2176]{1,0:T(8,128)(2,1)S(1)}, u32[]{:S(2)}, u32[]{:S(2)}) %collective-permute-start.20) | collective-permute-done | bytes 278560 | tf_op jit(solution)/shard_map/ppermute | solution.py:38
  210.0 5.1 %collective-permute-done.22.fourth = bf16[64,2176]{1,0:T(8,128)(2,1)S(1)} collective-permute-done((bf16[64,2176]{1,0:T(8,128)(2,1)S(1)}, bf16[64,2176]{1,0:T(8,128)(2,1)S(1)}, u32[]{:S(2)}, u32[]{:S(2)}) %collective-permute-start.22) | collective-permute-done | bytes 278560 | tf_op jit(solution)/shard_map/ppermute | solution.py:38
  215.8 3.1 shard_map.107
  218.9 5.2 %collective-permute-start.23 = (bf16[64,2176]{1,0:T(8,128)(2,1)}, bf16[64,2176]{1,0:T(8,128)(2,1)S(1)}, u32[]{:S(2)}, u32[]{:S(2)}) collective-permute-start(bf16[64,2176]{1,0:T(8,128)(2,1)} %get-tuple-element.52.own), channel_id=1, source_target_pairs={{0,62},{8,0},{16,8},{24,16},{32,24},{40,32},{48,40},{56,48},{2,56}... | collective-permute-start | bytes 835592 | tf_op jit(solution)/shard_map/ppermute | solution.py:38
  224.1 4.4 %collective-permute-done.23 = bf16[64,2176]{1,0:T(8,128)(2,1)S(1)} collective-permute-done((bf16[64,2176]{1,0:T(8,128)(2,1)}, bf16[64,2176]{1,0:T(8,128)(2,1)S(1)}, u32[]{:S(2)}, u32[]{:S(2)}) %collective-permute-start.23) | collective-permute-done | bytes 278560 | tf_op jit(solution)/shard_map/ppermute | solution.py:38
  229.4 5.5 %collective-permute-start.24 = (bf16[64,2176]{1,0:T(8,128)(2,1)S(1)}, bf16[64,2176]{1,0:T(8,128)(2,1)S(1)}, u32[]{:S(2)}, u32[]{:S(2)}) collective-permute-start(bf16[64,2176]{1,0:T(8,128)(2,1)S(1)} %add_convert_fusion.2), channel_id=1, source_target_pairs={{0,62},{1,9},{8,0},{9,17},{16,8},{17,25},{24,16},{25,33},{32,24},{... | collective-permute-start | bytes 835592 | tf_op jit(solution)/shard_map/ppermute | solution.py:38
  234.9 4.0 %collective-permute-done.24 = bf16[64,2176]{1,0:T(8,128)(2,1)S(1)} collective-permute-done((bf16[64,2176]{1,0:T(8,128)(2,1)S(1)}, bf16[64,2176]{1,0:T(8,128)(2,1)S(1)}, u32[]{:S(2)}, u32[]{:S(2)}) %collective-permute-start.24) | collective-permute-done | bytes 278560 | tf_op jit(solution)/shard_map/ppermute | solution.py:38
  240.0 5.6 %collective-permute-start.25 = (bf16[64,2176]{1,0:T(8,128)(2,1)S(1)}, bf16[64,2176]{1,0:T(8,128)(2,1)S(1)}, u32[]{:S(2)}, u32[]{:S(2)}) collective-permute-start(bf16[64,2176]{1,0:T(8,128)(2,1)S(1)} %add_convert_fusion.1), channel_id=1, source_target_pairs={{0,62},{1,9},{8,0},{9,17},{16,8},{17,25},{24,16},{25,33},{32,24},{... | collective-permute-start | bytes 835592 | tf_op jit(solution)/shard_map/ppermute | solution.py:38
  245.6 4.0 %collective-permute-done.25 = bf16[64,2176]{1,0:T(8,128)(2,1)S(1)} collective-permute-done((bf16[64,2176]{1,0:T(8,128)(2,1)S(1)}, bf16[64,2176]{1,0:T(8,128)(2,1)S(1)}, u32[]{:S(2)}, u32[]{:S(2)}) %collective-permute-start.25) | collective-permute-done | bytes 278560 | tf_op jit(solution)/shard_map/ppermute | solution.py:38
  250.7 5.6 %collective-permute-start.26 = (bf16[64,2176]{1,0:T(8,128)(2,1)S(1)}, bf16[64,2176]{1,0:T(8,128)(2,1)S(1)}, u32[]{:S(2)}, u32[]{:S(2)}) collective-permute-start(bf16[64,2176]{1,0:T(8,128)(2,1)S(1)} %add_convert_fusion), channel_id=1, source_target_pairs={{0,62},{1,9},{8,0},{9,17},{16,8},{17,25},{24,16},{25,33},{32,24},{... | collective-permute-start | bytes 835592 | tf_op jit(solution)/shard_map/ppermute | solution.py:38
  256.3 4.0 %collective-permute-done.26.arrived = bf16[64,2176]{1,0:T(8,128)(2,1)S(1)} collective-permute-done((bf16[64,2176]{1,0:T(8,128)(2,1)S(1)}, bf16[64,2176]{1,0:T(8,128)(2,1)S(1)}, u32[]{:S(2)}, u32[]{:S(2)}) %collective-permute-start.26) | collective-permute-done | bytes 278560 | tf_op jit(solution)/shard_map/ppermute | solution.py:38
  261.1 1.8 shard_map.108
  262.9 1.9 collective-permute-start.27
  264.8 1.5 collective-permute-done.27.arrived
  267.0 1.7 shard_map.109
  268.7 3.3 %collective-permute-start.28 = (bf16[64,384]{1,0:T(8,128)(2,1)}, bf16[64,384]{1,0:T(8,128)(2,1)S(1)}, u32[]{:S(2)}, u32[]{:S(2)}) collective-permute-start(bf16[64,384]{1,0:T(8,128)(2,1)} %get-tuple-element.59), channel_id=1, source_target_pairs={{0,2},{1,3},{8,10},{9,11},{16,18},{17,19},{24,26},{25,27},{32,34},... | collective-permute-start | bytes 147464 | tf_op jit(solution)/shard_map/ppermute | solution.py:38
  272.0 11.2 %collective-permute-start.29 = (bf16[64,384]{1,0:T(8,128)(2,1)}, bf16[64,384]{1,0:T(8,128)(2,1)S(1)}, u32[]{:S(2)}, u32[]{:S(2)}) collective-permute-start(bf16[64,384]{1,0:T(8,128)(2,1)} %get-tuple-element.60), channel_id=1, source_target_pairs={{0,6},{1,7},{8,14},{9,15},{16,22},{17,23},{24,30},{25,31},{32,38},... | collective-permute-start | bytes 147464 | tf_op jit(solution)/shard_map/ppermute | solution.py:38
  283.3 11.3 %collective-permute-start.30 = (bf16[64,384]{1,0:T(8,128)(2,1)}, bf16[64,384]{1,0:T(8,128)(2,1)S(1)}, u32[]{:S(2)}, u32[]{:S(2)}) collective-permute-start(bf16[64,384]{1,0:T(8,128)(2,1)} %get-tuple-element.61), channel_id=1, source_target_pairs={{0,4},{1,5},{8,12},{9,13},{16,20},{17,21},{24,28},{25,29},{32,36},... | collective-permute-start | bytes 147464 | tf_op jit(solution)/shard_map/ppermute | solution.py:38
  294.6 18.2 %collective-permute-done.30.across = bf16[64,384]{1,0:T(8,128)(2,1)S(1)} collective-permute-done((bf16[64,384]{1,0:T(8,128)(2,1)}, bf16[64,384]{1,0:T(8,128)(2,1)S(1)}, u32[]{:S(2)}, u32[]{:S(2)}) %collective-permute-start.30) | collective-permute-done | bytes 49184 | tf_op jit(solution)/shard_map/ppermute | solution.py:38
  313.4 1.6 shard_map.110
  316.4 2.1 slice.8
  318.4 1.8 slice.9
  (96 shorter events, 20.0 us)
Async XLA Ops:
  7.2 309.2 %reduce-scatter.2.cloned.1.call-start = ((), (), s32[]{:S(2)}) async-start(), calls=%async_computation.1 | async-start | bytes 5898240 | tf_op jit(solution)/shard_map/reduce_scatter | solution.py:374
  8.7 50.8 %copy-start.19 = (bf16[64,512]{1,0:T(8,128)(2,1)}, bf16[64,512]{1,0:T(8,128)(2,1)S(1)}, u32[]{:S(2)}) copy-start(bf16[64,512]{1,0:T(8,128)(2,1)S(1)} %constant_dynamic-update-slice_fusion.own) | copy-start | bytes 196612
  8.7 44.8 %collective-permute-start = (bf16[64,512]{1,0:T(8,128)(2,1)S(1)}, bf16[64,512]{1,0:T(8,128)(2,1)S(1)}, u32[]{:S(2)}, u32[]{:S(2)}) collective-permute-start(bf16[64,512]{1,0:T(8,128)(2,1)S(1)} %constant_dynamic-update-slice_fusion.own), channel_id=1, source_target_pairs={{0,2},{1,3},{8,10},{9,11},{16,18},{17,19},{24,26},{25,27},{32,34},... | collective-permute-start | bytes 196616 | tf_op jit(solution)/shard_map/ppermute | solution.py:38
  24.5 29.1 %collective-permute-start.1 = (bf16[64,512]{1,0:T(8,128)(2,1)S(1)}, bf16[64,512]{1,0:T(8,128)(2,1)S(1)}, u32[]{:S(2)}, u32[]{:S(2)}) collective-permute-start(bf16[64,512]{1,0:T(8,128)(2,1)S(1)} %constant_dynamic-update-slice_fusion.own), channel_id=1, source_target_pairs={{0,6},{1,7},{8,14},{9,15},{16,22},{17,23},{24,30},{25,31},{32,38},... | collective-permute-start | bytes 196616 | tf_op jit(solution)/shard_map/ppermute | solution.py:38
  33.7 25.8 %collective-permute-start.2 = (bf16[64,512]{1,0:T(8,128)(2,1)S(1)}, bf16[64,512]{1,0:T(8,128)(2,1)S(1)}, u32[]{:S(2)}, u32[]{:S(2)}) collective-permute-start(bf16[64,512]{1,0:T(8,128)(2,1)S(1)} %constant_dynamic-update-slice_fusion.own), channel_id=1, source_target_pairs={{0,4},{1,5},{8,12},{9,13},{16,20},{17,21},{24,28},{25,29},{32,36},... | collective-permute-start | bytes 196616 | tf_op jit(solution)/shard_map/ppermute | solution.py:38
  53.6 5.9 %copy-start.21 = (bf16[64,512]{1,0:T(8,128)(2,1)}, bf16[64,512]{1,0:T(8,128)(2,1)S(1)}, u32[]{:S(2)}) copy-start(bf16[64,512]{1,0:T(8,128)(2,1)S(1)} %collective-permute-done.before) | copy-start | bytes 196612
  53.6 5.9 %copy-start.22 = (bf16[64,512]{1,0:T(8,128)(2,1)}, bf16[64,512]{1,0:T(8,128)(2,1)S(1)}, u32[]{:S(2)}) copy-start(bf16[64,512]{1,0:T(8,128)(2,1)S(1)} %collective-permute-done.1.after) | copy-start | bytes 196612
  59.5 0.6 copy-start.23
  61.8 4.7 %collective-permute-start.3 = (bf16[64,2048]{1,0:T(8,128)(2,1)}, bf16[64,2048]{1,0:T(8,128)(2,1)S(1)}, u32[]{:S(2)}, u32[]{:S(2)}) collective-permute-start(bf16[64,2048]{1,0:T(8,128)(2,1)} %shard_map.102.own), channel_id=1, source_target_pairs={{0,1},{1,0},{8,9},{9,8},{16,17},{17,16},{24,25},{25,24},{32,33},{3... | collective-permute-start | bytes 786440 | tf_op jit(solution)/shard_map/ppermute | solution.py:38
  66.5 0.7 copy-start.14
  69.1 20.0 %collective-permute-start.4 = (bf16[64,2176]{1,0:T(8,128)(2,1)}, bf16[64,2176]{1,0:T(8,128)(2,1)S(1)}, u32[]{:S(2)}, u32[]{:S(2)}) collective-permute-start(bf16[64,2176]{1,0:T(8,128)(2,1)} %get-tuple-element.35.own), channel_id=1, source_target_pairs={{0,8},{1,63},{8,16},{9,1},{16,24},{17,9},{24,32},{25,17},{32,40},{... | collective-permute-start | bytes 835592 | tf_op jit(solution)/shard_map/ppermute | solution.py:38
  89.1 36.7 %copy-start.10 = (bf16[64,2176]{1,0:T(8,128)(2,1)}, bf16[64,2176]{1,0:T(8,128)(2,1)S(1)}, u32[]{:S(2)}) copy-start(bf16[64,2176]{1,0:T(8,128)(2,1)S(1)} %collective-permute-done.4.first) | copy-start | bytes 835588
  89.1 9.6 %collective-permute-start.5 = (bf16[64,2176]{1,0:T(8,128)(2,1)S(1)}, bf16[64,2176]{1,0:T(8,128)(2,1)S(1)}, u32[]{:S(2)}, u32[]{:S(2)}) collective-permute-start(bf16[64,2176]{1,0:T(8,128)(2,1)S(1)} %collective-permute-done.4.first), channel_id=1, source_target_pairs={{0,8},{1,63},{8,16},{9,1},{16,24},{17,9},{24,32},{25,17},{32,40},{... | collective-permute-start | bytes 835592 | tf_op jit(solution)/shard_map/ppermute | solution.py:38
  93.3 9.7 %collective-permute-start.11 = (bf16[64,2048]{1,0:T(8,128)(2,1)}, bf16[64,2048]{1,0:T(8,128)(2,1)S(1)}, u32[]{:S(2)}, u32[]{:S(2)}) collective-permute-start(bf16[64,2048]{1,0:T(8,128)(2,1)} %get-tuple-element.43.own), channel_id=1, source_target_pairs={{0,8},{1,63},{8,16},{9,1},{16,24},{17,9},{24,32},{25,17},{32,40},{... | collective-permute-start | bytes 786440 | tf_op jit(solution)/shard_map/ppermute | solution.py:38
  95.2 72.5 %collective-permute-start.18 = (bf16[2,2,192,2048]{3,2,1,0:T(8,128)(2,1)}, bf16[2,2,192,2048]{3,2,1,0:T(8,128)(2,1)S(1)}, u32[]{:S(2)}, u32[]{:S(2)}) collective-permute-start(bf16[2,2,192,2048]{3,2,1,0:T(8,128)(2,1)} %gate_up.1), channel_id=1, source_target_pairs={{0,1},{1,0},{8,9},{9,8},{16,17},{17,16},{24,25},{25,24},{32,33},{3... | collective-permute-start | bytes 9437192 | tf_op jit(solution)/shard_map/ppermute | solution.py:38
  98.8 27.1 %copy-start.11 = (bf16[64,2176]{1,0:T(8,128)(2,1)}, bf16[64,2176]{1,0:T(8,128)(2,1)S(1)}, u32[]{:S(2)}) copy-start(bf16[64,2176]{1,0:T(8,128)(2,1)S(1)} %collective-permute-done.5.second) | copy-start | bytes 835588
  98.8 9.6 %collective-permute-start.6 = (bf16[64,2176]{1,0:T(8,128)(2,1)S(1)}, bf16[64,2176]{1,0:T(8,128)(2,1)S(1)}, u32[]{:S(2)}, u32[]{:S(2)}) collective-permute-start(bf16[64,2176]{1,0:T(8,128)(2,1)S(1)} %collective-permute-done.5.second), channel_id=1, source_target_pairs={{0,8},{1,63},{8,16},{9,1},{16,24},{17,9},{24,32},{25,17},{32,40},{... | collective-permute-start | bytes 835592 | tf_op jit(solution)/shard_map/ppermute | solution.py:38
  103.0 39.7 %copy-start.15 = (bf16[64,2048]{1,0:T(8,128)(2,1)}, bf16[64,2048]{1,0:T(8,128)(2,1)S(1)}, u32[]{:S(2)}) copy-start(bf16[64,2048]{1,0:T(8,128)(2,1)S(1)} %collective-permute-done.11.first) | copy-start | bytes 786436
  103.0 9.5 %collective-permute-start.12 = (bf16[64,2048]{1,0:T(8,128)(2,1)S(1)}, bf16[64,2048]{1,0:T(8,128)(2,1)S(1)}, u32[]{:S(2)}, u32[]{:S(2)}) collective-permute-start(bf16[64,2048]{1,0:T(8,128)(2,1)S(1)} %collective-permute-done.11.first), channel_id=1, source_target_pairs={{0,8},{1,63},{8,16},{9,1},{16,24},{17,9},{24,32},{25,17},{32,40},{... | collective-permute-start | bytes 786440 | tf_op jit(solution)/shard_map/ppermute | solution.py:38
  108.4 17.4 %copy-start.12 = (bf16[64,2176]{1,0:T(8,128)(2,1)}, bf16[64,2176]{1,0:T(8,128)(2,1)S(1)}, u32[]{:S(2)}) copy-start(bf16[64,2176]{1,0:T(8,128)(2,1)S(1)} %collective-permute-done.6.third) | copy-start | bytes 835588
  108.4 17.4 %collective-permute-start.7 = (bf16[64,2176]{1,0:T(8,128)(2,1)S(1)}, bf16[64,2176]{1,0:T(8,128)(2,1)S(1)}, u32[]{:S(2)}, u32[]{:S(2)}) collective-permute-start(bf16[64,2176]{1,0:T(8,128)(2,1)S(1)} %collective-permute-done.6.third), channel_id=1, source_target_pairs={{0,8},{8,16},{16,24},{24,32},{32,40},{40,48},{48,56},{56,2},{2,10}... | collective-permute-start | bytes 835592 | tf_op jit(solution)/shard_map/ppermute | solution.py:38
  112.4 30.2 %copy-start.16 = (bf16[64,2048]{1,0:T(8,128)(2,1)}, bf16[64,2048]{1,0:T(8,128)(2,1)S(1)}, u32[]{:S(2)}) copy-start(bf16[64,2048]{1,0:T(8,128)(2,1)S(1)} %collective-permute-done.12.second) | copy-start | bytes 786436
  112.4 9.5 %collective-permute-start.13 = (bf16[64,2048]{1,0:T(8,128)(2,1)S(1)}, bf16[64,2048]{1,0:T(8,128)(2,1)S(1)}, u32[]{:S(2)}, u32[]{:S(2)}) collective-permute-start(bf16[64,2048]{1,0:T(8,128)(2,1)S(1)} %collective-permute-done.12.second), channel_id=1, source_target_pairs={{0,8},{1,63},{8,16},{9,1},{16,24},{17,9},{24,32},{25,17},{32,40},{... | collective-permute-start | bytes 786440 | tf_op jit(solution)/shard_map/ppermute | solution.py:38
  121.9 20.8 %copy-start.17 = (bf16[64,2048]{1,0:T(8,128)(2,1)}, bf16[64,2048]{1,0:T(8,128)(2,1)S(1)}, u32[]{:S(2)}) copy-start(bf16[64,2048]{1,0:T(8,128)(2,1)S(1)} %collective-permute-done.13.third) | copy-start | bytes 786436
  121.9 17.4 %collective-permute-start.14 = (bf16[64,2048]{1,0:T(8,128)(2,1)S(1)}, bf16[64,2048]{1,0:T(8,128)(2,1)S(1)}, u32[]{:S(2)}, u32[]{:S(2)}) collective-permute-start(bf16[64,2048]{1,0:T(8,128)(2,1)S(1)} %collective-permute-done.13.third), channel_id=1, source_target_pairs={{0,8},{8,16},{16,24},{24,32},{32,40},{40,48},{48,56},{56,2},{2,10}... | collective-permute-start | bytes 786440 | tf_op jit(solution)/shard_map/ppermute | solution.py:38
  123.8 43.9 %collective-permute-start.19 = (bf16[2,192,2048]{2,1,0:T(8,128)(2,1)}, bf16[2,192,2048]{2,1,0:T(8,128)(2,1)S(1)}, u32[]{:S(2)}, u32[]{:S(2)}) collective-permute-start(bf16[2,192,2048]{2,1,0:T(8,128)(2,1)} %down.1), channel_id=1, source_target_pairs={{0,1},{1,0},{8,9},{9,8},{16,17},{17,16},{24,25},{25,24},{32,33},{3... | collective-permute-start | bytes 4718600 | tf_op jit(solution)/shard_map/ppermute | solution.py:38
  125.8 0.7 copy-start.13
  130.1 16.3 %collective-permute-start.8 = (bf16[64,2048]{1,0:T(8,128)(2,1)}, bf16[64,2048]{1,0:T(8,128)(2,1)S(1)}, u32[]{:S(2)}, u32[]{:S(2)}) collective-permute-start(bf16[64,2048]{1,0:T(8,128)(2,1)} %get-tuple-element.39), channel_id=1, source_target_pairs={{0,64},{1,65},{8,72},{9,73},{16,80},{17,81},{24,88},{25,89},{32,96... | collective-permute-start | bytes 786440 | tf_op jit(solution)/shard_map/ppermute | solution.py:38
  134.5 14.5 %collective-permute-start.9 = (bf16[64,2048]{1,0:T(8,128)(2,1)}, bf16[64,2048]{1,0:T(8,128)(2,1)S(1)}, u32[]{:S(2)}, u32[]{:S(2)}) collective-permute-start(bf16[64,2048]{1,0:T(8,128)(2,1)} %get-tuple-element.40), channel_id=1, source_target_pairs={{0,128},{1,129},{8,136},{9,137},{16,144},{17,145},{24,152},{25,153... | collective-permute-start | bytes 786440 | tf_op jit(solution)/shard_map/ppermute | solution.py:38
  139.4 3.3 %copy-start.18 = (bf16[64,2048]{1,0:T(8,128)(2,1)}, bf16[64,2048]{1,0:T(8,128)(2,1)S(1)}, u32[]{:S(2)}) copy-start(bf16[64,2048]{1,0:T(8,128)(2,1)S(1)} %collective-permute-done.14.fourth) | copy-start | bytes 786436
  139.4 14.2 %collective-permute-start.10 = (bf16[64,2048]{1,0:T(8,128)(2,1)}, bf16[64,2048]{1,0:T(8,128)(2,1)S(1)}, u32[]{:S(2)}, u32[]{:S(2)}) collective-permute-start(bf16[64,2048]{1,0:T(8,128)(2,1)} %get-tuple-element.41), channel_id=1, source_target_pairs={{0,192},{1,193},{8,200},{9,201},{16,208},{17,209},{24,216},{25,217... | collective-permute-start | bytes 786440 | tf_op jit(solution)/shard_map/ppermute | solution.py:38
  146.4 16.8 %collective-permute-start.15 = (bf16[64,2048]{1,0:T(8,128)(2,1)}, bf16[64,2048]{1,0:T(8,128)(2,1)S(1)}, u32[]{:S(2)}, u32[]{:S(2)}) collective-permute-start(bf16[64,2048]{1,0:T(8,128)(2,1)} %get-tuple-element.45), channel_id=1, source_target_pairs={{0,64},{1,65},{8,72},{9,73},{16,80},{17,81},{24,88},{25,89},{32,96... | collective-permute-start | bytes 786440 | tf_op jit(solution)/shard_map/ppermute | solution.py:38
  149.0 16.1 %collective-permute-start.16 = (bf16[64,2048]{1,0:T(8,128)(2,1)}, bf16[64,2048]{1,0:T(8,128)(2,1)S(1)}, u32[]{:S(2)}, u32[]{:S(2)}) collective-permute-start(bf16[64,2048]{1,0:T(8,128)(2,1)} %get-tuple-element.46), channel_id=1, source_target_pairs={{0,128},{1,129},{8,136},{9,137},{16,144},{17,145},{24,152},{25,153... | collective-permute-start | bytes 786440 | tf_op jit(solution)/shard_map/ppermute | solution.py:38
  153.6 12.1 %collective-permute-start.17 = (bf16[64,2048]{1,0:T(8,128)(2,1)}, bf16[64,2048]{1,0:T(8,128)(2,1)S(1)}, u32[]{:S(2)}, u32[]{:S(2)}) collective-permute-start(bf16[64,2048]{1,0:T(8,128)(2,1)} %get-tuple-element.47), channel_id=1, source_target_pairs={{0,192},{1,193},{8,200},{9,201},{16,208},{17,209},{24,216},{25,217... | collective-permute-start | bytes 786440 | tf_op jit(solution)/shard_map/ppermute | solution.py:38
  158.2 9.6 %copy-start.1 = (bf16[256,2048]{1,0:T(8,128)(2,1)}, bf16[256,2048]{1,0:T(8,128)(2,1)S(1)}, u32[]{:S(2)}) copy-start(bf16[256,2048]{1,0:T(8,128)(2,1)S(1)} %constant_dynamic-update-slice_fusion.2.rows) | copy-start | bytes 3145732
  163.2 20.0 %collective-permute-start.31 = (bf16[256,2048]{1,0:T(8,128)(2,1)S(1)}, bf16[256,2048]{1,0:T(8,128)(2,1)S(1)}, u32[]{:S(2)}, u32[]{:S(2)}) collective-permute-start(bf16[256,2048]{1,0:T(8,128)(2,1)S(1)} %constant_dynamic-update-slice_fusion.2.rows), channel_id=1, source_target_pairs={{0,1},{1,0},{8,9},{9,8},{16,17},{17,16},{24,25},{25,24},{32,33},{3... | collective-permute-start | bytes 3145736 | tf_op jit(solution)/shard_map/ppermute | solution.py:38
  165.8 2.0 copy-start
  165.8 17.5 %collective-permute-start.32 = (bf16[256,2048]{1,0:T(8,128)(2,1)S(1)}, bf16[256,2048]{1,0:T(8,128)(2,1)}, u32[]{:S(2)}, u32[]{:S(2)}) collective-permute-start(bf16[256,2048]{1,0:T(8,128)(2,1)S(1)} %constant_dynamic-update-slice_fusion.6.grads), channel_id=1, source_target_pairs={{0,1},{1,0},{8,9},{9,8},{16,17},{17,16},{24,25},{25,24},{32,33},{3... | collective-permute-start | bytes 3145736 | tf_op jit(solution)/shard_map/ppermute | solution.py:38
  167.7 1.2 copy-start.3
  168.9 1.6 copy-start.2
  180.8 3.9 %collective-permute-start.33 = (bf16[2,3,128,192]{3,2,1,0:T(8,128)(2,1)}, bf16[2,3,128,192]{3,2,1,0:T(8,128)(2,1)S(1)}, u32[]{:S(2)}, u32[]{:S(2)}) collective-permute-start(bf16[2,3,128,192]{3,2,1,0:T(8,128)(2,1)} %get-tuple-element.65), channel_id=1, source_target_pairs={{0,1},{1,0},{8,9},{9,8},{16,17},{17,16},{24,25},{25,24},{32,33},{3... | collective-permute-start | bytes 884744 | tf_op jit(solution)/shard_map/ppermute | solution.py:38
  183.3 1.5 copy-start.4
  184.8 0.7 copy-start.5
  191.5 1.0 copy-start.29
  191.5 5.5 %copy-start.28 = (bf16[64,2176]{1,0:T(8,128)(2,1)S(1)}, bf16[64,2176]{1,0:T(8,128)(2,1)}, u32[]{:S(2)}) copy-start(bf16[64,2176]{1,0:T(8,128)(2,1)} %get-tuple-element.50) | copy-start | bytes 835588
  191.5 8.0 %copy-start.27 = (bf16[64,2176]{1,0:T(8,128)(2,1)S(1)}, bf16[64,2176]{1,0:T(8,128)(2,1)}, u32[]{:S(2)}) copy-start(bf16[64,2176]{1,0:T(8,128)(2,1)} %get-tuple-element.51) | copy-start | bytes 835588
  192.5 17.0 %collective-permute-start.20 = (bf16[64,2176]{1,0:T(8,128)(2,1)S(1)}, bf16[64,2176]{1,0:T(8,128)(2,1)S(1)}, u32[]{:S(2)}, u32[]{:S(2)}) collective-permute-start(bf16[64,2176]{1,0:T(8,128)(2,1)S(1)} %copy-done.29), channel_id=1, source_target_pairs={{0,192},{1,193},{8,200},{9,201},{16,208},{17,209},{24,216},{25,217... | collective-permute-start | bytes 835592 | tf_op jit(solution)/shard_map/ppermute | solution.py:38
  197.1 13.0 %collective-permute-start.21 = (bf16[64,2176]{1,0:T(8,128)(2,1)S(1)}, bf16[64,2176]{1,0:T(8,128)(2,1)S(1)}, u32[]{:S(2)}, u32[]{:S(2)}) collective-permute-start(bf16[64,2176]{1,0:T(8,128)(2,1)S(1)} %copy-done.28), channel_id=1, source_target_pairs={{0,128},{1,129},{8,136},{9,137},{16,144},{17,145},{24,152},{25,153... | collective-permute-start | bytes 835592 | tf_op jit(solution)/shard_map/ppermute | solution.py:38
  199.5 15.5 %collective-permute-start.22 = (bf16[64,2176]{1,0:T(8,128)(2,1)S(1)}, bf16[64,2176]{1,0:T(8,128)(2,1)S(1)}, u32[]{:S(2)}, u32[]{:S(2)}) collective-permute-start(bf16[64,2176]{1,0:T(8,128)(2,1)S(1)} %copy-done.27), channel_id=1, source_target_pairs={{0,64},{1,65},{8,72},{9,73},{16,80},{17,81},{24,88},{25,89},{32,96... | collective-permute-start | bytes 835592 | tf_op jit(solution)/shard_map/ppermute | solution.py:38
  209.5 5.6 %copy-start.6 = (bf16[64,2176]{1,0:T(8,128)(2,1)}, bf16[64,2176]{1,0:T(8,128)(2,1)S(1)}, u32[]{:S(2)}) copy-start(bf16[64,2176]{1,0:T(8,128)(2,1)S(1)} %collective-permute-done.20.second) | copy-start | bytes 835588
  210.0 5.1 %copy-start.7 = (bf16[64,2176]{1,0:T(8,128)(2,1)}, bf16[64,2176]{1,0:T(8,128)(2,1)S(1)}, u32[]{:S(2)}) copy-start(bf16[64,2176]{1,0:T(8,128)(2,1)S(1)} %collective-permute-done.21.third) | copy-start | bytes 835588
  215.1 0.7 copy-start.8
  218.9 9.5 %collective-permute-start.23 = (bf16[64,2176]{1,0:T(8,128)(2,1)}, bf16[64,2176]{1,0:T(8,128)(2,1)S(1)}, u32[]{:S(2)}, u32[]{:S(2)}) collective-permute-start(bf16[64,2176]{1,0:T(8,128)(2,1)} %get-tuple-element.52.own), channel_id=1, source_target_pairs={{0,62},{8,0},{16,8},{24,16},{32,24},{40,32},{48,40},{56,48},{2,56}... | collective-permute-start | bytes 835592 | tf_op jit(solution)/shard_map/ppermute | solution.py:38
  229.4 9.5 %collective-permute-start.24 = (bf16[64,2176]{1,0:T(8,128)(2,1)S(1)}, bf16[64,2176]{1,0:T(8,128)(2,1)S(1)}, u32[]{:S(2)}, u32[]{:S(2)}) collective-permute-start(bf16[64,2176]{1,0:T(8,128)(2,1)S(1)} %add_convert_fusion.2), channel_id=1, source_target_pairs={{0,62},{1,9},{8,0},{9,17},{16,8},{17,25},{24,16},{25,33},{32,24},{... | collective-permute-start | bytes 835592 | tf_op jit(solution)/shard_map/ppermute | solution.py:38
  240.0 9.6 %collective-permute-start.25 = (bf16[64,2176]{1,0:T(8,128)(2,1)S(1)}, bf16[64,2176]{1,0:T(8,128)(2,1)S(1)}, u32[]{:S(2)}, u32[]{:S(2)}) collective-permute-start(bf16[64,2176]{1,0:T(8,128)(2,1)S(1)} %add_convert_fusion.1), channel_id=1, source_target_pairs={{0,62},{1,9},{8,0},{9,17},{16,8},{17,25},{24,16},{25,33},{32,24},{... | collective-permute-start | bytes 835592 | tf_op jit(solution)/shard_map/ppermute | solution.py:38
  250.7 9.7 %collective-permute-start.26 = (bf16[64,2176]{1,0:T(8,128)(2,1)S(1)}, bf16[64,2176]{1,0:T(8,128)(2,1)S(1)}, u32[]{:S(2)}, u32[]{:S(2)}) collective-permute-start(bf16[64,2176]{1,0:T(8,128)(2,1)S(1)} %add_convert_fusion), channel_id=1, source_target_pairs={{0,62},{1,9},{8,0},{9,17},{16,8},{17,25},{24,16},{25,33},{32,24},{... | collective-permute-start | bytes 835592 | tf_op jit(solution)/shard_map/ppermute | solution.py:38
  260.3 0.7 copy-start.9
  262.9 3.5 %collective-permute-start.27 = (bf16[64,1152]{1,0:T(8,128)(2,1)}, bf16[64,1152]{1,0:T(8,128)(2,1)S(1)}, u32[]{:S(2)}, u32[]{:S(2)}) collective-permute-start(bf16[64,1152]{1,0:T(8,128)(2,1)} %get-tuple-element.57), channel_id=1, source_target_pairs={{0,1},{1,0},{8,9},{9,8},{16,17},{17,16},{24,25},{25,24},{32,33},{3... | collective-permute-start | bytes 442376 | tf_op jit(solution)/shard_map/ppermute | solution.py:38
  266.3 0.7 copy-start.20
  268.7 25.9 %collective-permute-start.28 = (bf16[64,384]{1,0:T(8,128)(2,1)}, bf16[64,384]{1,0:T(8,128)(2,1)S(1)}, u32[]{:S(2)}, u32[]{:S(2)}) collective-permute-start(bf16[64,384]{1,0:T(8,128)(2,1)} %get-tuple-element.59), channel_id=1, source_target_pairs={{0,2},{1,3},{8,10},{9,11},{16,18},{17,19},{24,26},{25,27},{32,34},... | collective-permute-start | bytes 147464 | tf_op jit(solution)/shard_map/ppermute | solution.py:38
  272.0 22.6 %collective-permute-start.29 = (bf16[64,384]{1,0:T(8,128)(2,1)}, bf16[64,384]{1,0:T(8,128)(2,1)S(1)}, u32[]{:S(2)}, u32[]{:S(2)}) collective-permute-start(bf16[64,384]{1,0:T(8,128)(2,1)} %get-tuple-element.60), channel_id=1, source_target_pairs={{0,6},{1,7},{8,14},{9,15},{16,22},{17,23},{24,30},{25,31},{32,38},... | collective-permute-start | bytes 147464 | tf_op jit(solution)/shard_map/ppermute | solution.py:38
  283.3 29.6 %collective-permute-start.30 = (bf16[64,384]{1,0:T(8,128)(2,1)}, bf16[64,384]{1,0:T(8,128)(2,1)S(1)}, u32[]{:S(2)}, u32[]{:S(2)}) collective-permute-start(bf16[64,384]{1,0:T(8,128)(2,1)} %get-tuple-element.61), channel_id=1, source_target_pairs={{0,4},{1,5},{8,12},{9,13},{16,20},{17,21},{24,28},{25,29},{32,36},... | collective-permute-start | bytes 147464 | tf_op jit(solution)/shard_map/ppermute | solution.py:38
  294.6 18.2 %copy-start.24 = (bf16[64,384]{1,0:T(8,128)(2,1)}, bf16[64,384]{1,0:T(8,128)(2,1)S(1)}, u32[]{:S(2)}) copy-start(bf16[64,384]{1,0:T(8,128)(2,1)S(1)} %collective-permute-done.28.before) | copy-start | bytes 147460
  294.6 18.2 %copy-start.25 = (bf16[64,384]{1,0:T(8,128)(2,1)}, bf16[64,384]{1,0:T(8,128)(2,1)S(1)}, u32[]{:S(2)}) copy-start(bf16[64,384]{1,0:T(8,128)(2,1)S(1)} %collective-permute-done.29.after) | copy-start | bytes 147460
  (1 other events, 0.6 us)
Sparse Core Ops, SparseCore 0:
  191.6 57.3 reduce-scatter.1

commit v2 on v1

v2 whole, which is shorter than its diff:
```python
import functools

import jax
import jax.numpy as jnp
from jax import lax
from jax.experimental import pallas as pl
from jax.experimental.pallas import tpu as pltpu
from jax.sharding import PartitionSpec as P

BF = jnp.bfloat16
F32 = jnp.float32
NY, NLO, NHI, NCORE = 4, 8, 4, 2
NZ = NLO * NHI
META = 128
NT_DIMS = (((1,), (1,)), ((), ()))
TN_DIMS = (((0,), (0,)), ((), ()))
PLANE = ("expert", "tensor")
VMEM = pl.BlockSpec(memory_space=pltpu.VMEM)
SMEM = pl.BlockSpec(memory_space=pltpu.SMEM)
LIMIT = 56 * 1024 * 1024


def place(y, z, core):
    return ((y * NLO + z % NLO) * NHI + z // NLO) * NCORE + core


def send(array, to):
    pairs = []
    for y in range(NY):
        for z in range(NZ):
            for core in range(NCORE):
                step = to(core)
                if step is None:
                    continue
                dy, dz, dcore = step
                there = place((y + dy) % NY, (z + dz) % NZ, (core + dcore) % NCORE)
                pairs.append((place(y, z, core), there))
    return lax.ppermute(array, PLANE, pairs)


def swap_y(array):
    groups = [[y * NLO + lo for y in range(NY)] for lo in range(NLO)]
    return lax.all_to_all(
        array, "expert", split_axis=0, concat_axis=0, tiled=True, axis_index_groups=groups
    )


def swap_hi(array):
    groups = [[hi * NCORE + core for hi in range(NHI)] for core in range(NCORE)]
    return lax.all_to_all(
        array, "tensor", split_axis=0, concat_axis=0, tiled=True, axis_index_groups=groups
    )


def to_other_core(array):
    return send(array, lambda core: (0, 0, 1))


def call(kernel, outs, *args, scalars=0, flops=0):
    moved = sum(a.size * a.dtype.itemsize for a in args)
    moved += sum(o.size * o.dtype.itemsize for o in outs)
    return pl.pallas_call(
        kernel,
        out_shape=outs,
        in_specs=[SMEM] * scalars + [VMEM] * (len(args) - scalars),
        out_specs=[VMEM] * len(outs),
        compiler_params=pltpu.CompilerParams(vmem_limit_bytes=LIMIT),
        cost_estimate=pl.CostEstimate(flops=flops, bytes_accessed=moved, transcendentals=0),
    )(*args)


def struct(shape, dtype=BF):
    return jax.ShapeDtypeStruct(shape, dtype)


def eye(size):
    row = lax.broadcasted_iota(jnp.int32, (size, size), 0)
    column = lax.broadcasted_iota(jnp.int32, (size, size), 1)
    return (row == column).astype(F32).astype(BF)


def group_blocks(core, received, fourth, own):
    last = jnp.where(core == 0, fourth[...].astype(F32), own[...].astype(F32)).astype(BF)
    return [r[...] for r in received] + [last]


def select_kernel(where, scale, *refs):
    row_refs, grad_refs, (sends, placing, metas) = refs[:5], refs[5:10], refs[10:]
    y, lo, core, length = where[0], where[1], where[3], where[4]
    parts = NHI * NCORE
    tokens = grad_refs[0].shape[0] // parts
    width = grad_refs[0].shape[1]
    total = placing.shape[0]
    share = total // NY
    slots = share // 8
    rows = group_blocks(core, row_refs[:3], row_refs[3], row_refs[4])
    grads = group_blocks(core, grad_refs[:3], grad_refs[3], grad_refs[4])
    slot = lax.broadcasted_iota(jnp.int32, (tokens, total), 1)
    expert = (((slot // share) * NLO + lo) * 2 + (slot // (4 * slots)) % 2).astype(F32)
    rank_of = (slot % slots).astype(F32)
    group_of = (slot // slots) % 4
    token = lax.broadcasted_iota(jnp.int32, (tokens, total), 0)
    lower = (
        lax.broadcasted_iota(jnp.int32, (tokens, tokens), 0)
        >= lax.broadcasted_iota(jnp.int32, (tokens, tokens), 1)
    ).astype(F32).astype(BF)
    placed_parts, weighted = [], []
    for group in range(4):
        packed = rows[group][parts * tokens :, :tokens]
        named = lax.dot_general(eye(tokens), packed, NT_DIMS, preferred_element_type=F32)
        metas[group * tokens : (group + 1) * tokens] = named
        hit = jnp.zeros((tokens, total), F32)
        weight = jnp.zeros((tokens, total), F32)
        for k in range(8):
            same = named[:, k : k + 1] == expert
            hit += same.astype(F32)
            weight += jnp.where(same, named[:, 8 + k : 9 + k], 0.0)
        hit = jnp.where(group_of == group, hit, 0.0)
        rank = jnp.dot(lower, hit.astype(BF), preferred_element_type=F32)
        placed = jnp.where(rank == rank_of + 1.0, hit, 0.0)
        step = group + 1
        offset = jnp.where(core == 0, -step, step if group < 3 else 0)
        position = (y * NLO + (lo + offset + NLO) % NLO) * tokens + token
        placed_parts.append(placed)
        weighted.append(jnp.where(position < length, placed * weight, 0.0))
    matrix = jnp.concatenate(placed_parts, axis=0).T.astype(BF)
    weight_matrix = jnp.concatenate(weighted, axis=0).astype(BF)
    placing[...] = matrix
    ones = jnp.ones((4 * tokens, width), BF)
    coefs = lax.dot_general(weight_matrix, ones, TN_DIMS, preferred_element_type=F32) * scale[0]
    for blocks, start in ((rows, 0), (grads, parts * width)):
        for part in range(parts):
            here = jnp.concatenate([b[part * tokens : (part + 1) * tokens] for b in blocks], axis=0)
            chosen = jnp.dot(matrix, here, preferred_element_type=F32)
            if start:
                chosen = chosen * coefs
            chosen = chosen.astype(BF)
            at = start + part * width
            for step in range(NY):
                sends[step, :, at : at + width] = chosen[step * share : (step + 1) * share]


def of_expert(routes, expert, start, size):
    half = routes.shape[1] // 2
    here = slice(expert * half, (expert + 1) * half)
    return jnp.concatenate([routes[step, here, start : start + size] for step in range(NY)], axis=0)


def expert_kernel(where, routes, gate_up, down, gate_up_other, down_other, returns, acts, acts_other):
    half = routes.shape[1] // 2
    features = routes.shape[2] // 2
    y = where[0]
    units = down.shape[1]
    lane = lax.broadcasted_iota(jnp.int32, (half, META), 1)
    for expert in range(2):
        inputs = of_expert(routes, expert, 0, features).T
        cotangents = of_expert(routes, expert, features, features).T
        back = jnp.zeros((NY * half, features), F32)
        gate = jnp.zeros((1, NY * half), F32)
        for w_in, w_out, acts_here in ((gate_up, down, acts), (gate_up_other, down_other, acts_other)):
            w_gate, w_up = w_in[expert, 0], w_in[expert, 1]
            pre_gate = jnp.dot(w_gate, inputs, preferred_element_type=F32)
            pre_up = jnp.dot(w_up, inputs, preferred_element_type=F32)
            hidden_grad = jnp.dot(w_out[expert], cotangents, preferred_element_type=F32)
            sigmoid = jax.nn.sigmoid(pre_gate)
            active = pre_gate * sigmoid
            slope = sigmoid * (1.0 + pre_gate * (1.0 - sigmoid))
            hidden = (active * pre_up).astype(BF)
            gate += jnp.sum(hidden.astype(F32) * hidden_grad, axis=0, keepdims=True)
            act_gate = (hidden_grad * pre_up * slope).astype(BF)
            act_up = (hidden_grad * active).astype(BF)
            acts_here[expert, 0] = act_gate
            acts_here[expert, 1] = act_up
            acts_here[expert, 2] = hidden
            back += lax.dot_general(act_gate, w_gate, TN_DIMS, preferred_element_type=F32)
            back += lax.dot_general(act_up, w_up, TN_DIMS, preferred_element_type=F32)
        back = back.astype(BF)
        gate_rows = jnp.broadcast_to(gate, (META, NY * half)).astype(BF)
        gate_columns = lax.dot_general(eye(NY * half), gate_rows, NT_DIMS, preferred_element_type=F32)
        for step in range(NY):
            here = slice(expert * half, (expert + 1) * half)
            there = slice(step * half, (step + 1) * half)
            returns[step, here, :features] = back[there]
            returns[step, here, features:] = jnp.where(
                lane == y * 2 + expert, gate_columns[there], 0.0
            ).astype(BF)


def weight_grad_kernel(routes, routes_other, acts, acts_other, out):
    units = acts.shape[2]
    features = routes.shape[2] // 2

    def both(expert, start):
        pieces = [of_expert(r, expert, start, features) for r in (routes, routes_other)]
        return jnp.concatenate(pieces, axis=0)

    for expert in range(2):
        inputs = both(expert, 0)
        cotangents = both(expert, features)
        for which, right, at in (
            (0, inputs, expert * 2 * units),
            (1, inputs, (expert * 2 + 1) * units),
            (2, cotangents, (4 + expert) * units),
        ):
            left = jnp.concatenate([acts[expert, which], acts_other[expert, which]], axis=1)
            out[at : at + units] = jnp.dot(left, right, preferred_element_type=F32).astype(BF)


def combine_kernel(where, placing, metas, returned, *outs):
    lo, core = where[1], where[3]
    features = returned.shape[2] - META
    back = jnp.concatenate([returned[step] for step in range(NY)], axis=0)
    summed = lax.dot_general(placing[...], back, TN_DIMS, preferred_element_type=F32)
    named = metas[:, :8]
    gate = jnp.zeros(named.shape, F32)
    for step in range(NY):
        for j in range(2):
            expert = (step * NLO + lo) * 2 + j
            at = features + step * 2 + j
            gate += jnp.where(named == expert.astype(F32), summed[:, at : at + 1], 0.0)
    tokens = outs[0].shape[0]
    for out, up, other in zip(outs, (3, 2, 1, 0), (2, 1, 0, 3), strict=True):
        a, b = (slice(g * tokens, (g + 1) * tokens) for g in (up, other))
        out[:, :features] = jnp.where(core == 0, summed[a, :features], summed[b, :features]).astype(BF)
        out[:, features:] = jnp.zeros((tokens, META), BF)
        out[:, features : features + 8] = jnp.where(core == 0, gate[a], gate[b]).astype(BF)


def split_core_kernel(where, arrived, below, kept, keep, give):
    tokens, features = arrived.shape[0], arrived.shape[1] - META
    width = features // (NHI * NCORE)
    first = where[3] == 0
    last = jnp.where(first, below[...].astype(F32), kept[...].astype(F32))
    total = arrived[...].astype(F32) + last
    gate = lax.dot_general(total[:, features:].astype(BF), eye(tokens), TN_DIMS, preferred_element_type=F32)
    for hi in range(NHI):
        blocks = []
        for part in (hi * NCORE, hi * NCORE + 1):
            row = jnp.broadcast_to(gate[part : part + 1], (16, tokens))
            blocks.append((total[:, part * width : (part + 1) * width], row))
        (zero, zero_gate), (one, one_gate) = blocks
        for out, swap in ((keep, first), (give, jnp.logical_not(first))):
            out[hi, :tokens] = jnp.where(swap, zero, one).astype(BF)
            out[hi, tokens:] = jnp.zeros((16, width), BF)
            out[hi, tokens:, :tokens] = jnp.where(swap, zero_gate, one_gate).astype(BF)


def finish_kernel(where, weights, pieces, input_grad, gate_grad):
    column = where[2] * NCORE + where[3]
    tokens = input_grad.shape[0]
    total = pieces[0].astype(F32)
    for hi in range(1, NHI):
        total += pieces[hi].astype(F32)
    input_grad[...] = total[:tokens].astype(BF)
    route = lax.broadcasted_iota(jnp.int32, weights.shape, 0)
    under = jnp.sum(jnp.where(route == column, weights[...].astype(F32), 0.0), axis=0, keepdims=True)
    gate_grad[...] = total[tokens : tokens + 1, :tokens] / under


def local(
    hidden_states,
    expert_ids,
    gate_weights,
    completion_lengths,
    output_grad,
    gate_up_proj,
    down_proj,
):
    tokens, width = hidden_states.shape
    parts = NHI * NCORE
    features = width * parts
    units = gate_up_proj.shape[2]
    slots = tokens * expert_ids.shape[1] // (NY * NLO * 2)
    total = NY * 2 * 4 * slots
    share = total // NY
    expert_at, tensor_at = lax.axis_index("expert"), lax.axis_index("tensor")
    where = jnp.stack(
        [
            expert_at // NLO,
            expert_at % NLO,
            tensor_at // NCORE,
            tensor_at % NCORE,
            completion_lengths[0],
        ]
    ).astype(jnp.int32)
    scale = ((tokens * NY * NLO) / completion_lengths.astype(F32)).astype(F32)
    weights_across = gate_weights.T
    meta = jnp.concatenate([expert_ids.T.astype(F32).astype(BF), weights_across], axis=0)
    meta = jnp.pad(meta, ((0, 0), (0, width - tokens)))

    gathered = lax.all_gather(
        jnp.concatenate([hidden_states, output_grad], axis=1), "tensor", axis=0, tiled=True
    )
    gate_up_other, down_other = to_other_core(gate_up_proj), to_other_core(down_proj)
    rows = jnp.concatenate([gathered[:, :width], meta], axis=0)
    grads = gathered[:, width:]

    def onward(block):
        return send(block, lambda core: (0, 1 if core == 0 else -1, 0))

    def onward_last(block):
        return send(block, lambda core: (0, 1, 0) if core == 0 else None)

    row_blocks, grad_blocks = [rows], [grads]
    for _ in range(3):
        row_blocks.append(onward(row_blocks[-1]))
        grad_blocks.append(onward(grad_blocks[-1]))
    row_blocks = row_blocks[1:] + [onward_last(row_blocks[-1])]
    grad_blocks = grad_blocks[1:] + [onward_last(grad_blocks[-1])]
    sends, placing, metas = call(
        select_kernel,
        [
            struct((NY, share, 2 * features)),
            struct((total, 4 * tokens)),
            struct((4 * tokens, 16), F32),
        ],
        where, scale, *row_blocks, rows, *grad_blocks, grads,
        scalars=2, flops=4 * 4 * tokens * total * features,
    )
    routes = swap_y(sends)
    routes_other = to_other_core(routes)
    acts_shape = struct((2, 3, units, total // 2))
    returns, acts, acts_theirs = call(
        expert_kernel,
        [struct((NY, share, features + META)), acts_shape, acts_shape],
        where, routes, gate_up_proj, down_proj, gate_up_other, down_other,
        scalars=1, flops=2 * total * 2 * units * features * 5,
    )
    acts_other = to_other_core(acts_theirs)
    returned = swap_y(returns)
    (weight_parts,) = call(
        weight_grad_kernel,
        [struct((6 * units, features))],
        routes, routes_other, acts, acts_other,
        flops=2 * 2 * total * units * features * 3,
    )
    weight_grads = lax.psum_scatter(weight_parts, "dp", scatter_dimension=1, tiled=True)

    far, next_far, near, last = call(
        combine_kernel,
        [struct((tokens, features + META))] * 4,
        where, placing, metas, returned, scalars=1, flops=2 * 4 * tokens * total * features,
    )

    def two_back(block):
        return send(block, lambda core: (0, -2 if core == 0 else 2, 0))

    def add(one, other):
        return (one.astype(F32) + other.astype(F32)).astype(BF)

    near = add(near, two_back(far))
    last = add(last, two_back(next_far))
    arrived = send(near, lambda core: (0, -2 if core == 0 else 1, 0))
    below = send(last, lambda core: (0, -1, 0) if core == 0 else None)
    keep, give = call(
        split_core_kernel,
        [struct((NHI, tokens + 16, width))] * 2,
        where, arrived, below, last, scalars=1,
    )
    pieces = swap_hi(add(keep, to_other_core(give)))
    input_grad, gate_grad = call(
        finish_kernel,
        [struct((tokens, width)), struct((1, tokens), F32)],
        where, weights_across, pieces, scalars=1,
    )
    part = weight_grads.shape[1]
    gate_up_grad = weight_grads[: 4 * units].reshape(2, 2, units, part)
    down_grad = weight_grads[4 * units :].reshape(2, units, part)
    return (input_grad, gate_grad.reshape(tokens, 1), gate_up_grad, down_grad)


def solution(mesh):
    placed = (
        P(("dp", "expert"), "tensor"),
        P(("dp", "expert"), None),
        P(("dp", "expert"), None),
        P("dp"),
        P(("dp", "expert"), "tensor"),
        P("expert", None, "tensor", None),
        P("expert", "tensor", None),
    )
    return jax.shard_map(
        local,
        mesh=mesh,
        in_specs=placed,
        out_specs=(
            P(("dp", "expert"), "tensor"),
            P(("dp", "expert"), "tensor"),
            P("expert", None, "tensor", "dp"),
            P("expert", "tensor", "dp"),
        ),
        check_vma=False,
    )
```

time: 329 us -> 280 us (0.85)
  the two profiles are of different devices: /device:TPU:4 before, /device:TPU:38 now
where the time goes in v2:
time: 280 us; the launch traced here: 279 us
  blocking collectives  117 us (42%)
  waiting for transfers between devices  55.2 us (20%)
  starting transfers between devices  47.9 us (17%)
  Pallas kernels  28 us (10%)
  between operations  15 us (5%)
  local copies, waits for them, and re-layouts  10.4 us (4%)
  other arithmetic  5.22 us (2%)
    all_gather x1, blocking collectives, local(): lax.all_gather(jnp.concatenate([hidden_states, output_grad], axis=1), 'te...  51.4 us
    all_to_all x1, blocking collectives, swap_hi(): lax.all_to_all(array, 'tensor', split_axis=0, concat_axis=0, tiled=True,...  45.9 us
    ppermute x17, starting transfers between devices, send(): return lax.ppermute(array, PLANE, pairs)  43.5 us
    ppermute x17, waiting for transfers between devices, send(): return lax.ppermute(array, PLANE, pairs)  40.6 us
    pallas_call x6, Pallas kernels, call(): pl.pallas_call(kernel, out_shape=outs, in_specs=[SMEM] * scalars + [VMEM]...  28 us
    all_to_all x1, blocking collectives, swap_y(): lax.all_to_all(array, 'expert', split_axis=0, concat_axis=0, tiled=True,...  19.5 us
    all_to_all x1, waiting for transfers between devices, swap_y(): lax.all_to_all(array, 'expert', split_axis=0, concat_axis=0, tiled=True,...  14.6 us
    unnamed x36, local copies, waits for them, and re-layouts  5.95 us
  transfers between devices with their start and end apart: 19, of which 13 were waited for; matrix products, arithmetic and copies ran while one was open for 1% of the time, Pallas kernels for 6%

profile of v2, /device:TPU:38, one launch (start us, length us, event | category | flops | bytes accessed | tf_op | source)
XLA Modules:
  0.0 278.7 jit_solution(9633949040737647927)
XLA Ops:
  7.2 0.7 fusion.3
  7.9 0.8 pad_maximum_fusion.1
  8.6 51.4 %all_gather.3 = bf16[512,512]{1,0:T(8,128)(2,1)S(1)} all-gather(bf16[64,512]{1,0:T(8,128)(2,1)S(1)} %pad_maximum_fusion.1), channel_id=1, replica_groups=mesh['dp'=4,'expert'=32,'tensor'=8] {'tensor'}, dimensions={0}, use_global_device_ids=true | all-gather | bytes 589824 | tf_op jit(solution)/shard_map/all_gather | solution.py:291
  60.1 0.0 copy-start.6
  60.1 0.7 fusion.2
  60.9 1.9 collective-permute-start
  62.8 2.5 collective-permute-start.4
  65.3 3.9 %collective-permute-done.refs_0_ = bf16[528,256]{1,0:T(8,128)(2,1)S(1)} collective-permute-done((bf16[528,256]{1,0:T(8,128)(2,1)S(1)}, bf16[528,256]{1,0:T(8,128)(2,1)S(1)}, u32[]{:S(2)}, u32[]{:S(2)}) %collective-permute-start) | collective-permute-done | bytes 270368 | tf_op jit(solution)/shard_map/ppermute | solution.py:38
  69.2 1.9 collective-permute-start.1
  71.1 0.9 collective-permute-done.4.refs_5_
  72.0 1.9 collective-permute-start.5
  73.9 4.8 %collective-permute-done.1.refs_1_ = bf16[528,256]{1,0:T(8,128)(2,1)S(1)} collective-permute-done((bf16[528,256]{1,0:T(8,128)(2,1)S(1)}, bf16[528,256]{1,0:T(8,128)(2,1)S(1)}, u32[]{:S(2)}, u32[]{:S(2)}) %collective-permute-start.1) | collective-permute-done | bytes 270368 | tf_op jit(solution)/shard_map/ppermute | solution.py:38
  78.7 1.9 collective-permute-start.2
  80.7 0.9 collective-permute-done.5.refs_6_
  81.6 1.9 collective-permute-start.6
  83.5 4.8 %collective-permute-done.2.refs_2_ = bf16[528,256]{1,0:T(8,128)(2,1)S(1)} collective-permute-done((bf16[528,256]{1,0:T(8,128)(2,1)S(1)}, bf16[528,256]{1,0:T(8,128)(2,1)S(1)}, u32[]{:S(2)}, u32[]{:S(2)}) %collective-permute-start.2) | collective-permute-done | bytes 270368 | tf_op jit(solution)/shard_map/ppermute | solution.py:38
  88.3 1.9 collective-permute-start.3
  90.2 0.9 collective-permute-done.6.refs_7_
  91.1 1.9 collective-permute-start.7
  93.8 0.6 stack.19.where
  94.3 6.3 %collective-permute-done.7.refs_8_ = bf16[512,256]{1,0:T(8,128)(2,1)S(1)} collective-permute-done((bf16[512,256]{1,0:T(8,128)(2,1)S(1)}, bf16[512,256]{1,0:T(8,128)(2,1)S(1)}, u32[]{:S(2)}, u32[]{:S(2)}) %collective-permute-start.7) | collective-permute-done | bytes 262176 | tf_op jit(solution)/shard_map/ppermute | solution.py:38
  100.7 0.0 collective-permute-done.3.refs_3_
  100.7 0.6 copy-done.17
  101.4 0.7 copy-done.13
  102.1 5.0 %shard_map.102 = (bf16[4,64,4096]{2,1,0:T(8,128)(2,1)}, bf16[256,256]{1,0:T(8,128)(2,1)}, f32[256,16]{1,0:T(8,128)}) custom-call(s32[5]{0:T(128)} %stack.19.where, f32[1]{0:T(128)S(6)} %div.24.scale, bf16[528,256]{1,0:T(8,128)(2,1)} %copy-done.10, bf16[528,256]{1,0:T(8,128)(2,1)} %copy-done.11, bf16[528,256]{1,0:T(8,128)(2,1)} %copy-done.12, ...), custom_call_target="tpu_custom_call" | custom-call | flops 536870912 | bytes 4907032 | tf_op jit(solution)/shard_map/pallas_call | solution.py:62
  107.1 4.5 %all-to-all-start = ((bf16[4,64,4096]{2,1,0:T(8,128)(2,1)}), bf16[4,64,4096]{2,1,0:T(8,128)(2,1)S(1)}, u32[]{:S(2)}, u32[]{:S(2)}) async-start(bf16[4,64,4096]{2,1,0:T(8,128)(2,1)} %get-tuple-element.20), calls=%async_computation | async-start | bytes 4194304 | tf_op jit(solution)/shard_map/all_to_all | solution.py:43
  111.6 1.9 collective-permute-start.8
  113.5 14.6 %all-to-all-done.routes = bf16[4,64,4096]{2,1,0:T(8,128)(2,1)S(1)} async-done(((bf16[4,64,4096]{2,1,0:T(8,128)(2,1)}), bf16[4,64,4096]{2,1,0:T(8,128)(2,1)S(1)}, u32[]{:S(2)}, u32[]{:S(2)}) %all-to-all-start) | async-done | bytes 2097184 | tf_op jit(solution)/shard_map/all_to_all | solution.py:43
  128.1 1.9 collective-permute-start.15
  130.0 2.4 collective-permute-start.9
  132.4 4.2 %collective-permute-done.9.down_other = bf16[2,192,2048]{2,1,0:T(8,128)(2,1)S(1)} collective-permute-done((bf16[2,192,2048]{2,1,0:T(8,128)(2,1)}, bf16[2,192,2048]{2,1,0:T(8,128)(2,1)S(1)}, u32[]{:S(2)}, u32[]{:S(2)}) %collective-permute-start.9) | collective-permute-done | bytes 1572896 | tf_op jit(solution)/shard_map/ppermute | solution.py:38
  136.6 0.0 collective-permute-done.8.gate_up_other
  136.6 1.1 copy-done.2
  137.7 10.2 %shard_map.103 = (bf16[4,64,2176]{2,1,0:T(8,128)(2,1)}, bf16[2,3,192,128]{3,2,1,0:T(8,128)(2,1)}, bf16[2,3,192,128]{3,2,1,0:T(8,128)(2,1)}) custom-call(s32[5]{0:T(128)} %stack.19.where, bf16[4,64,4096]{2,1,0:T(8,128)(2,1)} %copy-done, bf16[2,2,192,2048]{3,2,1,0:T(8,128)(2,1)} %gate_up.1, bf16[2,192,2048]{2,1,0:T(8,128)(2,1)} %down.1, ...), custom_call_target="tpu_custom_call" | custom-call | flops 2013265920 | bytes 13238292 | tf_op jit(solution)/shard_map/pallas_call | solution.py:62
  148.0 2.0 collective-permute-start.16
  150.0 1.6 collective-permute-done.16.acts_other
  151.6 0.0 collective-permute-done.15.routes_other
  151.7 0.7 copy-done.7
  152.4 0.8 copy-done.1
  153.1 5.9 %shard_map.107 = bf16[1152,2048]{1,0:T(8,128)(2,1)} custom-call(bf16[4,64,4096]{2,1,0:T(8,128)(2,1)} %copy-done, bf16[4,64,4096]{2,1,0:T(8,128)(2,1)} %copy-done.1, bf16[2,3,192,128]{3,2,1,0:T(8,128)(2,1)} %get-tuple-element.30.acts, bf16[2,3,192,128]{3,2,1,0:T(8,128)(2,1)} %copy-done.7), custom_call_target="tpu_custom_call" | custom-call | flops 1207959552 | bytes 9502720 | tf_op jit(solution)/shard_map/pallas_call | solution.py:62
  159.0 0.0 reduce-scatter.2.cloned.1.call-update
  159.0 1.2 copy-done.3
  160.2 19.5 %all_to_all.15.returned = bf16[4,64,2176]{2,1,0:T(8,128)(2,1)} all-to-all(bf16[4,64,2176]{2,1,0:T(8,128)(2,1)S(1)} %copy-done.3), channel_id=1, replica_groups={{0,64,128,192},{8,72,136,200},{16,80,144,208},{24,88,152,216},{32,96,16..., dimensions={0} | all-to-all | bytes 2228224 | tf_op jit(solution)/shard_map/all_to_all | solution.py:43
  179.8 3.2 %shard_map.104 = (bf16[64,2176]{1,0:T(8,128)(2,1)}, bf16[64,2176]{1,0:T(8,128)(2,1)}, bf16[64,2176]{1,0:T(8,128)(2,1)}, bf16[64,2176]{1,0:T(8,128)(2,1)}) custom-call(s32[5]{0:T(128)} %stack.19.where, bf16[256,256]{1,0:T(8,128)(2,1)} %get-tuple-element.18.placing, f32[256,16]{1,0:T(8,128)} %get-tuple-element.19.metas, bf16[4,64,2176]{2,1,0:T(8,128)(2,1)} %all_to_all.15.returned), custom_call_target="tpu_custom_call" | custom-call | flops 268435456 | bytes 2375700 | tf_op jit(solution)/shard_map/pallas_call | solution.py:62
  182.9 5.6 %collective-permute-start.10 = (bf16[64,2176]{1,0:T(8,128)(2,1)}, bf16[64,2176]{1,0:T(8,128)(2,1)S(1)}, u32[]{:S(2)}, u32[]{:S(2)}) collective-permute-start(bf16[64,2176]{1,0:T(8,128)(2,1)} %get-tuple-element.23), channel_id=1, source_target_pairs={{0,54},{1,17},{8,62},{9,25},{16,0},{17,33},{24,8},{25,41},{32,16},... | collective-permute-start | bytes 835592 | tf_op jit(solution)/shard_map/ppermute | solution.py:38
  188.6 1.9 collective-permute-start.12
  190.5 4.9 %collective-permute-done.10 = bf16[64,2176]{1,0:T(8,128)(2,1)S(1)} collective-permute-done((bf16[64,2176]{1,0:T(8,128)(2,1)}, bf16[64,2176]{1,0:T(8,128)(2,1)S(1)}, u32[]{:S(2)}, u32[]{:S(2)}) %collective-permute-start.10) | collective-permute-done | bytes 278560 | tf_op jit(solution)/shard_map/ppermute | solution.py:38
  195.4 1.0 add_convert_fusion.1
  196.4 5.5 %collective-permute-start.11 = (bf16[64,2176]{1,0:T(8,128)(2,1)S(1)}, bf16[64,2176]{1,0:T(8,128)(2,1)S(1)}, u32[]{:S(2)}, u32[]{:S(2)}) collective-permute-start(bf16[64,2176]{1,0:T(8,128)(2,1)S(1)} %add_convert_fusion.1), channel_id=1, source_target_pairs={{0,54},{1,9},{8,62},{9,17},{16,0},{17,25},{24,8},{25,33},{32,16},{... | collective-permute-start | bytes 835592 | tf_op jit(solution)/shard_map/ppermute | solution.py:38
  201.9 0.0 collective-permute-done.12
  201.9 1.0 add_convert_fusion.kept
  203.0 4.3 %collective-permute-start.13 = (bf16[64,2176]{1,0:T(8,128)(2,1)S(1)}, bf16[64,2176]{1,0:T(8,128)(2,1)S(1)}, u32[]{:S(2)}, u32[]{:S(2)}) collective-permute-start(bf16[64,2176]{1,0:T(8,128)(2,1)S(1)} %add_convert_fusion.kept), channel_id=1, source_target_pairs={{0,62},{8,0},{16,8},{24,16},{32,24},{40,32},{48,40},{56,48},{2,56}... | collective-permute-start | bytes 835592 | tf_op jit(solution)/shard_map/ppermute | solution.py:38
  207.3 0.0 collective-permute-done.11.arrived
  207.3 0.0 copy-start.8
  207.3 5.8 %collective-permute-done.13.below = bf16[64,2176]{1,0:T(8,128)(2,1)S(1)} collective-permute-done((bf16[64,2176]{1,0:T(8,128)(2,1)S(1)}, bf16[64,2176]{1,0:T(8,128)(2,1)S(1)}, u32[]{:S(2)}, u32[]{:S(2)}) %collective-permute-start.13) | collective-permute-done | bytes 278560 | tf_op jit(solution)/shard_map/ppermute | solution.py:38
  213.2 0.7 copy-done.9
  213.9 2.2 shard_map.105
  216.0 1.9 collective-permute-start.14
  218.0 1.6 collective-permute-done.14
  219.5 1.0 add_convert_fusion.2
  220.5 45.9 %all_to_all.16.pieces = bf16[4,80,256]{2,1,0:T(8,128)(2,1)} all-to-all(bf16[4,80,256]{2,1,0:T(8,128)(2,1)S(1)} %add_convert_fusion.2), channel_id=1, replica_groups={{0,2,4,6},{1,3,5,7},{8,10,12,14},{9,11,13,15},{16,18,20,22},{17,19,21,2..., dimensions={0} | all-to-all | bytes 327680 | tf_op jit(solution)/shard_map/all_to_all | solution.py:50
  266.4 1.6 shard_map.106
  268.0 2.1 slice.18
  270.1 1.8 slice.19
  (31 shorter events, 0.1 us)
Async XLA Ops:
  60.1 40.6 %copy-start.6 = (bf16[512,256]{1,0:T(8,128)(2,1)}, bf16[512,256]{1,0:T(8,128)(2,1)S(1)}, u32[]{:S(2)}) copy-start(bf16[512,256]{1,0:T(8,128)(2,1)S(1)} %get-tuple-element.32.refs_9_) | copy-start | bytes 786436
  60.9 39.8 %copy-start.5 = (bf16[528,256]{1,0:T(8,128)(2,1)}, bf16[528,256]{1,0:T(8,128)(2,1)S(1)}, u32[]{:S(2)}) copy-start(bf16[528,256]{1,0:T(8,128)(2,1)S(1)} %pad_maximum_fusion.refs_4_) | copy-start | bytes 811012
  60.9 8.4 %collective-permute-start = (bf16[528,256]{1,0:T(8,128)(2,1)S(1)}, bf16[528,256]{1,0:T(8,128)(2,1)S(1)}, u32[]{:S(2)}, u32[]{:S(2)}) collective-permute-start(bf16[528,256]{1,0:T(8,128)(2,1)S(1)} %pad_maximum_fusion.refs_4_), channel_id=1, source_target_pairs={{0,8},{1,63},{8,16},{9,1},{16,24},{17,9},{24,32},{25,17},{32,40},{... | collective-permute-start | bytes 811016 | tf_op jit(solution)/shard_map/ppermute | solution.py:38
  62.8 9.2 %collective-permute-start.4 = (bf16[512,256]{1,0:T(8,128)(2,1)S(1)}, bf16[512,256]{1,0:T(8,128)(2,1)S(1)}, u32[]{:S(2)}, u32[]{:S(2)}) collective-permute-start(bf16[512,256]{1,0:T(8,128)(2,1)S(1)} %get-tuple-element.32.refs_9_), channel_id=1, source_target_pairs={{0,8},{1,63},{8,16},{9,1},{16,24},{17,9},{24,32},{25,17},{32,40},{... | collective-permute-start | bytes 786440 | tf_op jit(solution)/shard_map/ppermute | solution.py:38
  69.2 31.5 %copy-start.10 = (bf16[528,256]{1,0:T(8,128)(2,1)}, bf16[528,256]{1,0:T(8,128)(2,1)S(1)}, u32[]{:S(2)}) copy-start(bf16[528,256]{1,0:T(8,128)(2,1)S(1)} %collective-permute-done.refs_0_) | copy-start | bytes 811012
  69.2 9.5 %collective-permute-start.1 = (bf16[528,256]{1,0:T(8,128)(2,1)S(1)}, bf16[528,256]{1,0:T(8,128)(2,1)S(1)}, u32[]{:S(2)}, u32[]{:S(2)}) collective-permute-start(bf16[528,256]{1,0:T(8,128)(2,1)S(1)} %collective-permute-done.refs_0_), channel_id=1, source_target_pairs={{0,8},{1,63},{8,16},{9,1},{16,24},{17,9},{24,32},{25,17},{32,40},{... | collective-permute-start | bytes 811016 | tf_op jit(solution)/shard_map/ppermute | solution.py:38
  72.0 28.7 %copy-start.14 = (bf16[512,256]{1,0:T(8,128)(2,1)}, bf16[512,256]{1,0:T(8,128)(2,1)S(1)}, u32[]{:S(2)}) copy-start(bf16[512,256]{1,0:T(8,128)(2,1)S(1)} %collective-permute-done.4.refs_5_) | copy-start | bytes 786436
  72.0 9.5 %collective-permute-start.5 = (bf16[512,256]{1,0:T(8,128)(2,1)S(1)}, bf16[512,256]{1,0:T(8,128)(2,1)S(1)}, u32[]{:S(2)}, u32[]{:S(2)}) collective-permute-start(bf16[512,256]{1,0:T(8,128)(2,1)S(1)} %collective-permute-done.4.refs_5_), channel_id=1, source_target_pairs={{0,8},{1,63},{8,16},{9,1},{16,24},{17,9},{24,32},{25,17},{32,40},{... | collective-permute-start | bytes 786440 | tf_op jit(solution)/shard_map/ppermute | solution.py:38
  78.7 22.0 %copy-start.11 = (bf16[528,256]{1,0:T(8,128)(2,1)}, bf16[528,256]{1,0:T(8,128)(2,1)S(1)}, u32[]{:S(2)}) copy-start(bf16[528,256]{1,0:T(8,128)(2,1)S(1)} %collective-permute-done.1.refs_1_) | copy-start | bytes 811012
  78.7 9.6 %collective-permute-start.2 = (bf16[528,256]{1,0:T(8,128)(2,1)S(1)}, bf16[528,256]{1,0:T(8,128)(2,1)S(1)}, u32[]{:S(2)}, u32[]{:S(2)}) collective-permute-start(bf16[528,256]{1,0:T(8,128)(2,1)S(1)} %collective-permute-done.1.refs_1_), channel_id=1, source_target_pairs={{0,8},{1,63},{8,16},{9,1},{16,24},{17,9},{24,32},{25,17},{32,40},{... | collective-permute-start | bytes 811016 | tf_op jit(solution)/shard_map/ppermute | solution.py:38
  81.6 19.2 %copy-start.15 = (bf16[512,256]{1,0:T(8,128)(2,1)}, bf16[512,256]{1,0:T(8,128)(2,1)S(1)}, u32[]{:S(2)}) copy-start(bf16[512,256]{1,0:T(8,128)(2,1)S(1)} %collective-permute-done.5.refs_6_) | copy-start | bytes 786436
  81.6 9.6 %collective-permute-start.6 = (bf16[512,256]{1,0:T(8,128)(2,1)S(1)}, bf16[512,256]{1,0:T(8,128)(2,1)S(1)}, u32[]{:S(2)}, u32[]{:S(2)}) collective-permute-start(bf16[512,256]{1,0:T(8,128)(2,1)S(1)} %collective-permute-done.5.refs_6_), channel_id=1, source_target_pairs={{0,8},{1,63},{8,16},{9,1},{16,24},{17,9},{24,32},{25,17},{32,40},{... | collective-permute-start | bytes 786440 | tf_op jit(solution)/shard_map/ppermute | solution.py:38
  88.3 12.4 %copy-start.12 = (bf16[528,256]{1,0:T(8,128)(2,1)}, bf16[528,256]{1,0:T(8,128)(2,1)S(1)}, u32[]{:S(2)}) copy-start(bf16[528,256]{1,0:T(8,128)(2,1)S(1)} %collective-permute-done.2.refs_2_) | copy-start | bytes 811012
  88.3 12.4 %collective-permute-start.3 = (bf16[528,256]{1,0:T(8,128)(2,1)S(1)}, bf16[528,256]{1,0:T(8,128)(2,1)S(1)}, u32[]{:S(2)}, u32[]{:S(2)}) collective-permute-start(bf16[528,256]{1,0:T(8,128)(2,1)S(1)} %collective-permute-done.2.refs_2_), channel_id=1, source_target_pairs={{0,8},{8,16},{16,24},{24,32},{32,40},{40,48},{48,56},{56,2},{2,10}... | collective-permute-start | bytes 811016 | tf_op jit(solution)/shard_map/ppermute | solution.py:38
  91.1 9.6 %copy-start.16 = (bf16[512,256]{1,0:T(8,128)(2,1)}, bf16[512,256]{1,0:T(8,128)(2,1)S(1)}, u32[]{:S(2)}) copy-start(bf16[512,256]{1,0:T(8,128)(2,1)S(1)} %collective-permute-done.6.refs_7_) | copy-start | bytes 786436
  91.1 9.6 %collective-permute-start.7 = (bf16[512,256]{1,0:T(8,128)(2,1)S(1)}, bf16[512,256]{1,0:T(8,128)(2,1)S(1)}, u32[]{:S(2)}, u32[]{:S(2)}) collective-permute-start(bf16[512,256]{1,0:T(8,128)(2,1)S(1)} %collective-permute-done.6.refs_7_), channel_id=1, source_target_pairs={{0,8},{8,16},{16,24},{24,32},{32,40},{40,48},{48,56},{56,2},{2,10}... | collective-permute-start | bytes 786440 | tf_op jit(solution)/shard_map/ppermute | solution.py:38
  100.7 0.7 copy-start.17
  101.4 0.7 copy-start.13
  107.1 21.0 %all-to-all-start = ((bf16[4,64,4096]{2,1,0:T(8,128)(2,1)}), bf16[4,64,4096]{2,1,0:T(8,128)(2,1)S(1)}, u32[]{:S(2)}, u32[]{:S(2)}) async-start(bf16[4,64,4096]{2,1,0:T(8,128)(2,1)} %get-tuple-element.20), calls=%async_computation | async-start | bytes 4194304 | tf_op jit(solution)/shard_map/all_to_all | solution.py:43
  111.6 156.4 %reduce-scatter.2.cloned.1.call-start = ((), (), s32[]{:S(2)}) async-start(), calls=%async_computation.4 | async-start | bytes 5898240 | tf_op jit(solution)/shard_map/reduce_scatter | solution.py:337
  111.6 25.0 %collective-permute-start.8 = (bf16[2,2,192,2048]{3,2,1,0:T(8,128)(2,1)}, bf16[2,2,192,2048]{3,2,1,0:T(8,128)(2,1)}, u32[]{:S(2)}, u32[]{:S(2)}) collective-permute-start(bf16[2,2,192,2048]{3,2,1,0:T(8,128)(2,1)} %gate_up.1), channel_id=1, source_target_pairs={{0,1},{1,0},{8,9},{9,8},{16,17},{17,16},{24,25},{25,24},{32,33},{3... | collective-permute-start | bytes 9437192 | tf_op jit(solution)/shard_map/ppermute | solution.py:38
  128.1 8.5 %copy-start = (bf16[4,64,4096]{2,1,0:T(8,128)(2,1)}, bf16[4,64,4096]{2,1,0:T(8,128)(2,1)S(1)}, u32[]{:S(2)}) copy-start(bf16[4,64,4096]{2,1,0:T(8,128)(2,1)S(1)} %all-to-all-done.routes) | copy-start | bytes 6291460
  128.1 23.6 %collective-permute-start.15 = (bf16[4,64,4096]{2,1,0:T(8,128)(2,1)S(1)}, bf16[4,64,4096]{2,1,0:T(8,128)(2,1)S(1)}, u32[]{:S(2)}, u32[]{:S(2)}) collective-permute-start(bf16[4,64,4096]{2,1,0:T(8,128)(2,1)S(1)} %all-to-all-done.routes), channel_id=1, source_target_pairs={{0,1},{1,0},{8,9},{9,8},{16,17},{17,16},{24,25},{25,24},{32,33},{3... | collective-permute-start | bytes 6291464 | tf_op jit(solution)/shard_map/ppermute | solution.py:38
  130.0 6.6 %collective-permute-start.9 = (bf16[2,192,2048]{2,1,0:T(8,128)(2,1)}, bf16[2,192,2048]{2,1,0:T(8,128)(2,1)S(1)}, u32[]{:S(2)}, u32[]{:S(2)}) collective-permute-start(bf16[2,192,2048]{2,1,0:T(8,128)(2,1)} %down.1), channel_id=1, source_target_pairs={{0,1},{1,0},{8,9},{9,8},{16,17},{17,16},{24,25},{25,24},{32,33},{3... | collective-permute-start | bytes 4718600 | tf_op jit(solution)/shard_map/ppermute | solution.py:38
  136.6 1.1 copy-start.2
  148.0 3.7 %collective-permute-start.16 = (bf16[2,3,192,128]{3,2,1,0:T(8,128)(2,1)}, bf16[2,3,192,128]{3,2,1,0:T(8,128)(2,1)S(1)}, u32[]{:S(2)}, u32[]{:S(2)}) collective-permute-start(bf16[2,3,192,128]{3,2,1,0:T(8,128)(2,1)} %get-tuple-element.31), channel_id=1, source_target_pairs={{0,1},{1,0},{8,9},{9,8},{16,17},{17,16},{24,25},{25,24},{32,33},{3... | collective-permute-start | bytes 884744 | tf_op jit(solution)/shard_map/ppermute | solution.py:38
  151.6 0.7 copy-start.7
  151.6 1.5 copy-start.1
  159.0 1.2 copy-start.3
  182.9 12.4 %collective-permute-start.10 = (bf16[64,2176]{1,0:T(8,128)(2,1)}, bf16[64,2176]{1,0:T(8,128)(2,1)S(1)}, u32[]{:S(2)}, u32[]{:S(2)}) collective-permute-start(bf16[64,2176]{1,0:T(8,128)(2,1)} %get-tuple-element.23), channel_id=1, source_target_pairs={{0,54},{1,17},{8,62},{9,25},{16,0},{17,33},{24,8},{25,41},{32,16},... | collective-permute-start | bytes 835592 | tf_op jit(solution)/shard_map/ppermute | solution.py:38
  188.6 13.3 %collective-permute-start.12 = (bf16[64,2176]{1,0:T(8,128)(2,1)}, bf16[64,2176]{1,0:T(8,128)(2,1)S(1)}, u32[]{:S(2)}, u32[]{:S(2)}) collective-permute-start(bf16[64,2176]{1,0:T(8,128)(2,1)} %get-tuple-element.25), channel_id=1, source_target_pairs={{0,54},{1,17},{8,62},{9,25},{16,0},{17,33},{24,8},{25,41},{32,16},... | collective-permute-start | bytes 835592 | tf_op jit(solution)/shard_map/ppermute | solution.py:38
  196.4 10.9 %collective-permute-start.11 = (bf16[64,2176]{1,0:T(8,128)(2,1)S(1)}, bf16[64,2176]{1,0:T(8,128)(2,1)S(1)}, u32[]{:S(2)}, u32[]{:S(2)}) collective-permute-start(bf16[64,2176]{1,0:T(8,128)(2,1)S(1)} %add_convert_fusion.1), channel_id=1, source_target_pairs={{0,54},{1,9},{8,62},{9,17},{16,0},{17,25},{24,8},{25,33},{32,16},{... | collective-permute-start | bytes 835592 | tf_op jit(solution)/shard_map/ppermute | solution.py:38
  203.0 10.2 %copy-start.4 = (bf16[64,2176]{1,0:T(8,128)(2,1)}, bf16[64,2176]{1,0:T(8,128)(2,1)S(1)}, u32[]{:S(2)}) copy-start(bf16[64,2176]{1,0:T(8,128)(2,1)S(1)} %add_convert_fusion.kept) | copy-start | bytes 835588
  203.0 10.2 %collective-permute-start.13 = (bf16[64,2176]{1,0:T(8,128)(2,1)S(1)}, bf16[64,2176]{1,0:T(8,128)(2,1)S(1)}, u32[]{:S(2)}, u32[]{:S(2)}) collective-permute-start(bf16[64,2176]{1,0:T(8,128)(2,1)S(1)} %add_convert_fusion.kept), channel_id=1, source_target_pairs={{0,62},{8,0},{16,8},{24,16},{32,24},{40,32},{48,40},{56,48},{2,56}... | collective-permute-start | bytes 835592 | tf_op jit(solution)/shard_map/ppermute | solution.py:38
  207.3 5.8 %copy-start.8 = (bf16[64,2176]{1,0:T(8,128)(2,1)}, bf16[64,2176]{1,0:T(8,128)(2,1)S(1)}, u32[]{:S(2)}) copy-start(bf16[64,2176]{1,0:T(8,128)(2,1)S(1)} %collective-permute-done.11.arrived) | copy-start | bytes 835588
  213.2 0.7 copy-start.9
  216.0 3.5 %collective-permute-start.14 = (bf16[4,80,256]{2,1,0:T(8,128)(2,1)}, bf16[4,80,256]{2,1,0:T(8,128)(2,1)S(1)}, u32[]{:S(2)}, u32[]{:S(2)}) collective-permute-start(bf16[4,80,256]{2,1,0:T(8,128)(2,1)} %get-tuple-element.27), channel_id=1, source_target_pairs={{0,1},{1,0},{8,9},{9,8},{16,17},{17,16},{24,25},{25,24},{32,33},{3... | collective-permute-start | bytes 491528 | tf_op jit(solution)/shard_map/ppermute | solution.py:38
Sparse Core Ops, SparseCore 0:
  159.1 58.3 reduce-scatter.1

commit v3 on v2

--- a/solution.py
+++ b/solution.py
@@ -59,10 +59,11 @@
 def call(kernel, outs, *args, scalars=0, flops=0):
     moved = sum(a.size * a.dtype.itemsize for a in args)
     moved += sum(o.size * o.dtype.itemsize for o in outs)
+    ins = [SMEM if i < scalars else VMEM for i in range(len(args))]
     return pl.pallas_call(
         kernel,
         out_shape=outs,
-        in_specs=[SMEM] * scalars + [VMEM] * (len(args) - scalars),
+        in_specs=ins,
         out_specs=[VMEM] * len(outs),
         compiler_params=pltpu.CompilerParams(vmem_limit_bytes=LIMIT),
         cost_estimate=pl.CostEstimate(flops=flops, bytes_accessed=moved, transcendentals=0),
@@ -245,7 +246,14 @@
             out[hi, tokens:, :tokens] = jnp.where(swap, zero_gate, one_gate).astype(BF)
 
 
-def finish_kernel(where, weights, pieces, input_grad, gate_grad):
+def finish_kernel(where, weights, pieces, weight_grads, input_grad, gate_grad, gate_up, down):
+    experts, units = down.shape[:2]
+    for expert in range(experts):
+        at = expert * 2 * units
+        gate_up[expert, 0] = weight_grads[at : at + units]
+        gate_up[expert, 1] = weight_grads[at + units : at + 2 * units]
+        at = (experts * 2 + expert) * units
+        down[expert] = weight_grads[at : at + units]
     column = where[2] * NCORE + where[3]
     tokens = input_grad.shape[0]
     total = pieces[0].astype(F32)
@@ -291,7 +299,8 @@
     gathered = lax.all_gather(
         jnp.concatenate([hidden_states, output_grad], axis=1), "tensor", axis=0, tiled=True
     )
-    gate_up_other, down_other = to_other_core(gate_up_proj), to_other_core(down_proj)
+    gathered, gate_up_kept, down_kept = lax.optimization_barrier((gathered, gate_up_proj, down_proj))
+    gate_up_other, down_other = to_other_core(gate_up_kept), to_other_core(down_kept)
     rows = jnp.concatenate([gathered[:, :width], meta], axis=0)
     grads = gathered[:, width:]
 
@@ -307,6 +316,9 @@
         grad_blocks.append(onward(grad_blocks[-1]))
     row_blocks = row_blocks[1:] + [onward_last(row_blocks[-1])]
     grad_blocks = grad_blocks[1:] + [onward_last(grad_blocks[-1])]
+    grad_blocks[0], gate_up_other, down_other = lax.optimization_barrier(
+        (grad_blocks[0], gate_up_other, down_other)
+    )
     sends, placing, metas = call(
         select_kernel,
         [
@@ -318,7 +330,6 @@
         scalars=2, flops=4 * 4 * tokens * total * features,
     )
     routes = swap_y(sends)
-    routes_other = to_other_core(routes)
     acts_shape = struct((2, 3, units, total // 2))
     returns, acts, acts_theirs = call(
         expert_kernel,
@@ -327,6 +338,8 @@
         scalars=1, flops=2 * total * 2 * units * features * 5,
     )
     acts_other = to_other_core(acts_theirs)
+    kept_routes, acts = lax.optimization_barrier((routes, acts))
+    routes_other = to_other_core(kept_routes)
     returned = swap_y(returns)
     (weight_parts,) = call(
         weight_grad_kernel,
@@ -334,13 +347,15 @@
         routes, routes_other, acts, acts_other,
         flops=2 * 2 * total * units * features * 3,
     )
-    weight_grads = lax.psum_scatter(weight_parts, "dp", scatter_dimension=1, tiled=True)
-
+    returned, weight_parts = lax.optimization_barrier((returned, weight_parts))
     far, next_far, near, last = call(
         combine_kernel,
         [struct((tokens, features + META))] * 4,
         where, placing, metas, returned, scalars=1, flops=2 * 4 * tokens * total * features,
     )
+
+    weight_parts, far, next_far = lax.optimization_barrier((weight_parts, far, next_far))
+    weight_grads = lax.psum_scatter(weight_parts, "dp", scatter_dimension=1, tiled=True)
 
     def two_back(block):
         return send(block, lambda core: (0, -2 if core == 0 else 2, 0))
@@ -358,14 +373,18 @@
         where, arrived, below, last, scalars=1,
     )
     pieces = swap_hi(add(keep, to_other_core(give)))
-    input_grad, gate_grad = call(
+    part = weight_grads.shape[1]
+    input_grad, gate_grad, gate_up_grad, down_grad = call(
         finish_kernel,
-        [struct((tokens, width)), struct((1, tokens), F32)],
-        where, weights_across, pieces, scalars=1,
-    )
-    part = weight_grads.shape[1]
-    gate_up_grad = weight_grads[: 4 * units].reshape(2, 2, units, part)
-    down_grad = weight_grads[4 * units :].reshape(2, units, part)
+        [
+            struct((tokens, width)),
+            struct((1, tokens), F32),
+            struct((2, 2, units, part)),
+            struct((2, units, part)),
+        ],
+        where, weights_across, pieces, weight_grads,
+        scalars=1,
+    )
     return (input_grad, gate_grad.reshape(tokens, 1), gate_up_grad, down_grad)
 
 

time: 280 us -> 263 us (0.939)
  waiting for transfers between devices: 55.2 us -> 43.1 us
  local copies, waits for them, and re-layouts: 10.4 us -> 4.78 us
    all_to_all x1, waiting for transfers between devices: 14.6 us -> 6.48 us  [swap_y(): lax.all_to_all(array, 'expert', split_axis=0, concat_axis=0, tiled=True,...]
    ppermute x17, waiting for transfers between devices: 40.6 us -> 36.6 us  [send(): return lax.ppermute(array, PLANE, pairs)]
    slice x2 -> x0, local copies, waits for them, and re-layouts: 3.83 us -> none  [the longest x1 2.06 us: local(): gate_up_grad = weight_grads[:4 * units].reshape(2, 2, units, part)]
  transfers between devices with their start and end apart: 19 -> 19, of which waited for: 13 -> 13; matrix products, arithmetic and copies ran while one was open for 1% -> 1% of each run, Pallas kernels for 6% -> 3%
where the time goes in v3:
time: 263 us; the launch traced here: 262 us
  blocking collectives  119 us (45%)
  starting transfers between devices  48 us (18%)
  waiting for transfers between devices  43.1 us (16%)
  Pallas kernels  29 us (11%)
  between operations  15 us (6%)
  local copies, waits for them, and re-layouts  4.78 us (2%)
  other arithmetic  3.28 us (1%)
    all_gather x1, blocking collectives, local(): lax.all_gather(jnp.concatenate([hidden_states, output_grad], axis=1), 'te...  51.4 us
    all_to_all x1, blocking collectives, swap_hi(): lax.all_to_all(array, 'tensor', split_axis=0, concat_axis=0, tiled=True,...  46.3 us
    ppermute x17, starting transfers between devices, send(): return lax.ppermute(array, PLANE, pairs)  44.4 us
    ppermute x17, waiting for transfers between devices, send(): return lax.ppermute(array, PLANE, pairs)  36.6 us
    pallas_call x6, Pallas kernels, call(): pl.pallas_call(kernel, out_shape=outs, in_specs=ins, out_specs=[VMEM] * l...  29 us
    all_to_all x1, blocking collectives, swap_y(): lax.all_to_all(array, 'expert', split_axis=0, concat_axis=0, tiled=True,...  21.1 us
    all_to_all x1, waiting for transfers between devices, swap_y(): lax.all_to_all(array, 'expert', split_axis=0, concat_axis=0, tiled=True,...  6.48 us
  transfers between devices with their start and end apart: 19, of which 13 were waited for; matrix products, arithmetic and copies ran while one was open for 1% of the time, Pallas kernels for 3%

profile of v3, /device:TPU:38, one launch (start us, length us, event | category | flops | bytes accessed | tf_op | source)
XLA Modules:
  0.0 261.9 jit_solution(12586717136117836655)
XLA Ops:
  7.2 0.8 pad_maximum_fusion.1
  7.9 51.4 %all_gather.3 = bf16[512,512]{1,0:T(8,128)(2,1)S(1)} all-gather(bf16[64,512]{1,0:T(8,128)(2,1)S(1)} %pad_maximum_fusion.1), channel_id=1, replica_groups=mesh['dp'=4,'expert'=32,'tensor'=8] {'tensor'}, dimensions={0}, use_global_device_ids=true | all-gather | bytes 589824 | tf_op jit(solution)/shard_map/all_gather | solution.py:299
  59.4 2.2 collective-permute-start.5
  61.6 2.1 collective-permute-start.6
  63.7 0.7 fusion.3
  64.4 0.7 fusion.2
  65.1 0.0 copy-start.5
  65.2 0.0 copy-start.4
  65.2 1.9 collective-permute-start
  67.1 2.5 collective-permute-start.4
  69.6 3.9 %collective-permute-done.refs_0_ = bf16[528,256]{1,0:T(8,128)(2,1)S(1)} collective-permute-done((bf16[528,256]{1,0:T(8,128)(2,1)S(1)}, bf16[528,256]{1,0:T(8,128)(2,1)S(1)}, u32[]{:S(2)}, u32[]{:S(2)}) %collective-permute-start) | collective-permute-done | bytes 270368 | tf_op jit(solution)/shard_map/ppermute | solution.py:38
  73.5 1.9 collective-permute-start.1
  75.5 0.9 collective-permute-done.4.refs_5_
  76.3 0.0 copy-done.11
  76.4 1.9 collective-permute-start.7
  78.3 4.8 %collective-permute-done.1.refs_1_ = bf16[528,256]{1,0:T(8,128)(2,1)S(1)} collective-permute-done((bf16[528,256]{1,0:T(8,128)(2,1)S(1)}, bf16[528,256]{1,0:T(8,128)(2,1)S(1)}, u32[]{:S(2)}, u32[]{:S(2)}) %collective-permute-start.1) | collective-permute-done | bytes 270368 | tf_op jit(solution)/shard_map/ppermute | solution.py:38
  83.1 0.7 copy-done.12
  83.8 1.9 collective-permute-start.2
  85.7 0.2 collective-permute-done.7.refs_6_
  85.9 1.9 collective-permute-start.8
  87.8 5.6 %collective-permute-done.2.refs_2_ = bf16[528,256]{1,0:T(8,128)(2,1)} collective-permute-done((bf16[528,256]{1,0:T(8,128)(2,1)S(1)}, bf16[528,256]{1,0:T(8,128)(2,1)}, u32[]{:S(2)}, u32[]{:S(2)}) %collective-permute-start.2) | collective-permute-done | bytes 270368 | tf_op jit(solution)/shard_map/ppermute | solution.py:38
  93.4 0.0 copy-done.13
  93.4 1.9 collective-permute-start.3
  95.4 0.9 collective-permute-done.8.refs_7_
  96.2 1.9 collective-permute-start.9
  98.9 0.6 stack.19.where
  99.5 0.0 collective-permute-done.6.down_other
  99.5 0.0 collective-permute-done.5.gate_up_other
  99.5 6.6 %collective-permute-done.9.refs_8_ = bf16[512,256]{1,0:T(8,128)(2,1)} collective-permute-done((bf16[512,256]{1,0:T(8,128)(2,1)}, bf16[512,256]{1,0:T(8,128)(2,1)}, u32[]{:S(2)}, u32[]{:S(2)}) %collective-permute-start.9) | collective-permute-done | bytes 262176 | tf_op jit(solution)/shard_map/ppermute | solution.py:38
  106.1 0.0 collective-permute-done.3.refs_3_
  106.1 5.0 %shard_map.102 = (bf16[4,64,4096]{2,1,0:T(8,128)(2,1)}, bf16[256,256]{1,0:T(8,128)(2,1)}, f32[256,16]{1,0:T(8,128)}) custom-call(s32[5]{0:T(128)} %stack.19.where, f32[1]{0:T(128)S(6)} %div.24.scale, bf16[528,256]{1,0:T(8,128)(2,1)} %copy-done.11, bf16[528,256]{1,0:T(8,128)(2,1)} %copy-done.12, bf16[528,256]{1,0:T(8,128)(2,1)} %collective-permute-done.2.refs_2_, ...), custom_call_target="tpu_custom_call" | custom-call | flops 536870912 | bytes 4907032 | tf_op jit(solution)/shard_map/pallas_call | solution.py:63
  111.1 21.1 %all_to_all.15.routes = bf16[4,64,4096]{2,1,0:T(8,128)(2,1)} all-to-all(bf16[4,64,4096]{2,1,0:T(8,128)(2,1)} %get-tuple-element.39), channel_id=1, replica_groups={{0,64,128,192},{8,72,136,200},{16,80,144,208},{24,88,152,216},{32,96,16..., dimensions={0} | all-to-all | bytes 4194304 | tf_op jit(solution)/shard_map/all_to_all | solution.py:43
  132.2 10.4 %shard_map.103 = (bf16[4,64,2176]{2,1,0:T(8,128)(2,1)}, bf16[2,3,192,128]{3,2,1,0:T(8,128)(2,1)}, bf16[2,3,192,128]{3,2,1,0:T(8,128)(2,1)}) custom-call(s32[5]{0:T(128)} %stack.19.where, bf16[4,64,4096]{2,1,0:T(8,128)(2,1)} %all_to_all.15.routes, bf16[2,2,192,2048]{3,2,1,0:T(8,128)(2,1)} %gate_up.1, bf16[2,192,2048]{2,1,0:T(8,128)(2,1)} %down.1, ...), custom_call_target="tpu_custom_call" | custom-call | flops 2013265920 | bytes 13238292 | tf_op jit(solution)/shard_map/pallas_call | solution.py:63
  142.6 2.1 collective-permute-start.10
  144.7 3.5 %all-to-all-start.1 = ((bf16[4,64,2176]{2,1,0:T(8,128)(2,1)}), bf16[4,64,2176]{2,1,0:T(8,128)(2,1)S(1)}, u32[]{:S(2)}, u32[]{:S(2)}) async-start(bf16[4,64,2176]{2,1,0:T(8,128)(2,1)} %get-tuple-element.42), calls=%async_computation.1 | async-start | bytes 2228224 | tf_op jit(solution)/shard_map/all_to_all | solution.py:43
  148.2 0.0 reduce-scatter.2.cloned.1.call-start
  148.3 2.4 collective-permute-start.11
  150.7 1.2 collective-permute-done.11.acts_other
  151.9 0.0 collective-permute-done.10.routes_other
  151.9 0.7 copy-done.6
  152.6 5.9 %shard_map.104 = bf16[1152,2048]{1,0:T(8,128)(2,1)} custom-call(bf16[4,64,4096]{2,1,0:T(8,128)(2,1)} %all_to_all.15.routes, bf16[4,64,4096]{2,1,0:T(8,128)(2,1)} %collective-permute-done.10.routes_other, bf16[2,3,192,128]{3,2,1,0:T(8,128)(2,1)} %get-tuple-element.45.acts, bf16[2,3,192,128]{3,2,1,0:T(8,128)(2,1)} %copy-done.6), custom_call_target="tpu_custom_call" | custom-call | flops 1207959552 | bytes 9502720 | tf_op jit(solution)/shard_map/pallas_call | solution.py:63
  158.4 6.5 %all-to-all-done.1.returned = bf16[4,64,2176]{2,1,0:T(8,128)(2,1)S(1)} async-done(((bf16[4,64,2176]{2,1,0:T(8,128)(2,1)}), bf16[4,64,2176]{2,1,0:T(8,128)(2,1)S(1)}, u32[]{:S(2)}, u32[]{:S(2)}) %all-to-all-start.1) | async-done | bytes 1114144 | tf_op jit(solution)/shard_map/all_to_all | solution.py:43
  164.9 1.0 copy-done.1
  166.0 3.2 %shard_map.105 = (bf16[64,2176]{1,0:T(8,128)(2,1)}, bf16[64,2176]{1,0:T(8,128)(2,1)}, bf16[64,2176]{1,0:T(8,128)(2,1)}, bf16[64,2176]{1,0:T(8,128)(2,1)}) custom-call(s32[5]{0:T(128)} %stack.19.where, bf16[256,256]{1,0:T(8,128)(2,1)} %get-tuple-element.37.placing, f32[256,16]{1,0:T(8,128)} %get-tuple-element.38.metas, bf16[4,64,2176]{2,1,0:T(8,128)(2,1)} %copy-done.1), custom_call_target="tpu_custom_call" | custom-call | flops 268435456 | bytes 2375700 | tf_op jit(solution)/shard_map/pallas_call | solution.py:63
  169.1 0.0 reduce-scatter.2.cloned.1.call-update
  169.2 0.9 copy-done.17
  170.1 5.9 %collective-permute-start.12 = (bf16[64,2176]{1,0:T(8,128)(2,1)S(1)}, bf16[64,2176]{1,0:T(8,128)(2,1)S(1)}, u32[]{:S(2)}, u32[]{:S(2)}) collective-permute-start(bf16[64,2176]{1,0:T(8,128)(2,1)S(1)} %copy-done.17), channel_id=1, source_target_pairs={{0,54},{1,17},{8,62},{9,25},{16,0},{17,33},{24,8},{25,41},{32,16},... | collective-permute-start | bytes 835592 | tf_op jit(solution)/shard_map/ppermute | solution.py:38
  176.0 1.9 collective-permute-start.14
  177.9 4.6 %collective-permute-done.12 = bf16[64,2176]{1,0:T(8,128)(2,1)S(1)} collective-permute-done((bf16[64,2176]{1,0:T(8,128)(2,1)S(1)}, bf16[64,2176]{1,0:T(8,128)(2,1)S(1)}, u32[]{:S(2)}, u32[]{:S(2)}) %collective-permute-start.12) | collective-permute-done | bytes 278560 | tf_op jit(solution)/shard_map/ppermute | solution.py:38
  182.5 0.1 add_convert_fusion.1
  182.6 6.4 %collective-permute-start.13 = (bf16[64,2176]{1,0:T(8,128)(2,1)S(1)}, bf16[64,2176]{1,0:T(8,128)(2,1)S(1)}, u32[]{:S(2)}, u32[]{:S(2)}) collective-permute-start(bf16[64,2176]{1,0:T(8,128)(2,1)S(1)} %add_convert_fusion.1), channel_id=1, source_target_pairs={{0,54},{1,9},{8,62},{9,17},{16,0},{17,25},{24,8},{25,33},{32,16},{... | collective-permute-start | bytes 835592 | tf_op jit(solution)/shard_map/ppermute | solution.py:38
  189.0 0.0 collective-permute-done.14
  189.0 0.1 add_convert_fusion.kept
  189.1 3.6 %collective-permute-start.15 = (bf16[64,2176]{1,0:T(8,128)(2,1)S(1)}, bf16[64,2176]{1,0:T(8,128)(2,1)S(1)}, u32[]{:S(2)}, u32[]{:S(2)}) collective-permute-start(bf16[64,2176]{1,0:T(8,128)(2,1)S(1)} %add_convert_fusion.kept), channel_id=1, source_target_pairs={{0,62},{8,0},{16,8},{24,16},{32,24},{40,32},{48,40},{56,48},{2,56}... | collective-permute-start | bytes 835592 | tf_op jit(solution)/shard_map/ppermute | solution.py:38
  192.7 3.3 %collective-permute-done.13.arrived = bf16[64,2176]{1,0:T(8,128)(2,1)S(1)} collective-permute-done((bf16[64,2176]{1,0:T(8,128)(2,1)S(1)}, bf16[64,2176]{1,0:T(8,128)(2,1)S(1)}, u32[]{:S(2)}, u32[]{:S(2)}) %collective-permute-start.13) | collective-permute-done | bytes 278560 | tf_op jit(solution)/shard_map/ppermute | solution.py:38
  196.0 3.0 %collective-permute-done.15.below = bf16[64,2176]{1,0:T(8,128)(2,1)S(1)} collective-permute-done((bf16[64,2176]{1,0:T(8,128)(2,1)S(1)}, bf16[64,2176]{1,0:T(8,128)(2,1)S(1)}, u32[]{:S(2)}, u32[]{:S(2)}) %collective-permute-start.15) | collective-permute-done | bytes 278560 | tf_op jit(solution)/shard_map/ppermute | solution.py:38
  199.0 0.0 copy-done.9
  199.0 0.7 copy-done.10
  199.7 2.1 shard_map.106
  201.9 1.9 collective-permute-start.16
  203.8 1.6 collective-permute-done.16
  205.3 1.0 add_convert_fusion.2
  206.3 46.3 %all_to_all.16.pieces = bf16[4,80,256]{2,1,0:T(8,128)(2,1)} all-to-all(bf16[4,80,256]{2,1,0:T(8,128)(2,1)S(1)} %add_convert_fusion.2), channel_id=1, replica_groups={{0,2,4,6},{1,3,5,7},{8,10,12,14},{9,11,13,15},{16,18,20,22},{17,19,21,2..., dimensions={0} | all-to-all | bytes 327680 | tf_op jit(solution)/shard_map/all_to_all | solution.py:50
  252.6 2.5 shard_map.107
  (29 shorter events, 0.1 us)
Async XLA Ops:
  59.4 40.1 %collective-permute-start.5 = (bf16[2,2,192,2048]{3,2,1,0:T(8,128)(2,1)}, bf16[2,2,192,2048]{3,2,1,0:T(8,128)(2,1)S(1)}, u32[]{:S(2)}, u32[]{:S(2)}) collective-permute-start(bf16[2,2,192,2048]{3,2,1,0:T(8,128)(2,1)} %gate_up.1), channel_id=1, source_target_pairs={{0,1},{1,0},{8,9},{9,8},{16,17},{17,16},{24,25},{25,24},{32,33},{3... | collective-permute-start | bytes 9437192 | tf_op jit(solution)/shard_map/ppermute | solution.py:38
  61.6 37.9 %collective-permute-start.6 = (bf16[2,192,2048]{2,1,0:T(8,128)(2,1)}, bf16[2,192,2048]{2,1,0:T(8,128)(2,1)}, u32[]{:S(2)}, u32[]{:S(2)}) collective-permute-start(bf16[2,192,2048]{2,1,0:T(8,128)(2,1)} %down.1), channel_id=1, source_target_pairs={{0,1},{1,0},{8,9},{9,8},{16,17},{17,16},{24,25},{25,24},{32,33},{3... | collective-permute-start | bytes 4718600 | tf_op jit(solution)/shard_map/ppermute | solution.py:38
  65.1 8.4 %copy-start.5 = (bf16[512,256]{1,0:T(8,128)(2,1)}, bf16[512,256]{1,0:T(8,128)(2,1)S(1)}, u32[]{:S(2)}) copy-start(bf16[512,256]{1,0:T(8,128)(2,1)S(1)} %get-tuple-element.62.refs_9_) | copy-start | bytes 786436
  65.2 40.9 %copy-start.4 = (bf16[528,256]{1,0:T(8,128)(2,1)}, bf16[528,256]{1,0:T(8,128)(2,1)S(1)}, u32[]{:S(2)}) copy-start(bf16[528,256]{1,0:T(8,128)(2,1)S(1)} %pad_maximum_fusion.refs_4_) | copy-start | bytes 811012
  65.2 8.4 %collective-permute-start = (bf16[528,256]{1,0:T(8,128)(2,1)S(1)}, bf16[528,256]{1,0:T(8,128)(2,1)S(1)}, u32[]{:S(2)}, u32[]{:S(2)}) collective-permute-start(bf16[528,256]{1,0:T(8,128)(2,1)S(1)} %pad_maximum_fusion.refs_4_), channel_id=1, source_target_pairs={{0,8},{1,63},{8,16},{9,1},{16,24},{17,9},{24,32},{25,17},{32,40},{... | collective-permute-start | bytes 811016 | tf_op jit(solution)/shard_map/ppermute | solution.py:38
  67.1 9.2 %collective-permute-start.4 = (bf16[512,256]{1,0:T(8,128)(2,1)S(1)}, bf16[512,256]{1,0:T(8,128)(2,1)S(1)}, u32[]{:S(2)}, u32[]{:S(2)}) collective-permute-start(bf16[512,256]{1,0:T(8,128)(2,1)S(1)} %get-tuple-element.62.refs_9_), channel_id=1, source_target_pairs={{0,8},{1,63},{8,16},{9,1},{16,24},{17,9},{24,32},{25,17},{32,40},{... | collective-permute-start | bytes 786440 | tf_op jit(solution)/shard_map/ppermute | solution.py:38
  73.5 2.8 %copy-start.11 = (bf16[528,256]{1,0:T(8,128)(2,1)}, bf16[528,256]{1,0:T(8,128)(2,1)S(1)}, u32[]{:S(2)}) copy-start(bf16[528,256]{1,0:T(8,128)(2,1)S(1)} %collective-permute-done.refs_0_) | copy-start | bytes 811012
  73.5 9.5 %collective-permute-start.1 = (bf16[528,256]{1,0:T(8,128)(2,1)S(1)}, bf16[528,256]{1,0:T(8,128)(2,1)S(1)}, u32[]{:S(2)}, u32[]{:S(2)}) collective-permute-start(bf16[528,256]{1,0:T(8,128)(2,1)S(1)} %collective-permute-done.refs_0_), channel_id=1, source_target_pairs={{0,8},{1,63},{8,16},{9,1},{16,24},{17,9},{24,32},{25,17},{32,40},{... | collective-permute-start | bytes 811016 | tf_op jit(solution)/shard_map/ppermute | solution.py:38
  76.3 17.1 %copy-start.13 = (bf16[512,256]{1,0:T(8,128)(2,1)}, bf16[512,256]{1,0:T(8,128)(2,1)S(1)}, u32[]{:S(2)}) copy-start(bf16[512,256]{1,0:T(8,128)(2,1)S(1)} %collective-permute-done.4.refs_5_) | copy-start | bytes 786436
  76.4 9.5 %collective-permute-start.7 = (bf16[512,256]{1,0:T(8,128)(2,1)S(1)}, bf16[512,256]{1,0:T(8,128)(2,1)S(1)}, u32[]{:S(2)}, u32[]{:S(2)}) collective-permute-start(bf16[512,256]{1,0:T(8,128)(2,1)S(1)} %collective-permute-done.4.refs_5_), channel_id=1, source_target_pairs={{0,8},{1,63},{8,16},{9,1},{16,24},{17,9},{24,32},{25,17},{32,40},{... | collective-permute-start | bytes 786440 | tf_op jit(solution)/shard_map/ppermute | solution.py:38
  83.1 0.7 copy-start.12
  83.8 9.7 %collective-permute-start.2 = (bf16[528,256]{1,0:T(8,128)(2,1)S(1)}, bf16[528,256]{1,0:T(8,128)(2,1)}, u32[]{:S(2)}, u32[]{:S(2)}) collective-permute-start(bf16[528,256]{1,0:T(8,128)(2,1)S(1)} %collective-permute-done.1.refs_1_), channel_id=1, source_target_pairs={{0,8},{1,63},{8,16},{9,1},{16,24},{17,9},{24,32},{25,17},{32,40},{... | collective-permute-start | bytes 811016 | tf_op jit(solution)/shard_map/ppermute | solution.py:38
  85.9 9.5 %copy-start.14 = (bf16[512,256]{1,0:T(8,128)(2,1)}, bf16[512,256]{1,0:T(8,128)(2,1)S(1)}, u32[]{:S(2)}) copy-start(bf16[512,256]{1,0:T(8,128)(2,1)S(1)} %collective-permute-done.7.refs_6_) | copy-start | bytes 786436
  85.9 10.4 %collective-permute-start.8 = (bf16[512,256]{1,0:T(8,128)(2,1)S(1)}, bf16[512,256]{1,0:T(8,128)(2,1)}, u32[]{:S(2)}, u32[]{:S(2)}) collective-permute-start(bf16[512,256]{1,0:T(8,128)(2,1)S(1)} %collective-permute-done.7.refs_6_), channel_id=1, source_target_pairs={{0,8},{1,63},{8,16},{9,1},{16,24},{17,9},{24,32},{25,17},{32,40},{... | collective-permute-start | bytes 786440 | tf_op jit(solution)/shard_map/ppermute | solution.py:38
  93.4 12.7 %collective-permute-start.3 = (bf16[528,256]{1,0:T(8,128)(2,1)}, bf16[528,256]{1,0:T(8,128)(2,1)}, u32[]{:S(2)}, u32[]{:S(2)}) collective-permute-start(bf16[528,256]{1,0:T(8,128)(2,1)} %collective-permute-done.2.refs_2_), channel_id=1, source_target_pairs={{0,8},{8,16},{16,24},{24,32},{32,40},{40,48},{48,56},{56,2},{2,10}... | collective-permute-start | bytes 811016 | tf_op jit(solution)/shard_map/ppermute | solution.py:38
  96.2 9.9 %collective-permute-start.9 = (bf16[512,256]{1,0:T(8,128)(2,1)}, bf16[512,256]{1,0:T(8,128)(2,1)}, u32[]{:S(2)}, u32[]{:S(2)}) collective-permute-start(bf16[512,256]{1,0:T(8,128)(2,1)} %collective-permute-done.8.refs_7_), channel_id=1, source_target_pairs={{0,8},{8,16},{16,24},{24,32},{32,40},{40,48},{48,56},{56,2},{2,10}... | collective-permute-start | bytes 786440 | tf_op jit(solution)/shard_map/ppermute | solution.py:38
  99.5 11.6 %copy-start.2 = (bf16[2,2,192,2048]{3,2,1,0:T(8,128)(2,1)}, bf16[2,2,192,2048]{3,2,1,0:T(8,128)(2,1)S(1)}, u32[]{:S(2)}) copy-start(bf16[2,2,192,2048]{3,2,1,0:T(8,128)(2,1)S(1)} %collective-permute-done.5.gate_up_other) | copy-start | bytes 9437188
  132.2 10.4 %copy-start = (bf16[4,64,4096]{2,1,0:T(8,128)(2,1)S(1)}, bf16[4,64,4096]{2,1,0:T(8,128)(2,1)}, u32[]{:S(2)}) copy-start(bf16[4,64,4096]{2,1,0:T(8,128)(2,1)} %all_to_all.15.routes) | copy-start | bytes 6291460
  142.6 5.7 %copy-start.15 = (bf16[2,3,192,128]{3,2,1,0:T(8,128)(2,1)S(1)}, bf16[2,3,192,128]{3,2,1,0:T(8,128)(2,1)}, u32[]{:S(2)}) copy-start(bf16[2,3,192,128]{3,2,1,0:T(8,128)(2,1)} %get-tuple-element.46) | copy-start | bytes 884740
  142.6 9.3 %collective-permute-start.10 = (bf16[4,64,4096]{2,1,0:T(8,128)(2,1)S(1)}, bf16[4,64,4096]{2,1,0:T(8,128)(2,1)}, u32[]{:S(2)}, u32[]{:S(2)}) collective-permute-start(bf16[4,64,4096]{2,1,0:T(8,128)(2,1)S(1)} %copy-done), channel_id=1, source_target_pairs={{0,1},{1,0},{8,9},{9,8},{16,17},{17,16},{24,25},{25,24},{32,33},{3... | collective-permute-start | bytes 6291464 | tf_op jit(solution)/shard_map/ppermute | solution.py:38
  144.7 20.2 %all-to-all-start.1 = ((bf16[4,64,2176]{2,1,0:T(8,128)(2,1)}), bf16[4,64,2176]{2,1,0:T(8,128)(2,1)S(1)}, u32[]{:S(2)}, u32[]{:S(2)}) async-start(bf16[4,64,2176]{2,1,0:T(8,128)(2,1)} %get-tuple-element.42), calls=%async_computation.1 | async-start | bytes 2228224 | tf_op jit(solution)/shard_map/all_to_all | solution.py:43
  148.2 104.4 %reduce-scatter.2.cloned.1.call-start = ((), (), s32[]{:S(2)}) async-start(), calls=%async_computation.4 | async-start | bytes 5898240 | tf_op jit(solution)/shard_map/reduce_scatter | solution.py:358
  148.3 3.6 %collective-permute-start.11 = (bf16[2,3,192,128]{3,2,1,0:T(8,128)(2,1)S(1)}, bf16[2,3,192,128]{3,2,1,0:T(8,128)(2,1)S(1)}, u32[]{:S(2)}, u32[]{:S(2)}) collective-permute-start(bf16[2,3,192,128]{3,2,1,0:T(8,128)(2,1)S(1)} %copy-done.15), channel_id=1, source_target_pairs={{0,1},{1,0},{8,9},{9,8},{16,17},{17,16},{24,25},{25,24},{32,33},{3... | collective-permute-start | bytes 884744 | tf_op jit(solution)/shard_map/ppermute | solution.py:38
  151.9 0.7 copy-start.6
  164.9 1.0 copy-start.1
  169.1 1.0 copy-start.17
  169.1 6.8 %copy-start.16 = (bf16[64,2176]{1,0:T(8,128)(2,1)S(1)}, bf16[64,2176]{1,0:T(8,128)(2,1)}, u32[]{:S(2)}) copy-start(bf16[64,2176]{1,0:T(8,128)(2,1)} %get-tuple-element.54) | copy-start | bytes 835588
  169.1 13.4 %copy-start.8 = (bf16[64,2176]{1,0:T(8,128)(2,1)S(1)}, bf16[64,2176]{1,0:T(8,128)(2,1)}, u32[]{:S(2)}) copy-start(bf16[64,2176]{1,0:T(8,128)(2,1)} %get-tuple-element.48) | copy-start | bytes 835588
  169.1 19.9 %copy-start.7 = (bf16[64,2176]{1,0:T(8,128)(2,1)S(1)}, bf16[64,2176]{1,0:T(8,128)(2,1)}, u32[]{:S(2)}) copy-start(bf16[64,2176]{1,0:T(8,128)(2,1)} %get-tuple-element.53) | copy-start | bytes 835588
  170.1 12.4 %collective-permute-start.12 = (bf16[64,2176]{1,0:T(8,128)(2,1)S(1)}, bf16[64,2176]{1,0:T(8,128)(2,1)S(1)}, u32[]{:S(2)}, u32[]{:S(2)}) collective-permute-start(bf16[64,2176]{1,0:T(8,128)(2,1)S(1)} %copy-done.17), channel_id=1, source_target_pairs={{0,54},{1,17},{8,62},{9,25},{16,0},{17,33},{24,8},{25,41},{32,16},... | collective-permute-start | bytes 835592 | tf_op jit(solution)/shard_map/ppermute | solution.py:38
  176.0 13.0 %collective-permute-start.14 = (bf16[64,2176]{1,0:T(8,128)(2,1)S(1)}, bf16[64,2176]{1,0:T(8,128)(2,1)S(1)}, u32[]{:S(2)}, u32[]{:S(2)}) collective-permute-start(bf16[64,2176]{1,0:T(8,128)(2,1)S(1)} %copy-done.16), channel_id=1, source_target_pairs={{0,54},{1,17},{8,62},{9,25},{16,0},{17,33},{24,8},{25,41},{32,16},... | collective-permute-start | bytes 835592 | tf_op jit(solution)/shard_map/ppermute | solution.py:38
  182.6 13.5 %collective-permute-start.13 = (bf16[64,2176]{1,0:T(8,128)(2,1)S(1)}, bf16[64,2176]{1,0:T(8,128)(2,1)S(1)}, u32[]{:S(2)}, u32[]{:S(2)}) collective-permute-start(bf16[64,2176]{1,0:T(8,128)(2,1)S(1)} %add_convert_fusion.1), channel_id=1, source_target_pairs={{0,54},{1,9},{8,62},{9,17},{16,0},{17,25},{24,8},{25,33},{32,16},{... | collective-permute-start | bytes 835592 | tf_op jit(solution)/shard_map/ppermute | solution.py:38
  189.1 10.0 %copy-start.3 = (bf16[64,2176]{1,0:T(8,128)(2,1)}, bf16[64,2176]{1,0:T(8,128)(2,1)S(1)}, u32[]{:S(2)}) copy-start(bf16[64,2176]{1,0:T(8,128)(2,1)S(1)} %add_convert_fusion.kept) | copy-start | bytes 835588
  189.1 9.9 %collective-permute-start.15 = (bf16[64,2176]{1,0:T(8,128)(2,1)S(1)}, bf16[64,2176]{1,0:T(8,128)(2,1)S(1)}, u32[]{:S(2)}, u32[]{:S(2)}) collective-permute-start(bf16[64,2176]{1,0:T(8,128)(2,1)S(1)} %add_convert_fusion.kept), channel_id=1, source_target_pairs={{0,62},{8,0},{16,8},{24,16},{32,24},{40,32},{48,40},{56,48},{2,56}... | collective-permute-start | bytes 835592 | tf_op jit(solution)/shard_map/ppermute | solution.py:38
  196.0 3.0 %copy-start.9 = (bf16[64,2176]{1,0:T(8,128)(2,1)}, bf16[64,2176]{1,0:T(8,128)(2,1)S(1)}, u32[]{:S(2)}) copy-start(bf16[64,2176]{1,0:T(8,128)(2,1)S(1)} %collective-permute-done.13.arrived) | copy-start | bytes 835588
  199.0 0.7 copy-start.10
  201.9 3.5 %collective-permute-start.16 = (bf16[4,80,256]{2,1,0:T(8,128)(2,1)}, bf16[4,80,256]{2,1,0:T(8,128)(2,1)S(1)}, u32[]{:S(2)}, u32[]{:S(2)}) collective-permute-start(bf16[4,80,256]{2,1,0:T(8,128)(2,1)} %get-tuple-element.56), channel_id=1, source_target_pairs={{0,1},{1,0},{8,9},{9,8},{16,17},{17,16},{24,25},{25,24},{32,33},{3... | collective-permute-start | bytes 491528 | tf_op jit(solution)/shard_map/ppermute | solution.py:38
Sparse Core Ops, SparseCore 0:
  169.3 58.3 reduce-scatter.1

commit v4 on v3

--- a/solution.py
+++ b/solution.py
@@ -17,7 +17,7 @@
 PLANE = ("expert", "tensor")
 VMEM = pl.BlockSpec(memory_space=pltpu.VMEM)
 SMEM = pl.BlockSpec(memory_space=pltpu.SMEM)
-LIMIT = 56 * 1024 * 1024
+LIMIT = 28 * 1024 * 1024
 
 
 def place(y, z, core):
@@ -38,6 +38,11 @@
     return lax.ppermute(array, PLANE, pairs)
 
 
+def both_cores(array):
+    pairs = [[hi * NCORE + core for core in range(NCORE)] for hi in range(NHI)]
+    return lax.all_gather(array, "tensor", axis_index_groups=pairs)
+
+
 def swap_y(array):
     groups = [[y * NLO + lo for y in range(NY)] for lo in range(NLO)]
     return lax.all_to_all(
@@ -80,22 +85,17 @@
     return (row == column).astype(F32).astype(BF)
 
 
-def group_blocks(core, received, fourth, own):
-    last = jnp.where(core == 0, fourth[...].astype(F32), own[...].astype(F32)).astype(BF)
-    return [r[...] for r in received] + [last]
-
-
-def select_kernel(where, scale, *refs):
-    row_refs, grad_refs, (sends, placing, metas) = refs[:5], refs[5:10], refs[10:]
+def placing_kernel(where, scale, first, second, third, fourth, own, placing, back_placing, coefs, metas):
     y, lo, core, length = where[0], where[1], where[3], where[4]
     parts = NHI * NCORE
-    tokens = grad_refs[0].shape[0] // parts
-    width = grad_refs[0].shape[1]
+    width = own.shape[1]
+    tokens = placing.shape[1] // 4
     total = placing.shape[0]
     share = total // NY
     slots = share // 8
-    rows = group_blocks(core, row_refs[:3], row_refs[3], row_refs[4])
-    grads = group_blocks(core, grad_refs[:3], grad_refs[3], grad_refs[4])
+    packed = [r[parts * tokens :, :tokens].astype(F32) for r in (first, second, third)]
+    last = (fourth[parts * tokens :, :tokens].astype(F32), own[parts * tokens :, :tokens].astype(F32))
+    packed.append(jnp.where(core == 0, *last))
     slot = lax.broadcasted_iota(jnp.int32, (tokens, total), 1)
     expert = (((slot // share) * NLO + lo) * 2 + (slot // (4 * slots)) % 2).astype(F32)
     rank_of = (slot % slots).astype(F32)
@@ -105,11 +105,11 @@
         lax.broadcasted_iota(jnp.int32, (tokens, tokens), 0)
         >= lax.broadcasted_iota(jnp.int32, (tokens, tokens), 1)
     ).astype(F32).astype(BF)
-    placed_parts, weighted = [], []
+    named_parts, placed_parts, weighted = [], [], []
     for group in range(4):
-        packed = rows[group][parts * tokens :, :tokens]
-        named = lax.dot_general(eye(tokens), packed, NT_DIMS, preferred_element_type=F32)
-        metas[group * tokens : (group + 1) * tokens] = named
+        named = lax.dot_general(
+            eye(tokens), packed[group].astype(BF), NT_DIMS, preferred_element_type=F32
+        )
         hit = jnp.zeros((tokens, total), F32)
         weight = jnp.zeros((tokens, total), F32)
         for k in range(8):
@@ -122,19 +122,35 @@
         step = group + 1
         offset = jnp.where(core == 0, -step, step if group < 3 else 0)
         position = (y * NLO + (lo + offset + NLO) % NLO) * tokens + token
+        named_parts.append(named)
         placed_parts.append(placed)
         weighted.append(jnp.where(position < length, placed * weight, 0.0))
-    matrix = jnp.concatenate(placed_parts, axis=0).T.astype(BF)
+    placing[...] = jnp.concatenate(placed_parts, axis=0).T.astype(BF)
+    for at, (up, other) in enumerate(zip((3, 2, 1, 0), (2, 1, 0, 3), strict=True)):
+        here = slice(at * tokens, (at + 1) * tokens)
+        back_placing[here] = jnp.where(core == 0, placed_parts[up], placed_parts[other]).astype(BF)
+        metas[here] = jnp.where(core == 0, named_parts[up], named_parts[other])
     weight_matrix = jnp.concatenate(weighted, axis=0).astype(BF)
-    placing[...] = matrix
     ones = jnp.ones((4 * tokens, width), BF)
-    coefs = lax.dot_general(weight_matrix, ones, TN_DIMS, preferred_element_type=F32) * scale[0]
-    for blocks, start in ((rows, 0), (grads, parts * width)):
+    coefs[...] = lax.dot_general(weight_matrix, ones, TN_DIMS, preferred_element_type=F32) * scale[0]
+
+
+def select_kernel(where, placing, coefs, *refs):
+    row_refs, grad_refs, sends = refs[:5], refs[5:10], refs[10]
+    core = where[3]
+    parts = NHI * NCORE
+    tokens = grad_refs[0].shape[0] // parts
+    width = grad_refs[0].shape[1]
+    share = placing.shape[0] // NY
+    matrix = placing[...]
+    for received, start in ((row_refs, 0), (grad_refs, parts * width)):
         for part in range(parts):
-            here = jnp.concatenate([b[part * tokens : (part + 1) * tokens] for b in blocks], axis=0)
-            chosen = jnp.dot(matrix, here, preferred_element_type=F32)
+            piece = slice(part * tokens, (part + 1) * tokens)
+            last = jnp.where(core == 0, received[3][piece].astype(F32), received[4][piece].astype(F32))
+            blocks = [r[piece] for r in received[:3]] + [last.astype(BF)]
+            chosen = jnp.dot(matrix, jnp.concatenate(blocks, axis=0), preferred_element_type=F32)
             if start:
-                chosen = chosen * coefs
+                chosen = chosen * coefs[...]
             chosen = chosen.astype(BF)
             at = start + part * width
             for step in range(NY):
@@ -147,22 +163,23 @@
     return jnp.concatenate([routes[step, here, start : start + size] for step in range(NY)], axis=0)
 
 
-def expert_kernel(where, routes, gate_up, down, gate_up_other, down_other, returns, acts, acts_other):
+def expert_kernel(where, routes, gate_up, down, returns, acts):
     half = routes.shape[1] // 2
     features = routes.shape[2] // 2
-    y = where[0]
-    units = down.shape[1]
+    y, core = where[0], where[3]
+    units = down.shape[2]
     lane = lax.broadcasted_iota(jnp.int32, (half, META), 1)
     for expert in range(2):
         inputs = of_expert(routes, expert, 0, features).T
         cotangents = of_expert(routes, expert, features, features).T
         back = jnp.zeros((NY * half, features), F32)
         gate = jnp.zeros((1, NY * half), F32)
-        for w_in, w_out, acts_here in ((gate_up, down, acts), (gate_up_other, down_other, acts_other)):
-            w_gate, w_up = w_in[expert, 0], w_in[expert, 1]
-            pre_gate = jnp.dot(w_gate, inputs, preferred_element_type=F32)
-            pre_up = jnp.dot(w_up, inputs, preferred_element_type=F32)
-            hidden_grad = jnp.dot(w_out[expert], cotangents, preferred_element_type=F32)
+        for side in range(NCORE):
+            other = (core + side) % NCORE
+            w_both = gate_up[side, expert].reshape(2 * units, features)
+            pre = jnp.dot(w_both, inputs, preferred_element_type=F32)
+            pre_gate, pre_up = pre[:units], pre[units:]
+            hidden_grad = jnp.dot(down[side, expert], cotangents, preferred_element_type=F32)
             sigmoid = jax.nn.sigmoid(pre_gate)
             active = pre_gate * sigmoid
             slope = sigmoid * (1.0 + pre_gate * (1.0 - sigmoid))
@@ -170,11 +187,11 @@
             gate += jnp.sum(hidden.astype(F32) * hidden_grad, axis=0, keepdims=True)
             act_gate = (hidden_grad * pre_up * slope).astype(BF)
             act_up = (hidden_grad * active).astype(BF)
-            acts_here[expert, 0] = act_gate
-            acts_here[expert, 1] = act_up
-            acts_here[expert, 2] = hidden
-            back += lax.dot_general(act_gate, w_gate, TN_DIMS, preferred_element_type=F32)
-            back += lax.dot_general(act_up, w_up, TN_DIMS, preferred_element_type=F32)
+            acts[other, expert, 0] = act_gate
+            acts[other, expert, 1] = act_up
+            acts[other, expert, 2] = hidden
+            act_both = jnp.concatenate([act_gate, act_up], axis=0)
+            back += lax.dot_general(act_both, w_both, TN_DIMS, preferred_element_type=F32)
         back = back.astype(BF)
         gate_rows = jnp.broadcast_to(gate, (META, NY * half)).astype(BF)
         gate_columns = lax.dot_general(eye(NY * half), gate_rows, NT_DIMS, preferred_element_type=F32)
@@ -188,7 +205,7 @@
 
 
 def weight_grad_kernel(routes, routes_other, acts, acts_other, out):
-    units = acts.shape[2]
+    units = acts.shape[3]
     features = routes.shape[2] // 2
 
     def both(expert, start):
@@ -203,28 +220,28 @@
             (1, inputs, (expert * 2 + 1) * units),
             (2, cotangents, (4 + expert) * units),
         ):
-            left = jnp.concatenate([acts[expert, which], acts_other[expert, which]], axis=1)
+            left = jnp.concatenate([acts[0, expert, which], acts_other[expert, which]], axis=1)
             out[at : at + units] = jnp.dot(left, right, preferred_element_type=F32).astype(BF)
 
 
 def combine_kernel(where, placing, metas, returned, *outs):
-    lo, core = where[1], where[3]
+    lo = where[1]
     features = returned.shape[2] - META
     back = jnp.concatenate([returned[step] for step in range(NY)], axis=0)
-    summed = lax.dot_general(placing[...], back, TN_DIMS, preferred_element_type=F32)
-    named = metas[:, :8]
-    gate = jnp.zeros(named.shape, F32)
-    for step in range(NY):
-        for j in range(2):
-            expert = (step * NLO + lo) * 2 + j
-            at = features + step * 2 + j
-            gate += jnp.where(named == expert.astype(F32), summed[:, at : at + 1], 0.0)
     tokens = outs[0].shape[0]
-    for out, up, other in zip(outs, (3, 2, 1, 0), (2, 1, 0, 3), strict=True):
-        a, b = (slice(g * tokens, (g + 1) * tokens) for g in (up, other))
-        out[:, :features] = jnp.where(core == 0, summed[a, :features], summed[b, :features]).astype(BF)
+    for group, out in enumerate(outs):
+        here = slice(group * tokens, (group + 1) * tokens)
+        summed = jnp.dot(placing[here], back, preferred_element_type=F32)
+        named = metas[here, :8]
+        gate = jnp.zeros(named.shape, F32)
+        for step in range(NY):
+            for j in range(2):
+                expert = (step * NLO + lo) * 2 + j
+                at = features + step * 2 + j
+                gate += jnp.where(named == expert.astype(F32), summed[:, at : at + 1], 0.0)
+        out[:, :features] = summed[:, :features].astype(BF)
         out[:, features:] = jnp.zeros((tokens, META), BF)
-        out[:, features : features + 8] = jnp.where(core == 0, gate[a], gate[b]).astype(BF)
+        out[:, features : features + 8] = gate.astype(BF)
 
 
 def split_core_kernel(where, arrived, below, kept, keep, give):
@@ -246,7 +263,7 @@
             out[hi, tokens:, :tokens] = jnp.where(swap, zero_gate, one_gate).astype(BF)
 
 
-def finish_kernel(where, weights, pieces, weight_grads, input_grad, gate_grad, gate_up, down):
+def part_kernel(weight_grads, gate_up, down):
     experts, units = down.shape[:2]
     for expert in range(experts):
         at = expert * 2 * units
@@ -254,6 +271,9 @@
         gate_up[expert, 1] = weight_grads[at + units : at + 2 * units]
         at = (experts * 2 + expert) * units
         down[expert] = weight_grads[at : at + units]
+
+
+def finish_kernel(where, weights, pieces, input_grad, gate_grad):
     column = where[2] * NCORE + where[3]
     tokens = input_grad.shape[0]
     total = pieces[0].astype(F32)
@@ -299,8 +319,6 @@
     gathered = lax.all_gather(
         jnp.concatenate([hidden_states, output_grad], axis=1), "tensor", axis=0, tiled=True
     )
-    gathered, gate_up_kept, down_kept = lax.optimization_barrier((gathered, gate_up_proj, down_proj))
-    gate_up_other, down_other = to_other_core(gate_up_kept), to_other_core(down_kept)
     rows = jnp.concatenate([gathered[:, :width], meta], axis=0)
     grads = gathered[:, width:]
 
@@ -310,34 +328,35 @@
     def onward_last(block):
         return send(block, lambda core: (0, 1, 0) if core == 0 else None)
 
-    row_blocks, grad_blocks = [rows], [grads]
-    for _ in range(3):
-        row_blocks.append(onward(row_blocks[-1]))
-        grad_blocks.append(onward(grad_blocks[-1]))
-    row_blocks = row_blocks[1:] + [onward_last(row_blocks[-1])]
-    grad_blocks = grad_blocks[1:] + [onward_last(grad_blocks[-1])]
-    grad_blocks[0], gate_up_other, down_other = lax.optimization_barrier(
-        (grad_blocks[0], gate_up_other, down_other)
-    )
-    sends, placing, metas = call(
-        select_kernel,
+    row_blocks, grad_blocks = [onward(rows)], [onward(grads)]
+    for move in (onward, onward, onward_last):
+        row_blocks.append(move(row_blocks[-1]))
+        grad_blocks.append(move(grad_blocks[-1]))
+    gate_up_both, down_both = both_cores(gate_up_proj), both_cores(down_proj)
+    placing, back_placing, coefs, metas = call(
+        placing_kernel,
         [
-            struct((NY, share, 2 * features)),
             struct((total, 4 * tokens)),
+            struct((4 * tokens, total)),
+            struct((total, width), F32),
             struct((4 * tokens, 16), F32),
         ],
-        where, scale, *row_blocks, rows, *grad_blocks, grads,
-        scalars=2, flops=4 * 4 * tokens * total * features,
+        where, scale, *row_blocks, rows, scalars=2, flops=2 * 4 * tokens * total * width,
+    )
+    (sends,) = call(
+        select_kernel,
+        [struct((NY, share, 2 * features))],
+        where, placing, coefs, *row_blocks, rows, *grad_blocks, grads,
+        scalars=1, flops=4 * 4 * tokens * total * features,
     )
     routes = swap_y(sends)
-    acts_shape = struct((2, 3, units, total // 2))
-    returns, acts, acts_theirs = call(
+    returns, acts = call(
         expert_kernel,
-        [struct((NY, share, features + META)), acts_shape, acts_shape],
-        where, routes, gate_up_proj, down_proj, gate_up_other, down_other,
+        [struct((NY, share, features + META)), struct((NCORE, 2, 3, units, total // 2))],
+        where, routes, gate_up_both, down_both,
         scalars=1, flops=2 * total * 2 * units * features * 5,
     )
-    acts_other = to_other_core(acts_theirs)
+    acts_other = to_other_core(acts[1])
     kept_routes, acts = lax.optimization_barrier((routes, acts))
     routes_other = to_other_core(kept_routes)
     returned = swap_y(returns)
@@ -351,7 +370,7 @@
     far, next_far, near, last = call(
         combine_kernel,
         [struct((tokens, features + META))] * 4,
-        where, placing, metas, returned, scalars=1, flops=2 * 4 * tokens * total * features,
+        where, back_placing, metas, returned, scalars=1, flops=2 * 4 * tokens * total * features,
     )
 
     weight_parts, far, next_far = lax.optimization_barrier((weight_parts, far, next_far))
@@ -374,16 +393,14 @@
     )
     pieces = swap_hi(add(keep, to_other_core(give)))
     part = weight_grads.shape[1]
-    input_grad, gate_grad, gate_up_grad, down_grad = call(
+    gate_up_grad, down_grad = call(
+        part_kernel, [struct((2, 2, units, part)), struct((2, units, part))], weight_grads
+    )
+    pieces, gate_up_grad, down_grad = lax.optimization_barrier((pieces, gate_up_grad, down_grad))
+    input_grad, gate_grad = call(
         finish_kernel,
-        [
-            struct((tokens, width)),
-            struct((1, tokens), F32),
-            struct((2, 2, units, part)),
-            struct((2, units, part)),
-        ],
-        where, weights_across, pieces, weight_grads,
-        scalars=1,
+        [struct((tokens, width)), struct((1, tokens), F32)],
+        where, weights_across, pieces, scalars=1,
     )
     return (input_grad, gate_grad.reshape(tokens, 1), gate_up_grad, down_grad)
 

time: 263 us -> 247 us (0.939)
  blocking collectives: 119 us -> 72.2 us
  waiting for transfers between devices: 43.1 us -> 72.6 us
  Pallas kernels: 29 us -> 15.4 us
  starting transfers between devices: 48 us -> 58 us
  local copies, waits for them, and re-layouts: 4.78 us -> 12.1 us
    all_to_all x1 -> x0, blocking collectives: 46.3 us -> none  [swap_hi(): lax.all_to_all(array, 'tensor', split_axis=0, concat_axis=0, tiled=True,...]
    all_to_all x0 -> x1, waiting for transfers between devices: none -> 20.4 us  [swap_hi(): lax.all_to_all(array, 'tensor', split_axis=0, concat_axis=0, tiled=True,...]
    pallas_call x6 -> x8, Pallas kernels: 29 us -> 15.4 us  [call(): pl.pallas_call(kernel, out_shape=outs, in_specs=ins, out_specs=[VMEM] * l...]
    all_to_all x0 -> x1, starting transfers between devices: none -> 12.1 us  [swap_hi(): lax.all_to_all(array, 'tensor', split_axis=0, concat_axis=0, tiled=True,...]
    reduce_scatter x1, waiting for transfers between devices: 0.01 us -> 9.85 us  [local(): lax.psum_scatter(weight_parts, 'dp', scatter_dimension=1, tiled=True)]
    unnamed x36 -> x22, local copies, waits for them, and re-layouts: 4.11 us -> 11 us
    ppermute x17 -> x15, starting transfers between devices: 44.4 us -> 42.3 us  [send(): return lax.ppermute(array, PLANE, pairs)]
    ppermute x17 -> x15, waiting for transfers between devices: 36.6 us -> 35.1 us  [send(): return lax.ppermute(array, PLANE, pairs)]
  transfers between devices with their start and end apart: 19 -> 20, of which waited for: 13 -> 15; matrix products, arithmetic and copies ran while one was open for 1% -> 1% of each run, Pallas kernels for 3% -> 3%
where the time goes in v4:
time: 247 us; the launch traced here: 246 us
  waiting for transfers between devices  72.6 us (29%)
  blocking collectives  72.2 us (29%)
  starting transfers between devices  58 us (23%)
  Pallas kernels  15.4 us (6%)
  between operations  14.8 us (6%)
  local copies, waits for them, and re-layouts  12.1 us (5%)
    all_gather x1, blocking collectives, local(): lax.all_gather(jnp.concatenate([hidden_states, output_grad], axis=1), 'te...  51.5 us
    ppermute x15, starting transfers between devices, send(): return lax.ppermute(array, PLANE, pairs)  42.3 us
    ppermute x15, waiting for transfers between devices, send(): return lax.ppermute(array, PLANE, pairs)  35.1 us
    all_to_all x1, blocking collectives, swap_y(): lax.all_to_all(array, 'expert', split_axis=0, concat_axis=0, tiled=True,...  20.8 us
    all_to_all x1, waiting for transfers between devices, swap_hi(): lax.all_to_all(array, 'tensor', split_axis=0, concat_axis=0, tiled=True,...  20.4 us
    pallas_call x8, Pallas kernels, call(): pl.pallas_call(kernel, out_shape=outs, in_specs=ins, out_specs=[VMEM] * l...  15.4 us
    all_to_all x1, starting transfers between devices, swap_hi(): lax.all_to_all(array, 'tensor', split_axis=0, concat_axis=0, tiled=True,...  12.1 us
    unnamed x22, local copies, waits for them, and re-layouts  11 us
  transfers between devices with their start and end apart: 20, of which 15 were waited for; matrix products, arithmetic and copies ran while one was open for 1% of the time, Pallas kernels for 3%

profile of v4, /device:TPU:38, one launch (start us, length us, event | category | flops | bytes accessed | tf_op | source)
XLA Modules:
  0.0 246.0 jit_solution(13023629468253835420)
XLA Ops:
  7.2 0.0 all-gather.7.cloned.1.call-start
  7.3 0.7 all-gather.7.cloned.1.call-update
  7.9 0.0 all-gather.5.cloned.1.call-start
  8.0 0.7 all-gather.5.cloned.1.call-update
  8.8 51.5 %all_gather.15 = bf16[512,512]{1,0:T(8,128)(2,1)S(1)} all-gather(bf16[64,512]{1,0:T(8,128)(2,1)S(1)} %pad_maximum_fusion.1), channel_id=1, replica_groups=mesh['dp'=4,'expert'=32,'tensor'=8] {'tensor'}, dimensions={0}, use_global_device_ids=true | all-gather | bytes 589824 | tf_op jit(solution)/shard_map/all_gather | solution.py:319
  60.3 1.9 collective-permute-start
  62.2 2.5 %collective-permute-start.4 = (bf16[512,256]{1,0:T(8,128)(2,1)S(1)}, bf16[512,256]{1,0:T(8,128)(2,1)S(1)}, u32[]{:S(2)}, u32[]{:S(2)}) collective-permute-start(bf16[512,256]{1,0:T(8,128)(2,1)S(1)} %get-tuple-element.56.refs_9_), channel_id=1, source_target_pairs={{0,8},{1,63},{8,16},{9,1},{16,24},{17,9},{24,32},{25,17},{32,40},{... | collective-permute-start | bytes 786440 | tf_op jit(solution)/shard_map/ppermute | solution.py:38
  64.7 3.9 %collective-permute-done.first.refs_0_ = bf16[528,256]{1,0:T(8,128)(2,1)S(1)} collective-permute-done((bf16[528,256]{1,0:T(8,128)(2,1)S(1)}, bf16[528,256]{1,0:T(8,128)(2,1)S(1)}, u32[]{:S(2)}, u32[]{:S(2)}) %collective-permute-start) | collective-permute-done | bytes 270368 | tf_op jit(solution)/shard_map/ppermute | solution.py:38
  68.6 1.9 collective-permute-start.1
  70.6 0.9 collective-permute-done.4.refs_5_
  71.5 1.9 collective-permute-start.5
  73.4 4.8 %collective-permute-done.1.second.refs_1_ = bf16[528,256]{1,0:T(8,128)(2,1)S(1)} collective-permute-done((bf16[528,256]{1,0:T(8,128)(2,1)S(1)}, bf16[528,256]{1,0:T(8,128)(2,1)S(1)}, u32[]{:S(2)}, u32[]{:S(2)}) %collective-permute-start.1) | collective-permute-done | bytes 270368 | tf_op jit(solution)/shard_map/ppermute | solution.py:38
  78.2 1.9 collective-permute-start.2
  80.1 0.9 collective-permute-done.5.refs_6_
  81.0 1.9 collective-permute-start.6
  82.9 4.8 %collective-permute-done.2.third.refs_2_ = bf16[528,256]{1,0:T(8,128)(2,1)S(1)} collective-permute-done((bf16[528,256]{1,0:T(8,128)(2,1)S(1)}, bf16[528,256]{1,0:T(8,128)(2,1)S(1)}, u32[]{:S(2)}, u32[]{:S(2)}) %collective-permute-start.2) | collective-permute-done | bytes 270368 | tf_op jit(solution)/shard_map/ppermute | solution.py:38
  87.7 1.9 collective-permute-start.3
  89.6 0.9 collective-permute-done.6.refs_7_
  90.5 1.9 collective-permute-start.7
  93.2 0.1 stack.19.where
  93.3 4.0 %collective-permute-done.3.fourth.refs_3_ = bf16[528,256]{1,0:T(8,128)(2,1)S(1)} collective-permute-done((bf16[528,256]{1,0:T(8,128)(2,1)S(1)}, bf16[528,256]{1,0:T(8,128)(2,1)S(1)}, u32[]{:S(2)}, u32[]{:S(2)}) %collective-permute-start.3) | collective-permute-done | bytes 270368 | tf_op jit(solution)/shard_map/ppermute | solution.py:38
  97.3 1.9 shard_map.102
  99.1 0.9 collective-permute-done.7.refs_8_
  100.1 1.3 shard_map.103
  101.4 20.8 %all_to_all.15.routes = bf16[4,64,4096]{2,1,0:T(8,128)(2,1)S(1)} all-to-all(bf16[4,64,4096]{2,1,0:T(8,128)(2,1)S(1)} %shard_map.103), channel_id=1, replica_groups={{0,64,128,192},{8,72,136,200},{16,80,144,208},{24,88,152,216},{32,96,16..., dimensions={0} | all-to-all | bytes 4194304 | tf_op jit(solution)/shard_map/all_to_all | solution.py:48
  122.2 2.8 %copy-done.1 = bf16[4,2,192,2048]{3,2,1,0:T(8,128)(2,1)S(1)} copy-done((bf16[4,2,192,2048]{3,2,1,0:T(8,128)(2,1)S(1)}, bf16[4,2,192,2048]{3,2,1,0:T(8,128)(2,1)}, u32[]{:S(2)}) %copy-start.1) | copy-done | bytes 6291480
  124.9 1.9 copy-done.2
  126.8 4.6 %shard_map.104 = (bf16[4,64,2176]{2,1,0:T(8,128)(2,1)S(1)}, bf16[2,2,3,192,128]{4,3,2,1,0:T(8,128)(2,1)S(1)}) custom-call(s32[5]{0:T(128)S(1)} %stack.19.where, bf16[4,64,4096]{2,1,0:T(8,128)(2,1)S(1)} %all_to_all.15.routes, bf16[2,2,2,192,2048]{4,3,2,1,0:T(8,128)(2,1)S(1)} %bitcast.12, bf16[2,2,192,2048]{3,2,1,0:T(8,128)(2,1)S(1)} %bitcast.13), custom_call_target="tpu_custom_call" | custom-call | flops 2013265920 | bytes 13238292 | tf_op jit(solution)/shard_map/pallas_call | solution.py:68
  131.5 0.0 copy-start.3
  131.5 0.8 copy-done.3
  132.3 1.0 copy-done.6
  133.3 1.9 collective-permute-start.8
  135.2 3.5 %all-to-all-start.1 = ((bf16[4,64,2176]{2,1,0:T(8,128)(2,1)}), bf16[4,64,2176]{2,1,0:T(8,128)(2,1)S(1)}, u32[]{:S(2)}, u32[]{:S(2)}) async-start(bf16[4,64,2176]{2,1,0:T(8,128)(2,1)} %copy-done.6), calls=%async_computation.1 | async-start | bytes 2228224 | tf_op jit(solution)/shard_map/all_to_all | solution.py:48
  138.8 0.0 reduce-scatter.2.cloned.1.call-start
  138.8 1.0 slice_bitcast_fusion
  139.8 2.4 collective-permute-start.9
  142.2 1.2 collective-permute-done.9.acts_other
  143.4 0.0 collective-permute-done.8.routes_other
  143.4 1.1 copy-done.4
  144.5 3.0 %shard_map.105 = bf16[1152,2048]{1,0:T(8,128)(2,1)S(1)} custom-call(bf16[4,64,4096]{2,1,0:T(8,128)(2,1)S(1)} %all_to_all.15.routes, bf16[4,64,4096]{2,1,0:T(8,128)(2,1)} %collective-permute-done.8.routes_other, bf16[2,2,3,192,128]{4,3,2,1,0:T(8,128)(2,1)S(1)} %copy-done.4, bf16[2,3,192,128]{3,2,1,0:T(8,128)(2,1)S(1)} %collective-permute-done.9.acts_other), custom_call_target="tpu_custom_call" | custom-call | flops 1207959552 | bytes 9797632 | tf_op jit(solution)/shard_map/pallas_call | solution.py:68
  147.5 2.1 copy-done
  149.6 5.9 %all-to-all-done.1.returned = bf16[4,64,2176]{2,1,0:T(8,128)(2,1)S(1)} async-done(((bf16[4,64,2176]{2,1,0:T(8,128)(2,1)}), bf16[4,64,2176]{2,1,0:T(8,128)(2,1)S(1)}, u32[]{:S(2)}, u32[]{:S(2)}) %all-to-all-start.1) | async-done | bytes 1114144 | tf_op jit(solution)/shard_map/all_to_all | solution.py:48
  155.5 1.5 shard_map.106
  157.0 0.0 reduce-scatter.2.cloned.1.call-update
  157.0 5.6 %collective-permute-start.12 = (bf16[64,2176]{1,0:T(8,128)(2,1)S(1)}, bf16[64,2176]{1,0:T(8,128)(2,1)S(1)}, u32[]{:S(2)}, u32[]{:S(2)}) collective-permute-start(bf16[64,2176]{1,0:T(8,128)(2,1)S(1)} %get-tuple-element.45), channel_id=1, source_target_pairs={{0,54},{1,17},{8,62},{9,25},{16,0},{17,33},{24,8},{25,41},{32,16},... | collective-permute-start | bytes 835592 | tf_op jit(solution)/shard_map/ppermute | solution.py:38
  162.6 1.9 collective-permute-start.10
  164.6 4.9 %collective-permute-done.12 = bf16[64,2176]{1,0:T(8,128)(2,1)S(1)} collective-permute-done((bf16[64,2176]{1,0:T(8,128)(2,1)S(1)}, bf16[64,2176]{1,0:T(8,128)(2,1)S(1)}, u32[]{:S(2)}, u32[]{:S(2)}) %collective-permute-start.12) | collective-permute-done | bytes 278560 | tf_op jit(solution)/shard_map/ppermute | solution.py:38
  169.4 0.1 add_convert_fusion.kept
  169.5 7.4 %collective-permute-start.13 = (bf16[64,2176]{1,0:T(8,128)(2,1)S(1)}, bf16[64,2176]{1,0:T(8,128)(2,1)S(1)}, u32[]{:S(2)}, u32[]{:S(2)}) collective-permute-start(bf16[64,2176]{1,0:T(8,128)(2,1)S(1)} %add_convert_fusion.kept), channel_id=1, source_target_pairs={{0,62},{8,0},{16,8},{24,16},{32,24},{40,32},{48,40},{56,48},{2,56}... | collective-permute-start | bytes 835592 | tf_op jit(solution)/shard_map/ppermute | solution.py:38
  176.9 0.0 collective-permute-done.10
  177.0 0.1 add_convert_fusion.1
  177.0 5.2 %collective-permute-start.11 = (bf16[64,2176]{1,0:T(8,128)(2,1)S(1)}, bf16[64,2176]{1,0:T(8,128)(2,1)S(1)}, u32[]{:S(2)}, u32[]{:S(2)}) collective-permute-start(bf16[64,2176]{1,0:T(8,128)(2,1)S(1)} %add_convert_fusion.1), channel_id=1, source_target_pairs={{0,54},{1,9},{8,62},{9,17},{16,0},{17,25},{24,8},{25,33},{32,16},{... | collective-permute-start | bytes 835592 | tf_op jit(solution)/shard_map/ppermute | solution.py:38
  182.3 0.0 collective-permute-done.13.below
  182.3 6.5 %collective-permute-done.11.arrived = bf16[64,2176]{1,0:T(8,128)(2,1)S(1)} collective-permute-done((bf16[64,2176]{1,0:T(8,128)(2,1)S(1)}, bf16[64,2176]{1,0:T(8,128)(2,1)S(1)}, u32[]{:S(2)}, u32[]{:S(2)}) %collective-permute-start.11) | collective-permute-done | bytes 278560 | tf_op jit(solution)/shard_map/ppermute | solution.py:38
  188.7 0.9 shard_map.107
  189.6 1.9 collective-permute-start.14
  191.6 1.4 collective-permute-done.14
  192.9 0.7 add_convert_fusion.2
  193.6 12.1 %all-to-all-start.2 = ((bf16[4,80,256]{2,1,0:T(8,128)(2,1)}), bf16[4,80,256]{2,1,0:T(8,128)(2,1)S(1)}, u32[]{:S(2)}, u32[]{:S(2)}) async-start(bf16[4,80,256]{2,1,0:T(8,128)(2,1)} %add_convert_fusion.2), calls=%async_computation.2 | async-start | bytes 327680 | tf_op jit(solution)/shard_map/all_to_all | solution.py:55
  205.7 9.9 %reduce-scatter.2.cloned.1.call-done.weight_grads = bf16[1152,512]{1,0:T(8,128)(2,1)} async-done(((bf16[1152,2048]{1,0:T(8,128)(2,1)}), bf16[1152,512]{1,0:T(8,128)(2,1)}) %reduce-scatter.2.cloned.1.call-update) | async-done | bytes 1179664 | tf_op jit(solution)/shard_map/reduce_scatter | solution.py:377
  215.5 1.3 copy-done.5
  216.8 1.1 shard_map.108
  217.9 20.4 %all-to-all-done.2.pieces = bf16[4,80,256]{2,1,0:T(8,128)(2,1)S(1)} async-done(((bf16[4,80,256]{2,1,0:T(8,128)(2,1)}), bf16[4,80,256]{2,1,0:T(8,128)(2,1)S(1)}, u32[]{:S(2)}, u32[]{:S(2)}) %all-to-all-start.2) | async-done | bytes 163872 | tf_op jit(solution)/shard_map/all_to_all | solution.py:55
  238.3 1.2 shard_map.109
  (21 shorter events, 0.1 us)
Async XLA Ops:
  7.2 1.5 copy-start.10
  7.2 1.5 copy-start.7
  7.2 1.6 copy-start.8
  7.2 1.6 copy-start.9
  7.2 114.9 %all-gather.7.cloned.1.call-start = ((), (), s32[]{:S(2)}) async-start(), calls=%async_computation.6 | async-start | bytes 4718592 | tf_op jit(solution)/shard_map/all_gather | solution.py:43
  7.9 114.2 %all-gather.5.cloned.1.call-start = ((), (), s32[]{:S(2)}) async-start(), calls=%async_computation.5 | async-start | bytes 9437184 | tf_op jit(solution)/shard_map/all_gather | solution.py:43
  60.3 8.4 %collective-permute-start = (bf16[528,256]{1,0:T(8,128)(2,1)S(1)}, bf16[528,256]{1,0:T(8,128)(2,1)S(1)}, u32[]{:S(2)}, u32[]{:S(2)}) collective-permute-start(bf16[528,256]{1,0:T(8,128)(2,1)S(1)} %pad_maximum_fusion.own.refs_4_), channel_id=1, source_target_pairs={{0,8},{1,63},{8,16},{9,1},{16,24},{17,9},{24,32},{25,17},{32,40},{... | collective-permute-start | bytes 811016 | tf_op jit(solution)/shard_map/ppermute | solution.py:38
  62.2 9.2 %collective-permute-start.4 = (bf16[512,256]{1,0:T(8,128)(2,1)S(1)}, bf16[512,256]{1,0:T(8,128)(2,1)S(1)}, u32[]{:S(2)}, u32[]{:S(2)}) collective-permute-start(bf16[512,256]{1,0:T(8,128)(2,1)S(1)} %get-tuple-element.56.refs_9_), channel_id=1, source_target_pairs={{0,8},{1,63},{8,16},{9,1},{16,24},{17,9},{24,32},{25,17},{32,40},{... | collective-permute-start | bytes 786440 | tf_op jit(solution)/shard_map/ppermute | solution.py:38
  68.6 9.5 %collective-permute-start.1 = (bf16[528,256]{1,0:T(8,128)(2,1)S(1)}, bf16[528,256]{1,0:T(8,128)(2,1)S(1)}, u32[]{:S(2)}, u32[]{:S(2)}) collective-permute-start(bf16[528,256]{1,0:T(8,128)(2,1)S(1)} %collective-permute-done.first.refs_0_), channel_id=1, source_target_pairs={{0,8},{1,63},{8,16},{9,1},{16,24},{17,9},{24,32},{25,17},{32,40},{... | collective-permute-start | bytes 811016 | tf_op jit(solution)/shard_map/ppermute | solution.py:38
  71.5 9.5 %collective-permute-start.5 = (bf16[512,256]{1,0:T(8,128)(2,1)S(1)}, bf16[512,256]{1,0:T(8,128)(2,1)S(1)}, u32[]{:S(2)}, u32[]{:S(2)}) collective-permute-start(bf16[512,256]{1,0:T(8,128)(2,1)S(1)} %collective-permute-done.4.refs_5_), channel_id=1, source_target_pairs={{0,8},{1,63},{8,16},{9,1},{16,24},{17,9},{24,32},{25,17},{32,40},{... | collective-permute-start | bytes 786440 | tf_op jit(solution)/shard_map/ppermute | solution.py:38
  78.2 9.6 %collective-permute-start.2 = (bf16[528,256]{1,0:T(8,128)(2,1)S(1)}, bf16[528,256]{1,0:T(8,128)(2,1)S(1)}, u32[]{:S(2)}, u32[]{:S(2)}) collective-permute-start(bf16[528,256]{1,0:T(8,128)(2,1)S(1)} %collective-permute-done.1.second.refs_1_), channel_id=1, source_target_pairs={{0,8},{1,63},{8,16},{9,1},{16,24},{17,9},{24,32},{25,17},{32,40},{... | collective-permute-start | bytes 811016 | tf_op jit(solution)/shard_map/ppermute | solution.py:38
  81.0 9.6 %collective-permute-start.6 = (bf16[512,256]{1,0:T(8,128)(2,1)S(1)}, bf16[512,256]{1,0:T(8,128)(2,1)S(1)}, u32[]{:S(2)}, u32[]{:S(2)}) collective-permute-start(bf16[512,256]{1,0:T(8,128)(2,1)S(1)} %collective-permute-done.5.refs_6_), channel_id=1, source_target_pairs={{0,8},{1,63},{8,16},{9,1},{16,24},{17,9},{24,32},{25,17},{32,40},{... | collective-permute-start | bytes 786440 | tf_op jit(solution)/shard_map/ppermute | solution.py:38
  87.7 9.6 %collective-permute-start.3 = (bf16[528,256]{1,0:T(8,128)(2,1)S(1)}, bf16[528,256]{1,0:T(8,128)(2,1)S(1)}, u32[]{:S(2)}, u32[]{:S(2)}) collective-permute-start(bf16[528,256]{1,0:T(8,128)(2,1)S(1)} %collective-permute-done.2.third.refs_2_), channel_id=1, source_target_pairs={{0,8},{8,16},{16,24},{24,32},{32,40},{40,48},{48,56},{56,2},{2,10}... | collective-permute-start | bytes 811016 | tf_op jit(solution)/shard_map/ppermute | solution.py:38
  90.5 9.6 %collective-permute-start.7 = (bf16[512,256]{1,0:T(8,128)(2,1)S(1)}, bf16[512,256]{1,0:T(8,128)(2,1)S(1)}, u32[]{:S(2)}, u32[]{:S(2)}) collective-permute-start(bf16[512,256]{1,0:T(8,128)(2,1)S(1)} %collective-permute-done.6.refs_7_), channel_id=1, source_target_pairs={{0,8},{8,16},{16,24},{24,32},{32,40},{40,48},{48,56},{56,2},{2,10}... | collective-permute-start | bytes 786440 | tf_op jit(solution)/shard_map/ppermute | solution.py:38
  122.2 2.8 %copy-start.1 = (bf16[4,2,192,2048]{3,2,1,0:T(8,128)(2,1)S(1)}, bf16[4,2,192,2048]{3,2,1,0:T(8,128)(2,1)}, u32[]{:S(2)}) copy-start(bf16[4,2,192,2048]{3,2,1,0:T(8,128)(2,1)} %all-gather.5.cloned.1.call-done) | copy-start | bytes 18874372
  124.9 1.9 copy-start.2
  131.5 0.8 copy-start.3
  132.3 1.0 copy-start.6
  133.3 10.1 %collective-permute-start.8 = (bf16[4,64,4096]{2,1,0:T(8,128)(2,1)S(1)}, bf16[4,64,4096]{2,1,0:T(8,128)(2,1)}, u32[]{:S(2)}, u32[]{:S(2)}) collective-permute-start(bf16[4,64,4096]{2,1,0:T(8,128)(2,1)S(1)} %all_to_all.15.routes), channel_id=1, source_target_pairs={{0,1},{1,0},{8,9},{9,8},{16,17},{17,16},{24,25},{25,24},{32,33},{3... | collective-permute-start | bytes 6291464 | tf_op jit(solution)/shard_map/ppermute | solution.py:38
  135.2 20.2 %all-to-all-start.1 = ((bf16[4,64,2176]{2,1,0:T(8,128)(2,1)}), bf16[4,64,2176]{2,1,0:T(8,128)(2,1)S(1)}, u32[]{:S(2)}, u32[]{:S(2)}) async-start(bf16[4,64,2176]{2,1,0:T(8,128)(2,1)} %copy-done.6), calls=%async_computation.1 | async-start | bytes 2228224 | tf_op jit(solution)/shard_map/all_to_all | solution.py:48
  138.8 76.8 %reduce-scatter.2.cloned.1.call-start = ((), (), s32[]{:S(2)}) async-start(), calls=%async_computation.4 | async-start | bytes 5898240 | tf_op jit(solution)/shard_map/reduce_scatter | solution.py:377
  139.8 3.6 %collective-permute-start.9 = (bf16[2,3,192,128]{3,2,1,0:T(8,128)(2,1)S(1)}, bf16[2,3,192,128]{3,2,1,0:T(8,128)(2,1)S(1)}, u32[]{:S(2)}, u32[]{:S(2)}) collective-permute-start(bf16[2,3,192,128]{3,2,1,0:T(8,128)(2,1)S(1)} %slice_bitcast_fusion), channel_id=1, source_target_pairs={{0,1},{1,0},{8,9},{9,8},{16,17},{17,16},{24,25},{25,24},{32,33},{3... | collective-permute-start | bytes 884744 | tf_op jit(solution)/shard_map/ppermute | solution.py:38
  143.4 1.1 copy-start.4
  147.5 2.1 copy-start
  157.0 12.4 %collective-permute-start.12 = (bf16[64,2176]{1,0:T(8,128)(2,1)S(1)}, bf16[64,2176]{1,0:T(8,128)(2,1)S(1)}, u32[]{:S(2)}, u32[]{:S(2)}) collective-permute-start(bf16[64,2176]{1,0:T(8,128)(2,1)S(1)} %get-tuple-element.45), channel_id=1, source_target_pairs={{0,54},{1,17},{8,62},{9,25},{16,0},{17,33},{24,8},{25,41},{32,16},... | collective-permute-start | bytes 835592 | tf_op jit(solution)/shard_map/ppermute | solution.py:38
  162.6 14.3 %collective-permute-start.10 = (bf16[64,2176]{1,0:T(8,128)(2,1)S(1)}, bf16[64,2176]{1,0:T(8,128)(2,1)S(1)}, u32[]{:S(2)}, u32[]{:S(2)}) collective-permute-start(bf16[64,2176]{1,0:T(8,128)(2,1)S(1)} %get-tuple-element.43), channel_id=1, source_target_pairs={{0,54},{1,17},{8,62},{9,25},{16,0},{17,33},{24,8},{25,41},{32,16},... | collective-permute-start | bytes 835592 | tf_op jit(solution)/shard_map/ppermute | solution.py:38
  169.5 12.8 %collective-permute-start.13 = (bf16[64,2176]{1,0:T(8,128)(2,1)S(1)}, bf16[64,2176]{1,0:T(8,128)(2,1)S(1)}, u32[]{:S(2)}, u32[]{:S(2)}) collective-permute-start(bf16[64,2176]{1,0:T(8,128)(2,1)S(1)} %add_convert_fusion.kept), channel_id=1, source_target_pairs={{0,62},{8,0},{16,8},{24,16},{32,24},{40,32},{48,40},{56,48},{2,56}... | collective-permute-start | bytes 835592 | tf_op jit(solution)/shard_map/ppermute | solution.py:38
  177.0 11.7 %collective-permute-start.11 = (bf16[64,2176]{1,0:T(8,128)(2,1)S(1)}, bf16[64,2176]{1,0:T(8,128)(2,1)S(1)}, u32[]{:S(2)}, u32[]{:S(2)}) collective-permute-start(bf16[64,2176]{1,0:T(8,128)(2,1)S(1)} %add_convert_fusion.1), channel_id=1, source_target_pairs={{0,54},{1,9},{8,62},{9,17},{16,0},{17,25},{24,8},{25,33},{32,16},{... | collective-permute-start | bytes 835592 | tf_op jit(solution)/shard_map/ppermute | solution.py:38
  189.6 3.3 %collective-permute-start.14 = (bf16[4,80,256]{2,1,0:T(8,128)(2,1)S(1)}, bf16[4,80,256]{2,1,0:T(8,128)(2,1)S(1)}, u32[]{:S(2)}, u32[]{:S(2)}) collective-permute-start(bf16[4,80,256]{2,1,0:T(8,128)(2,1)S(1)} %get-tuple-element.47), channel_id=1, source_target_pairs={{0,1},{1,0},{8,9},{9,8},{16,17},{17,16},{24,25},{25,24},{32,33},{3... | collective-permute-start | bytes 491528 | tf_op jit(solution)/shard_map/ppermute | solution.py:38
  193.6 44.7 %all-to-all-start.2 = ((bf16[4,80,256]{2,1,0:T(8,128)(2,1)}), bf16[4,80,256]{2,1,0:T(8,128)(2,1)S(1)}, u32[]{:S(2)}, u32[]{:S(2)}) async-start(bf16[4,80,256]{2,1,0:T(8,128)(2,1)} %add_convert_fusion.2), calls=%async_computation.2 | async-start | bytes 327680 | tf_op jit(solution)/shard_map/all_to_all | solution.py:55
  215.5 1.3 copy-start.5
Sparse Core Ops, SparseCore 0:
  10.7 39.9 all-gather.6
  53.4 38.8 all-gather.4
  157.1 58.3 reduce-scatter.1

commit v5 on v4

--- a/solution.py
+++ b/solution.py
@@ -349,6 +349,7 @@
         where, placing, coefs, *row_blocks, rows, *grad_blocks, grads,
         scalars=1, flops=4 * 4 * tokens * total * features,
     )
+    sends, gate_up_both, down_both = lax.optimization_barrier((sends, gate_up_both, down_both))
     routes = swap_y(sends)
     returns, acts = call(
         expert_kernel,
@@ -356,34 +357,32 @@
         where, routes, gate_up_both, down_both,
         scalars=1, flops=2 * total * 2 * units * features * 5,
     )
-    acts_other = to_other_core(acts[1])
-    kept_routes, acts = lax.optimization_barrier((routes, acts))
-    routes_other = to_other_core(kept_routes)
-    returned = swap_y(returns)
+    kept_routes, returned = lax.optimization_barrier((routes, swap_y(returns)))
+    acts_other, routes_other = to_other_core(acts[1]), to_other_core(kept_routes)
     (weight_parts,) = call(
         weight_grad_kernel,
         [struct((6 * units, features))],
         routes, routes_other, acts, acts_other,
         flops=2 * 2 * total * units * features * 3,
     )
-    returned, weight_parts = lax.optimization_barrier((returned, weight_parts))
     far, next_far, near, last = call(
         combine_kernel,
         [struct((tokens, features + META))] * 4,
         where, back_placing, metas, returned, scalars=1, flops=2 * 4 * tokens * total * features,
     )
 
-    weight_parts, far, next_far = lax.optimization_barrier((weight_parts, far, next_far))
-    weight_grads = lax.psum_scatter(weight_parts, "dp", scatter_dimension=1, tiled=True)
-
     def two_back(block):
         return send(block, lambda core: (0, -2 if core == 0 else 2, 0))
 
     def add(one, other):
         return (one.astype(F32) + other.astype(F32)).astype(BF)
 
-    near = add(near, two_back(far))
-    last = add(last, two_back(next_far))
+    weight_parts, far, next_far = lax.optimization_barrier(
+        (weight_parts, two_back(far), two_back(next_far))
+    )
+    weight_grads = lax.psum_scatter(weight_parts, "dp", scatter_dimension=1, tiled=True)
+    near = add(near, far)
+    last = add(last, next_far)
     arrived = send(near, lambda core: (0, -2 if core == 0 else 1, 0))
     below = send(last, lambda core: (0, -1, 0) if core == 0 else None)
     keep, give = call(

time: 247 us -> 252 us (1.020)
  the two profiles are of different devices: /device:TPU:38 before, /device:TPU:35 now
where the time goes in v5:
time: 252 us; the launch traced here: 251 us
  blocking collectives  85.2 us (34%)
  starting transfers between devices  70.6 us (28%)
  waiting for transfers between devices  51.5 us (20%)
  between operations  14.9 us (6%)
  local copies, waits for them, and re-layouts  14.5 us (6%)
  Pallas kernels  13.8 us (5%)
    ppermute x15, starting transfers between devices, send(): return lax.ppermute(array, PLANE, pairs)  53.8 us
    all_gather x1, blocking collectives, local(): lax.all_gather(jnp.concatenate([hidden_states, output_grad], axis=1), 'te...  52 us
    all_to_all x2, blocking collectives, swap_y(): lax.all_to_all(array, 'expert', split_axis=0, concat_axis=0, tiled=True,...  33.2 us
    reduce_scatter x1, waiting for transfers between devices, local(): lax.psum_scatter(weight_parts, 'dp', scatter_dimension=1, tiled=True)  24.8 us
    ppermute x15, waiting for transfers between devices, send(): return lax.ppermute(array, PLANE, pairs)  20.8 us
    all_to_all x1, starting transfers between devices, swap_hi(): lax.all_to_all(array, 'tensor', split_axis=0, concat_axis=0, tiled=True,...  16.7 us
    unnamed x44, local copies, waits for them, and re-layouts  14.4 us
    pallas_call x8, Pallas kernels, call(): pl.pallas_call(kernel, out_shape=outs, in_specs=ins, out_specs=[VMEM] * l...  13.8 us
  transfers between devices with their start and end apart: 19, of which 10 were waited for; matrix products, arithmetic and copies ran while one was open for 0% of the time, Pallas kernels for 3%

profile of v5, /device:TPU:35, one launch (start us, length us, event | category | flops | bytes accessed | tf_op | source)
XLA Modules:
  0.0 251.4 jit_solution(6628385779094323536)
XLA Ops:
  7.2 0.0 all-gather.7.cloned.1.call-start
  7.3 0.7 all-gather.7.cloned.1.call-update
  7.9 0.0 all-gather.5.cloned.1.call-start
  8.0 0.7 all-gather.5.cloned.1.call-update
  8.7 0.0 reduce-scatter.2.cloned.1.call-start
  8.8 52.0 %all_gather.15 = bf16[512,512]{1,0:T(8,128)(2,1)S(1)} all-gather(bf16[64,512]{1,0:T(8,128)(2,1)S(1)} %pad_maximum_fusion.1), channel_id=1, replica_groups=mesh['dp'=4,'expert'=32,'tensor'=8] {'tensor'}, dimensions={0}, use_global_device_ids=true | all-gather | bytes 589824 | tf_op jit(solution)/shard_map/all_gather | solution.py:319
  60.9 3.6 %collective-permute-start = (bf16[528,256]{1,0:T(8,128)(2,1)S(1)}, bf16[528,256]{1,0:T(8,128)(2,1)S(1)}, u32[]{:S(2)}, u32[]{:S(2)}) collective-permute-start(bf16[528,256]{1,0:T(8,128)(2,1)S(1)} %pad_maximum_fusion.own.refs_4_), channel_id=1, source_target_pairs={{0,8},{1,63},{8,16},{9,1},{16,24},{17,9},{24,32},{25,17},{32,40},{... | collective-permute-start | bytes 811016 | tf_op jit(solution)/shard_map/ppermute | solution.py:38
  64.5 1.9 collective-permute-start.4
  66.4 1.9 collective-permute-done.first.refs_0_
  68.4 3.6 %collective-permute-start.1 = (bf16[528,256]{1,0:T(8,128)(2,1)S(1)}, bf16[528,256]{1,0:T(8,128)(2,1)S(1)}, u32[]{:S(2)}, u32[]{:S(2)}) collective-permute-start(bf16[528,256]{1,0:T(8,128)(2,1)S(1)} %collective-permute-done.first.refs_0_), channel_id=1, source_target_pairs={{0,8},{1,63},{8,16},{9,1},{16,24},{17,9},{24,32},{25,17},{32,40},{... | collective-permute-start | bytes 811016 | tf_op jit(solution)/shard_map/ppermute | solution.py:38
  72.0 2.8 %collective-permute-start.5 = (bf16[512,256]{1,0:T(8,128)(2,1)S(1)}, bf16[512,256]{1,0:T(8,128)(2,1)S(1)}, u32[]{:S(2)}, u32[]{:S(2)}) collective-permute-start(bf16[512,256]{1,0:T(8,128)(2,1)S(1)} %collective-permute-done.4.refs_5_), channel_id=1, source_target_pairs={{0,8},{1,63},{8,16},{9,1},{16,24},{17,9},{24,32},{25,17},{32,40},{... | collective-permute-start | bytes 786440 | tf_op jit(solution)/shard_map/ppermute | solution.py:38
  74.8 0.0 copy-start.6
  74.8 0.7 copy-done.6
  75.5 0.3 collective-permute-done.1.second.refs_1_
  75.8 3.3 %collective-permute-start.2 = (bf16[528,256]{1,0:T(8,128)(2,1)S(1)}, bf16[528,256]{1,0:T(8,128)(2,1)S(1)}, u32[]{:S(2)}, u32[]{:S(2)}) collective-permute-start(bf16[528,256]{1,0:T(8,128)(2,1)S(1)} %collective-permute-done.1.second.refs_1_), channel_id=1, source_target_pairs={{0,8},{1,63},{8,16},{9,1},{16,24},{17,9},{24,32},{25,17},{32,40},{... | collective-permute-start | bytes 811016 | tf_op jit(solution)/shard_map/ppermute | solution.py:38
  79.2 0.2 collective-permute-done.5.refs_6_
  79.4 3.8 %collective-permute-start.6 = (bf16[512,256]{1,0:T(8,128)(2,1)S(1)}, bf16[512,256]{1,0:T(8,128)(2,1)S(1)}, u32[]{:S(2)}, u32[]{:S(2)}) collective-permute-start(bf16[512,256]{1,0:T(8,128)(2,1)S(1)} %collective-permute-done.5.refs_6_), channel_id=1, source_target_pairs={{0,8},{1,63},{8,16},{9,1},{16,24},{17,9},{24,32},{25,17},{32,40},{... | collective-permute-start | bytes 786440 | tf_op jit(solution)/shard_map/ppermute | solution.py:38
  83.2 0.0 copy-start.8
  83.2 0.7 copy-done.8
  83.9 0.7 collective-permute-start.3
  84.6 2.2 collective-permute-done.6.refs_7_
  86.8 0.7 collective-permute-start.7
  88.2 0.1 stack.19.where
  88.3 1.9 shard_map.102
  90.1 0.6 copy-done.14
  90.8 0.6 copy-done.16
  91.4 0.7 copy-done.12
  92.1 0.9 copy-done.5
  93.1 0.9 copy-done.7
  94.0 0.9 copy-done.9
  95.0 0.9 copy-done.11
  95.9 0.9 copy-done.13
  96.9 1.3 shard_map.103
  98.2 0.0 all-gather.7.cloned.1.call-done
  98.2 0.0 all-gather.5.cloned.1.call-done
  98.2 20.6 %all_to_all.15.routes = bf16[4,64,4096]{2,1,0:T(8,128)(2,1)S(1)} all-to-all(bf16[4,64,4096]{2,1,0:T(8,128)(2,1)S(1)} %shard_map.103), channel_id=1, replica_groups={{0,64,128,192},{8,72,136,200},{16,80,144,208},{24,88,152,216},{32,96,16..., dimensions={0} | all-to-all | bytes 4194304 | tf_op jit(solution)/shard_map/all_to_all | solution.py:48
  118.9 2.8 %copy-done.1 = bf16[4,2,192,2048]{3,2,1,0:T(8,128)(2,1)S(1)} copy-done((bf16[4,2,192,2048]{3,2,1,0:T(8,128)(2,1)S(1)}, bf16[4,2,192,2048]{3,2,1,0:T(8,128)(2,1)}, u32[]{:S(2)}) %copy-start.1) | copy-done | bytes 6291480
  121.6 4.7 %shard_map.104 = (bf16[4,64,2176]{2,1,0:T(8,128)(2,1)S(1)}, bf16[2,2,3,192,128]{4,3,2,1,0:T(8,128)(2,1)S(1)}) custom-call(s32[5]{0:T(128)S(1)} %stack.19.where, bf16[4,64,4096]{2,1,0:T(8,128)(2,1)S(1)} %all_to_all.15.routes, bf16[2,2,2,192,2048]{4,3,2,1,0:T(8,128)(2,1)S(1)} %bitcast.12, bf16[2,2,192,2048]{3,2,1,0:T(8,128)(2,1)S(1)} %bitcast.13), custom_call_target="tpu_custom_call" | custom-call | flops 2013265920 | bytes 13238292 | tf_op jit(solution)/shard_map/pallas_call | solution.py:68
  126.3 12.6 %all_to_all.16.returned = bf16[4,64,2176]{2,1,0:T(8,128)(2,1)S(1)} all-to-all(bf16[4,64,2176]{2,1,0:T(8,128)(2,1)S(1)} %get-tuple-element.38), channel_id=1, replica_groups={{0,64,128,192},{8,72,136,200},{16,80,144,208},{24,88,152,216},{32,96,16..., dimensions={0} | all-to-all | bytes 2228224 | tf_op jit(solution)/shard_map/all_to_all | solution.py:48
  139.0 14.0 %collective-permute-start.8 = (bf16[4,64,4096]{2,1,0:T(8,128)(2,1)S(1)}, bf16[4,64,4096]{2,1,0:T(8,128)(2,1)S(1)}, u32[]{:S(2)}, u32[]{:S(2)}) collective-permute-start(bf16[4,64,4096]{2,1,0:T(8,128)(2,1)S(1)} %all_to_all.15.routes), channel_id=1, source_target_pairs={{0,1},{1,0},{8,9},{9,8},{16,17},{17,16},{24,25},{25,24},{32,33},{3... | collective-permute-start | bytes 6291464 | tf_op jit(solution)/shard_map/ppermute | solution.py:38
  153.0 1.9 collective-permute-start.9
  154.9 1.5 shard_map.105
  156.4 3.8 %collective-permute-start.10 = (bf16[64,2176]{1,0:T(8,128)(2,1)S(1)}, bf16[64,2176]{1,0:T(8,128)(2,1)S(1)}, u32[]{:S(2)}, u32[]{:S(2)}) collective-permute-start(bf16[64,2176]{1,0:T(8,128)(2,1)S(1)} %get-tuple-element.43), channel_id=1, source_target_pairs={{0,54},{1,17},{8,62},{9,25},{16,0},{17,33},{24,8},{25,41},{32,16},... | collective-permute-start | bytes 835592 | tf_op jit(solution)/shard_map/ppermute | solution.py:38
  160.2 1.9 collective-permute-start.11
  162.1 1.4 shard_map.106
  163.6 2.2 copy-done
  165.7 2.9 %collective-permute-done.10 = bf16[64,2176]{1,0:T(8,128)(2,1)S(1)} collective-permute-done((bf16[64,2176]{1,0:T(8,128)(2,1)S(1)}, bf16[64,2176]{1,0:T(8,128)(2,1)S(1)}, u32[]{:S(2)}, u32[]{:S(2)}) %collective-permute-start.10) | collective-permute-done | bytes 278560 | tf_op jit(solution)/shard_map/ppermute | solution.py:38
  168.6 6.0 %collective-permute-done.11 = bf16[64,2176]{1,0:T(8,128)(2,1)S(1)} collective-permute-done((bf16[64,2176]{1,0:T(8,128)(2,1)S(1)}, bf16[64,2176]{1,0:T(8,128)(2,1)S(1)}, u32[]{:S(2)}, u32[]{:S(2)}) %collective-permute-start.11) | collective-permute-done | bytes 278560 | tf_op jit(solution)/shard_map/ppermute | solution.py:38
  174.6 0.0 reduce-scatter.2.cloned.1.call-update
  174.6 0.1 add_convert_fusion.kept
  174.7 0.7 collective-permute-start.13
  175.4 0.1 add_convert_fusion.1
  175.5 1.9 collective-permute-start.12
  177.4 6.2 %collective-permute-done.12.arrived = bf16[64,2176]{1,0:T(8,128)(2,1)S(1)} collective-permute-done((bf16[64,2176]{1,0:T(8,128)(2,1)S(1)}, bf16[64,2176]{1,0:T(8,128)(2,1)S(1)}, u32[]{:S(2)}, u32[]{:S(2)}) %collective-permute-start.12) | collective-permute-done | bytes 278560 | tf_op jit(solution)/shard_map/ppermute | solution.py:38
  183.6 0.9 shard_map.107
  184.5 9.2 %collective-permute-start.14 = (bf16[4,80,256]{2,1,0:T(8,128)(2,1)S(1)}, bf16[4,80,256]{2,1,0:T(8,128)(2,1)S(1)}, u32[]{:S(2)}, u32[]{:S(2)}) collective-permute-start(bf16[4,80,256]{2,1,0:T(8,128)(2,1)S(1)} %get-tuple-element.49), channel_id=1, source_target_pairs={{0,1},{1,0},{8,9},{9,8},{16,17},{17,16},{24,25},{25,24},{32,33},{3... | collective-permute-start | bytes 491528 | tf_op jit(solution)/shard_map/ppermute | solution.py:38
  193.7 1.0 collective-permute-done.14
  194.7 0.7 add_convert_fusion.2
  195.4 16.7 %all-to-all-start.2 = ((bf16[4,80,256]{2,1,0:T(8,128)(2,1)}), bf16[4,80,256]{2,1,0:T(8,128)(2,1)S(1)}, u32[]{:S(2)}, u32[]{:S(2)}) async-start(bf16[4,80,256]{2,1,0:T(8,128)(2,1)} %add_convert_fusion.2), calls=%async_computation.2 | async-start | bytes 327680 | tf_op jit(solution)/shard_map/all_to_all | solution.py:55
  212.1 24.8 %reduce-scatter.2.cloned.1.call-done.weight_grads = bf16[1152,512]{1,0:T(8,128)(2,1)} async-done(((bf16[1152,2048]{1,0:T(8,128)(2,1)}), bf16[1152,512]{1,0:T(8,128)(2,1)}) %reduce-scatter.2.cloned.1.call-update) | async-done | bytes 1179664 | tf_op jit(solution)/shard_map/reduce_scatter | solution.py:383
  236.9 1.3 copy-done.3
  238.2 1.1 shard_map.108
  239.3 4.4 %all-to-all-done.2.pieces = bf16[4,80,256]{2,1,0:T(8,128)(2,1)S(1)} async-done(((bf16[4,80,256]{2,1,0:T(8,128)(2,1)}), bf16[4,80,256]{2,1,0:T(8,128)(2,1)S(1)}, u32[]{:S(2)}, u32[]{:S(2)}) %all-to-all-start.2) | async-done | bytes 163872 | tf_op jit(solution)/shard_map/all_to_all | solution.py:55
  243.7 1.2 shard_map.109
  (42 shorter events, 0.2 us)
Async XLA Ops:
  7.2 1.6 copy-start.21
  7.2 1.6 copy-start.18
  7.2 1.6 copy-start.19
  7.2 1.6 copy-start.20
  7.2 91.0 %all-gather.7.cloned.1.call-start = ((), (), s32[]{:S(2)}) async-start(), calls=%async_computation.6 | async-start | bytes 4718592 | tf_op jit(solution)/shard_map/all_gather | solution.py:43
  7.9 90.3 %all-gather.5.cloned.1.call-start = ((), (), s32[]{:S(2)}) async-start(), calls=%async_computation.5 | async-start | bytes 9437184 | tf_op jit(solution)/shard_map/all_gather | solution.py:43
  8.7 228.2 %reduce-scatter.2.cloned.1.call-start = ((), (), s32[]{:S(2)}) async-start(), calls=%async_computation.4 | async-start | bytes 5898240 | tf_op jit(solution)/shard_map/reduce_scatter | solution.py:383
  60.8 23.1 %copy-start.4 = (bf16[512,256]{1,0:T(8,128)(2,1)}, bf16[512,256]{1,0:T(8,128)(2,1)S(1)}, u32[]{:S(2)}) copy-start(bf16[512,256]{1,0:T(8,128)(2,1)S(1)} %get-tuple-element.58.refs_9_) | copy-start | bytes 786436
  60.9 7.5 %collective-permute-start = (bf16[528,256]{1,0:T(8,128)(2,1)S(1)}, bf16[528,256]{1,0:T(8,128)(2,1)S(1)}, u32[]{:S(2)}, u32[]{:S(2)}) collective-permute-start(bf16[528,256]{1,0:T(8,128)(2,1)S(1)} %pad_maximum_fusion.own.refs_4_), channel_id=1, source_target_pairs={{0,8},{1,63},{8,16},{9,1},{16,24},{17,9},{24,32},{25,17},{32,40},{... | collective-permute-start | bytes 811016 | tf_op jit(solution)/shard_map/ppermute | solution.py:38
  64.5 7.5 %collective-permute-start.4 = (bf16[512,256]{1,0:T(8,128)(2,1)S(1)}, bf16[512,256]{1,0:T(8,128)(2,1)S(1)}, u32[]{:S(2)}, u32[]{:S(2)}) collective-permute-start(bf16[512,256]{1,0:T(8,128)(2,1)S(1)} %get-tuple-element.58.refs_9_), channel_id=1, source_target_pairs={{0,8},{1,63},{8,16},{9,1},{16,24},{17,9},{24,32},{25,17},{32,40},{... | collective-permute-start | bytes 786440 | tf_op jit(solution)/shard_map/ppermute | solution.py:38
  68.4 7.5 %collective-permute-start.1 = (bf16[528,256]{1,0:T(8,128)(2,1)S(1)}, bf16[528,256]{1,0:T(8,128)(2,1)S(1)}, u32[]{:S(2)}, u32[]{:S(2)}) collective-permute-start(bf16[528,256]{1,0:T(8,128)(2,1)S(1)} %collective-permute-done.first.refs_0_), channel_id=1, source_target_pairs={{0,8},{1,63},{8,16},{9,1},{16,24},{17,9},{24,32},{25,17},{32,40},{... | collective-permute-start | bytes 811016 | tf_op jit(solution)/shard_map/ppermute | solution.py:38
  72.0 7.4 %collective-permute-start.5 = (bf16[512,256]{1,0:T(8,128)(2,1)S(1)}, bf16[512,256]{1,0:T(8,128)(2,1)S(1)}, u32[]{:S(2)}, u32[]{:S(2)}) collective-permute-start(bf16[512,256]{1,0:T(8,128)(2,1)S(1)} %collective-permute-done.4.refs_5_), channel_id=1, source_target_pairs={{0,8},{1,63},{8,16},{9,1},{16,24},{17,9},{24,32},{25,17},{32,40},{... | collective-permute-start | bytes 786440 | tf_op jit(solution)/shard_map/ppermute | solution.py:38
  74.8 0.7 copy-start.6
  75.8 8.1 %collective-permute-start.2 = (bf16[528,256]{1,0:T(8,128)(2,1)S(1)}, bf16[528,256]{1,0:T(8,128)(2,1)S(1)}, u32[]{:S(2)}, u32[]{:S(2)}) collective-permute-start(bf16[528,256]{1,0:T(8,128)(2,1)S(1)} %collective-permute-done.1.second.refs_1_), channel_id=1, source_target_pairs={{0,8},{1,63},{8,16},{9,1},{16,24},{17,9},{24,32},{25,17},{32,40},{... | collective-permute-start | bytes 811016 | tf_op jit(solution)/shard_map/ppermute | solution.py:38
  79.4 7.4 %collective-permute-start.6 = (bf16[512,256]{1,0:T(8,128)(2,1)S(1)}, bf16[512,256]{1,0:T(8,128)(2,1)S(1)}, u32[]{:S(2)}, u32[]{:S(2)}) collective-permute-start(bf16[512,256]{1,0:T(8,128)(2,1)S(1)} %collective-permute-done.5.refs_6_), channel_id=1, source_target_pairs={{0,8},{1,63},{8,16},{9,1},{16,24},{17,9},{24,32},{25,17},{32,40},{... | collective-permute-start | bytes 786440 | tf_op jit(solution)/shard_map/ppermute | solution.py:38
  83.2 0.7 copy-start.8
  83.9 4.3 %collective-permute-start.3 = (bf16[528,256]{1,0:T(8,128)(2,1)S(1)}, bf16[528,256]{1,0:T(8,128)(2,1)S(1)}, u32[]{:S(2)}, u32[]{:S(2)}) collective-permute-start(bf16[528,256]{1,0:T(8,128)(2,1)S(1)} %collective-permute-done.2.third.refs_2_), channel_id=1, source_target_pairs={{0,8},{8,16},{16,24},{24,32},{32,40},{40,48},{48,56},{56,2},{2,10}... | collective-permute-start | bytes 811016 | tf_op jit(solution)/shard_map/ppermute | solution.py:38
  86.8 5.4 %copy-start.10 = (bf16[512,256]{1,0:T(8,128)(2,1)}, bf16[512,256]{1,0:T(8,128)(2,1)S(1)}, u32[]{:S(2)}) copy-start(bf16[512,256]{1,0:T(8,128)(2,1)S(1)} %collective-permute-done.6.refs_7_) | copy-start | bytes 786436
  86.8 4.7 %collective-permute-start.7 = (bf16[512,256]{1,0:T(8,128)(2,1)S(1)}, bf16[512,256]{1,0:T(8,128)(2,1)S(1)}, u32[]{:S(2)}, u32[]{:S(2)}) collective-permute-start(bf16[512,256]{1,0:T(8,128)(2,1)S(1)} %collective-permute-done.6.refs_7_), channel_id=1, source_target_pairs={{0,8},{8,16},{16,24},{24,32},{32,40},{40,48},{48,56},{56,2},{2,10}... | collective-permute-start | bytes 786440 | tf_op jit(solution)/shard_map/ppermute | solution.py:38
  90.1 0.7 copy-start.14
  90.8 0.6 copy-start.16
  91.4 0.7 copy-start.12
  92.1 1.0 copy-start.5
  93.1 0.9 copy-start.7
  94.0 0.9 copy-start.9
  95.0 0.9 copy-start.11
  95.9 0.9 copy-start.13
  98.2 20.6 %copy-start.2 = (bf16[4,192,2048]{2,1,0:T(8,128)(2,1)S(1)}, bf16[4,192,2048]{2,1,0:T(8,128)(2,1)}, u32[]{:S(2)}) copy-start(bf16[4,192,2048]{2,1,0:T(8,128)(2,1)} %all-gather.7.cloned.1.call-done) | copy-start | bytes 9437188
  118.9 2.8 %copy-start.1 = (bf16[4,2,192,2048]{3,2,1,0:T(8,128)(2,1)S(1)}, bf16[4,2,192,2048]{3,2,1,0:T(8,128)(2,1)}, u32[]{:S(2)}) copy-start(bf16[4,2,192,2048]{3,2,1,0:T(8,128)(2,1)} %all-gather.5.cloned.1.call-done) | copy-start | bytes 18874372
  126.3 28.6 %copy-start.15 = (bf16[256,256]{1,0:T(8,128)(2,1)S(1)}, bf16[256,256]{1,0:T(8,128)(2,1)}, u32[]{:S(2)}) copy-start(bf16[256,256]{1,0:T(8,128)(2,1)} %copy-done.14) | copy-start | bytes 393220
  126.3 28.6 %copy-start.17 = (f32[256,16]{1,0:T(8,128)S(1)}, f32[256,16]{1,0:T(8,128)}, u32[]{:S(2)}) copy-start(f32[256,16]{1,0:T(8,128)} %copy-done.16) | copy-start | bytes 49156
  139.0 23.2 %collective-permute-start.8 = (bf16[4,64,4096]{2,1,0:T(8,128)(2,1)S(1)}, bf16[4,64,4096]{2,1,0:T(8,128)(2,1)S(1)}, u32[]{:S(2)}, u32[]{:S(2)}) collective-permute-start(bf16[4,64,4096]{2,1,0:T(8,128)(2,1)S(1)} %all_to_all.15.routes), channel_id=1, source_target_pairs={{0,1},{1,0},{8,9},{9,8},{16,17},{17,16},{24,25},{25,24},{32,33},{3... | collective-permute-start | bytes 6291464 | tf_op jit(solution)/shard_map/ppermute | solution.py:38
  153.0 9.1 %collective-permute-start.9 = (bf16[2,3,192,128]{3,2,1,0:T(8,128)(2,1)S(1)}, bf16[2,3,192,128]{3,2,1,0:T(8,128)(2,1)S(1)}, u32[]{:S(2)}, u32[]{:S(2)}) collective-permute-start(bf16[2,3,192,128]{3,2,1,0:T(8,128)(2,1)S(1)} %slice_bitcast_fusion), channel_id=1, source_target_pairs={{0,1},{1,0},{8,9},{9,8},{16,17},{17,16},{24,25},{25,24},{32,33},{3... | collective-permute-start | bytes 884744 | tf_op jit(solution)/shard_map/ppermute | solution.py:38
  156.4 12.2 %collective-permute-start.10 = (bf16[64,2176]{1,0:T(8,128)(2,1)S(1)}, bf16[64,2176]{1,0:T(8,128)(2,1)S(1)}, u32[]{:S(2)}, u32[]{:S(2)}) collective-permute-start(bf16[64,2176]{1,0:T(8,128)(2,1)S(1)} %get-tuple-element.43), channel_id=1, source_target_pairs={{0,54},{1,17},{8,62},{9,25},{16,0},{17,33},{24,8},{25,41},{32,16},... | collective-permute-start | bytes 835592 | tf_op jit(solution)/shard_map/ppermute | solution.py:38
  160.2 14.4 %collective-permute-start.11 = (bf16[64,2176]{1,0:T(8,128)(2,1)S(1)}, bf16[64,2176]{1,0:T(8,128)(2,1)S(1)}, u32[]{:S(2)}, u32[]{:S(2)}) collective-permute-start(bf16[64,2176]{1,0:T(8,128)(2,1)S(1)} %get-tuple-element.44), channel_id=1, source_target_pairs={{0,54},{1,17},{8,62},{9,25},{16,0},{17,33},{24,8},{25,41},{32,16},... | collective-permute-start | bytes 835592 | tf_op jit(solution)/shard_map/ppermute | solution.py:38
  163.6 2.2 copy-start
  174.7 2.7 %collective-permute-start.13 = (bf16[64,2176]{1,0:T(8,128)(2,1)S(1)}, bf16[64,2176]{1,0:T(8,128)(2,1)S(1)}, u32[]{:S(2)}, u32[]{:S(2)}) collective-permute-start(bf16[64,2176]{1,0:T(8,128)(2,1)S(1)} %add_convert_fusion.kept), channel_id=1, source_target_pairs={{0,62},{8,0},{16,8},{24,16},{32,24},{40,32},{48,40},{56,48},{2,56}... | collective-permute-start | bytes 835592 | tf_op jit(solution)/shard_map/ppermute | solution.py:38
  175.5 8.2 %collective-permute-start.12 = (bf16[64,2176]{1,0:T(8,128)(2,1)S(1)}, bf16[64,2176]{1,0:T(8,128)(2,1)S(1)}, u32[]{:S(2)}, u32[]{:S(2)}) collective-permute-start(bf16[64,2176]{1,0:T(8,128)(2,1)S(1)} %add_convert_fusion.1), channel_id=1, source_target_pairs={{0,54},{1,9},{8,62},{9,17},{16,0},{17,25},{24,8},{25,33},{32,16},{... | collective-permute-start | bytes 835592 | tf_op jit(solution)/shard_map/ppermute | solution.py:38
  184.5 10.2 %collective-permute-start.14 = (bf16[4,80,256]{2,1,0:T(8,128)(2,1)S(1)}, bf16[4,80,256]{2,1,0:T(8,128)(2,1)S(1)}, u32[]{:S(2)}, u32[]{:S(2)}) collective-permute-start(bf16[4,80,256]{2,1,0:T(8,128)(2,1)S(1)} %get-tuple-element.49), channel_id=1, source_target_pairs={{0,1},{1,0},{8,9},{9,8},{16,17},{17,16},{24,25},{25,24},{32,33},{3... | collective-permute-start | bytes 491528 | tf_op jit(solution)/shard_map/ppermute | solution.py:38
  195.4 48.3 %all-to-all-start.2 = ((bf16[4,80,256]{2,1,0:T(8,128)(2,1)}), bf16[4,80,256]{2,1,0:T(8,128)(2,1)S(1)}, u32[]{:S(2)}, u32[]{:S(2)}) async-start(bf16[4,80,256]{2,1,0:T(8,128)(2,1)} %add_convert_fusion.2), calls=%async_computation.2 | async-start | bytes 327680 | tf_op jit(solution)/shard_map/all_to_all | solution.py:55
  236.9 1.3 copy-start.3
Sparse Core Ops, SparseCore 0:
  10.7 40.4 all-gather.6
  53.9 38.8 all-gather.4
  174.8 62.1 reduce-scatter.1
